TPU v7x, 512 devices: a whole 4x4x16 slice. The times are simulated.
512 devices in a mesh: ctx: 256 (over y_lo, x, z, core), head: 2 (over y_hi).
Axes of the slice: x: 4, y: 4 (y_hi: 2, y_lo: 2; y = y_hi * 2 + y_lo), z: 16, core: 2. Of those that a mesh axis runs over, the one named last changes fastest.
Arguments:
- queries: bfloat16 [32768, 1536], P('ctx', 'head'), may hold values from -8 to 8
- key_states: bfloat16 [32768, 1536], P('ctx', 'head'), may hold values from -8 to 8
- value_states: bfloat16 [32768, 1536], P('ctx', 'head'), may hold values from -6 to 6
- out_grad: bfloat16 [32768, 1536], P('ctx', 'head'), may hold values from -24 to 24
- rel_table: bfloat16 [256, 128], replicated, may hold values from -3 to 3
- block_mask: int32 [256, 3], P('ctx'), may hold values 0 or 1
- distance_shift: int32 [256, 3], P('ctx'), may hold values from 0 to 127
Outputs:
- query_grad: bfloat16 [32768, 1536], P('ctx', 'head')
- key_grad: bfloat16 [32768, 1536], P('ctx', 'head')
- value_grad: bfloat16 [32768, 1536], P('ctx', 'head')
- table_grad: float32 [256, 128], replicated
All inputs are finite; a program needn't handle non-finite values. No bound on the sum of `block_mask` on one device may be relied on, other than what follows from the above.
Results may differ from a plain program's by a relative error of at most 0.033.
Values may be sent and summed in bfloat16 or wider, within the bound.
No kernel may reach another device: no remote copies, remote signals or barrier semaphores. Data moves between devices by JAX's collectives and lax.ppermute only.
A program may use at most 64 MiB of HBM per device.

v0:
```python
from functools import reduce

import jax
import jax.numpy as jnp
from jax import lax
from jax.sharding import PartitionSpec as P

HEAD_DIM = 128


def shifted(block, axis, distance):
    devices = range(lax.axis_size(axis))
    route = [(i - distance, i) for i in devices if i - distance in devices]
    return lax.ppermute(block, axis, route)


def skewed(block):
    width = block.shape[-2]
    lead = block.shape[:-2]
    flipped = jnp.flip(block[..., : 2 * width - 1], axis=-1)
    padded = jnp.concatenate([flipped, jnp.zeros(lead + (width, 1), block.dtype)], axis=-1)
    flat = padded.reshape(lead + (2 * width * width,))[..., : width * (2 * width - 1)]
    return flat.reshape(lead + (width, 2 * width - 1))[..., width - 1 : 2 * width - 1]


def unskewed(grad_block):
    width = grad_block.shape[-1]
    shape = grad_block.shape[:-1] + (2 * width,)
    _, pullback = jax.vjp(skewed, jnp.zeros(shape, grad_block.dtype))
    return pullback(grad_block)[0]


def padded_table(rel_table, width):
    first = jnp.broadcast_to(rel_table[:1], (2 * width, rel_table.shape[1]))
    last = jnp.broadcast_to(rel_table[-1:], (2 * width, rel_table.shape[1]))
    return jnp.concatenate([first, rel_table, last], axis=0)


def window_rows(table, offset, step, width):
    start = step * width + width + 1 - offset
    return (lax.dynamic_slice_in_dim(table, start, 2 * width, 0), start)


def folded_table(padded_grad, width, rows):
    middle = padded_grad[2 * width : 2 * width + rows]
    low = jnp.sum(padded_grad[: 2 * width], axis=0)
    high = jnp.sum(padded_grad[2 * width + rows :], axis=0)
    middle = middle.at[0].add(low)
    return middle.at[rows - 1].add(high)


def shards(queries, key_states, value_states, out_grad, rel_table, block_mask, distance_shift):
    width = queries.shape[0]
    heads = queries.shape[1] // HEAD_DIM
    steps = block_mask.shape[1]
    rows = rel_table.shape[0]
    scale = HEAD_DIM ** (-0.5)
    shape_h = (width, heads, HEAD_DIM)
    query = queries.reshape(shape_h)
    grads_out = out_grad.reshape(shape_h)
    table = padded_table(rel_table, width)
    block_id = lax.axis_index("ctx")
    lower = jnp.arange(width)[None, :] <= jnp.arange(width)[:, None]
    key_list = [key_states]
    value_list = [value_states]
    moving = (key_states, value_states)
    for step in range(1, steps):
        moving = shifted((moving[0], moving[1]), "ctx", 1)
        key_list.append(moving[0])
        value_list.append(moving[1])
    keys_h = [item.reshape(shape_h) for item in key_list]
    values_h = [item.reshape(shape_h) for item in value_list]
    scores, seen_list, windows, starts = ([], [], [], [])
    for step in range(steps):
        rows_w, start = window_rows(table, distance_shift[0, step], step, width)
        if step == 0:
            seen = lower
        else:
            seen = jnp.broadcast_to((block_mask[0, step] == 1) & (block_id >= step), (width, width))
        content = jnp.einsum(
            "ihd,jhd->hij", query, keys_h[step], preferred_element_type=jnp.float32
        )
        relative = jnp.einsum("ihd,ud->hiu", query, rows_w, preferred_element_type=jnp.float32)
        scores.append(scale * (content + skewed(relative)))
        seen_list.append(seen)
        windows.append(rows_w)
        starts.append(start)
    top = reduce(
        jnp.maximum,
        [jnp.max(jnp.where(s[None], x, -jnp.inf), axis=-1) for x, s in zip(scores, seen_list)],
    )
    total = sum(
        [
            jnp.sum(jnp.where(s[None], jnp.exp(x - top[..., None]), 0.0), axis=-1)
            for x, s in zip(scores, seen_list)
        ]
    )
    lse = top + jnp.log(total)
    probs = [
        jnp.where(s[None], jnp.exp(x - lse[..., None]), 0.0) for x, s in zip(scores, seen_list)
    ]
    weights = [p.astype(jnp.bfloat16) for p in probs]
    output = sum(
        [
            jnp.einsum("hij,jhd->ihd", w, v, preferred_element_type=jnp.float32)
            for w, v in zip(weights, values_h)
        ]
    )
    output = output.astype(jnp.bfloat16)
    delta = jnp.einsum("ihd,ihd->hi", grads_out, output, preferred_element_type=jnp.float32)
    query_acc = jnp.zeros(shape_h, jnp.float32)
    table_acc = jnp.zeros(table.shape, jnp.float32)
    parts = []
    for step in range(steps):
        dprob = jnp.einsum(
            "ihd,jhd->hij", grads_out, values_h[step], preferred_element_type=jnp.float32
        )
        dscore = (scale * probs[step] * (dprob - delta[..., None])).astype(jnp.bfloat16)
        rel_grad = unskewed(dscore)
        query_acc = query_acc + jnp.einsum(
            "hij,jhd->ihd", dscore, keys_h[step], preferred_element_type=jnp.float32
        )
        query_acc = query_acc + jnp.einsum(
            "hiu,ud->ihd", rel_grad, windows[step], preferred_element_type=jnp.float32
        )
        rows_grad = jnp.einsum("hiu,ihd->ud", rel_grad, query, preferred_element_type=jnp.float32)
        current = lax.dynamic_slice_in_dim(table_acc, starts[step], 2 * width, 0)
        table_acc = lax.dynamic_update_slice_in_dim(table_acc, current + rows_grad, starts[step], 0)
        key_part = jnp.einsum("hij,ihd->jhd", dscore, query, preferred_element_type=jnp.float32)
        value_part = jnp.einsum(
            "hij,ihd->jhd", weights[step], grads_out, preferred_element_type=jnp.float32
        )
        parts.append(jnp.stack([key_part.reshape(width, -1), value_part.reshape(width, -1)]))
    carried = jnp.zeros_like(parts[0])
    for step in range(steps - 1, 0, -1):
        carried = shifted(carried + parts[step], "ctx", -1)
    combined = carried + parts[0]
    key_total = combined[0]
    value_total = combined[1]
    table_grad = lax.psum(folded_table(table_acc, width, rows), ("ctx", "head"))
    query_grad = query_acc.reshape(width, -1).astype(jnp.bfloat16)
    return (
        query_grad,
        key_total.astype(jnp.bfloat16),
        value_total.astype(jnp.bfloat16),
        table_grad,
    )


def solution(mesh):
    return jax.shard_map(
        shards,
        mesh=mesh,
        in_specs=(
            P("ctx", "head"),
            P("ctx", "head"),
            P("ctx", "head"),
            P("ctx", "head"),
            P(),
            P("ctx", None),
            P("ctx", None),
        ),
        out_specs=(P("ctx", "head"), P("ctx", "head"), P("ctx", "head"), P()),
        check_vma=False,
    )
```

profile of v0, /device:TPU:1, one launch (start us, length us, event | category | flops | bytes accessed | tf_op | source)
XLA Modules:
  0.0 559.2 jit_solution(4565982314279522937)
XLA Ops:
  7.2 1.1 copy.78
  8.4 5.1 collective-permute-start.2
  13.6 1.9 collective-permute-start
  24.1 1.2 rev.22
  28.5 1.2 rev.21
  32.9 1.2 rev.20
  36.6 3.9 collective-permute-start.3
  40.5 2.1 collective-permute-start.1
  43.0 2.5 collective-permute-done.1
  46.4 1.0 fusion.47
  47.9 1.2 convolution_add_fusion.1
  49.2 1.0 fusion.41
  52.3 1.2 fusion.13
  55.1 1.2 reverse.2
  56.5 1.0 convolution_bitcast_fusion.11
  57.5 1.0 convolution_bitcast_fusion.8
  59.2 1.0 fusion.72
  62.2 1.2 reverse
  64.7 4.3 reverse.1
  69.0 1.2 slice.148
  70.2 1.1 convolution_bitcast_fusion.7
  73.4 1.0 dynamic_update_slice.10
  75.4 1.9 pad_maximum_fusion
  77.4 1.9 collective-permute-start.4
  79.6 1.1 convolution_bitcast_fusion.6
  85.0 6.8 %collective-permute-done.4 = f32[2,128,768]{2,1,0:T(8,128)} collective-permute-done((f32[2,128,768]{2,1,0:T(8,128)}, f32[2,128,768]{2,1,0:T(8,128)}, u32[]{:S(2)}, u32[]{:S(2)}) %collective-permute-start.4) | collective-permute-done | bytes 786464 | tf_op jit(solution)/shard_map/ppermute | solution.py:14
  91.8 1.2 maximum_add_fusion
  93.0 2.1 collective-permute-start.5
  97.3 9.2 %collective-permute-done.5 = f32[2,128,768]{2,1,0:T(8,128)} collective-permute-done((f32[2,128,768]{2,1,0:T(8,128)S(1)}, f32[2,128,768]{2,1,0:T(8,128)}, u32[]{:S(2)}, u32[]{:S(2)}) %collective-permute-start.5) | collective-permute-done | bytes 786464 | tf_op jit(solution)/shard_map/ppermute | solution.py:14
  106.5 1.2 fusion.19
  108.5 442.3 %all-reduce.14.cloned.1.call-done = f32[256,128]{1,0:T(8,128)} async-done(((f32[256,128]{1,0:T(8,128)}), f32[256,128]{1,0:T(8,128)}) %all-reduce.14.cloned.1.call-update) | async-done | bytes 131088 | tf_op jit(solution)/shard_map/psum | solution.py:140
  550.8 1.6 copy.190
  (142 shorter events, 32.2 us)
Async XLA Ops:
  7.2 6.3 %copy-start.19 = (bf16[128,768]{1,0:T(8,128)(2,1)S(1)}, bf16[128,768]{1,0:T(8,128)(2,1)}, u32[]{:S(2)}) copy-start(bf16[128,768]{1,0:T(8,128)(2,1)} %param.12) | copy-start | bytes 589828
  7.2 543.6 %all-reduce.14.cloned.1.call-start = ((), (), s32[]{:S(2)}) async-start(), calls=%async_computation | async-start | bytes 262144 | tf_op jit(solution)/shard_map/psum | solution.py:140
  8.3 9.8 %copy-start.22 = (bf16[256,128]{1,0:T(8,128)(2,1)S(1)}, bf16[256,128]{1,0:T(8,128)(2,1)}, u32[]{:S(2)}) copy-start(bf16[256,128]{1,0:T(8,128)(2,1)} %param.15) | copy-start | bytes 196612
  8.4 14.3 %copy-start.20 = (bf16[128,768]{1,0:T(8,128)(2,1)S(1)}, bf16[128,768]{1,0:T(8,128)(2,1)}, u32[]{:S(2)}) copy-start(bf16[128,768]{1,0:T(8,128)(2,1)} %param.14) | copy-start | bytes 589828
  8.4 28.2 %collective-permute-start.2 = (bf16[128,768]{0,1:T(8,128)(2,1)S(1)}, bf16[128,768]{0,1:T(8,128)(2,1)}, u32[]{:S(2)}, u32[]{:S(2)}) collective-permute-start(bf16[128,768]{0,1:T(8,128)(2,1)S(1)} %copy.78), channel_id=1, source_target_pairs={{0,2},{2,4},{4,6},{6,8},{8,10},{10,12},{12,14},{14,16},{16,18},{18... | collective-permute-start | bytes 589832 | tf_op jit(solution)/shard_map/ppermute | solution.py:14
  13.6 26.9 %collective-permute-start = (bf16[128,768]{0,1:T(8,128)(2,1)S(1)}, bf16[128,768]{0,1:T(8,128)(2,1)S(1)}, u32[]{:S(2)}, u32[]{:S(2)}) collective-permute-start(bf16[128,768]{0,1:T(8,128)(2,1)S(1)} %copy.60), channel_id=1, source_target_pairs={{0,2},{2,4},{4,6},{6,8},{8,10},{10,12},{12,14},{14,16},{16,18},{18... | collective-permute-start | bytes 589832 | tf_op jit(solution)/shard_map/ppermute | solution.py:14
  15.6 0.7 copy-start.24
  16.8 1.3 copy-start.23
  22.7 0.9 copy-start.21
  36.3 6.4 %copy-start.5 = (f32[6,128,128]{1,2,0:T(8,128)S(1)}, f32[6,128,128]{1,2,0:T(8,128)}, u32[]{:S(2)}) copy-start(f32[6,128,128]{1,2,0:T(8,128)} %copy.164) | copy-start | bytes 1179652
  36.6 13.6 %collective-permute-start.3 = (bf16[128,768]{0,1:T(8,128)(2,1)}, bf16[128,768]{0,1:T(8,128)(2,1)S(1)}, u32[]{:S(2)}, u32[]{:S(2)}) collective-permute-start(bf16[128,768]{0,1:T(8,128)(2,1)} %collective-permute-done.2), channel_id=1, source_target_pairs={{0,2},{2,4},{4,6},{6,8},{8,10},{10,12},{12,14},{14,16},{16,18},{18... | collective-permute-start | bytes 589832 | tf_op jit(solution)/shard_map/ppermute | solution.py:14
  40.5 2.4 copy-start.11
  40.5 4.9 collective-permute-start.1
  42.7 2.8 copy-start.3
  45.4 0.7 copy-start.13
  46.3 3.8 copy-start.17
  50.2 0.7 copy-start.9
  51.3 0.7 copy-start.18
  52.3 1.3 copy-start.10
  59.1 1.0 copy-start.1
  71.3 0.9 copy-start.15
  74.5 1.0 copy-start.6
  77.4 14.4 %collective-permute-start.4 = (f32[2,128,768]{2,1,0:T(8,128)}, f32[2,128,768]{2,1,0:T(8,128)}, u32[]{:S(2)}, u32[]{:S(2)}) collective-permute-start(f32[2,128,768]{2,1,0:T(8,128)} %pad_maximum_fusion), channel_id=1, source_target_pairs={{2,0},{4,2},{6,4},{8,6},{10,8},{12,10},{14,12},{16,14},{18,16},{20... | collective-permute-start | bytes 2359304 | tf_op jit(solution)/shard_map/ppermute | solution.py:14
  80.7 1.0 copy-start
  81.7 1.0 copy-start.4
  82.7 1.0 copy-start.7
  82.7 1.0 copy-start.12
  83.7 1.0 copy-start.8
  83.7 1.0 copy-start.14
  93.0 2.1 copy-start.2
  93.0 13.5 %collective-permute-start.5 = (f32[2,128,768]{2,1,0:T(8,128)S(1)}, f32[2,128,768]{2,1,0:T(8,128)}, u32[]{:S(2)}, u32[]{:S(2)}) collective-permute-start(f32[2,128,768]{2,1,0:T(8,128)S(1)} %maximum_add_fusion), channel_id=1, source_target_pairs={{2,0},{4,2},{6,4},{8,6},{10,8},{12,10},{14,12},{16,14},{18,16},{20... | collective-permute-start | bytes 2359304 | tf_op jit(solution)/shard_map/ppermute | solution.py:14
  96.2 0.7 copy-start.16
Sparse Core Ops, SparseCore 0:
  97.0 453.7 all-reduce.13
where the time goes:
time: 560 us; the launch traced here: 559 us
  waiting for transfers between devices  461 us (82%)
  local copies, waits for them, and re-layouts  42.3 us (8%)
  between operations  20.1 us (4%)
  starting transfers between devices  17 us (3%)
  matrix products  14.2 us (3%)
    psum x1, waiting for transfers between devices, shards(): table_grad = lax.psum(folded_table(table_acc, width, rows), ('ctx', 'head'))  442 us
    unnamed x81, local copies, waits for them, and re-layouts  24.8 us
    ppermute x6, waiting for transfers between devices, shifted(): return lax.ppermute(block, axis, route)  18.5 us
    ppermute x6, starting transfers between devices, shifted(): return lax.ppermute(block, axis, route)  17 us
  transfers between devices with their start and end apart: 7, of which 4 were waited for; matrix products, arithmetic and copies ran while one was open for 5% of the time, Pallas kernels for 0%

commit v1 on v0

v1 whole, which is shorter than its diff:
```python
import jax
import jax.numpy as jnp
from jax import lax
from jax.experimental import pallas as pl
from jax.experimental.pallas import tpu as pltpu
from jax.sharding import PartitionSpec as P

HEAD_DIM = 128
AXES = ("ctx", "head")
NT = (((1,), (1,)), ((), ()))
TN = (((0,), (0,)), ((), ()))


def dot(a, b, dims=(((1,), (0,)), ((), ()))):
    return lax.dot_general(a, b, dims, preferred_element_type=jnp.float32)


def lanes(values, index):
    return jnp.take_along_axis(values, index, axis=1, mode="promise_in_bounds")


def block_kernel(
    block_ref, mask_ref, shift_ref, query_ref, grad_ref, key_ref, value_ref, far_ref, pair_ref,
    cross_ref, table_ref, query_out, own_out, near_out, far_out, table_out, near_kv
):
    width = query_ref.shape[0]
    heads = query_ref.shape[1] // HEAD_DIM
    rows = table_ref.shape[0]
    scale = HEAD_DIM ** (-0.5)
    block = block_ref[0]
    odd = lax.rem(block, 2) == 1

    @pl.when(odd)
    def _():
        near_kv[...] = pair_ref[0]

    @pl.when(jnp.logical_not(odd))
    def _():
        near_kv[...] = cross_ref[1]

    row = lax.broadcasted_iota(jnp.int32, (width, width), 0)
    col = lax.broadcasted_iota(jnp.int32, (width, width), 1)
    bases = [step * width - shift_ref[0, step] for step in range(3)]
    seen = col <= row
    biases = [
        jnp.where((mask_ref[0, step] == 1) & (block >= step), 0.0, -jnp.inf) for step in (1, 2)
    ]
    place = [col - row + (rows - 1) - base for base in bases]
    high = [place[0] > rows - 1, place[1] > rows - 1]
    low = place[2] < 0
    place = [jnp.clip(item, 0, rows - 1) for item in place]
    upper = [item >= width for item in place]
    place = [item & (width - 1) for item in place]
    source = [col + row - (rows - 1) + base for base in bases]
    in_low = [(item >= 0) & (item < width) for item in source]
    in_high = [(item >= -width) & (item < 0) for item in source]
    source = [item & (width - 1) for item in source]
    table = table_ref[...]
    table_sum = jnp.zeros((rows, HEAD_DIM), jnp.float32)
    for head in range(heads):
        part = slice(head * HEAD_DIM, (head + 1) * HEAD_DIM)
        query = query_ref[:, part]
        grad = grad_ref[:, part]
        keys = [key_ref[:, part], near_kv[0, :, part], far_ref[0, :, part]]
        values = [value_ref[:, part], near_kv[1, :, part], far_ref[1, :, part]]
        keys_all = jnp.concatenate(keys + [table], axis=0)
        values_all = jnp.concatenate(values, axis=0)
        content = dot(query, keys_all, NT)
        dprob = dot(grad, values_all, NT)
        relative = [content[:, 3 * width : 4 * width], content[:, 4 * width :]]
        scores = []
        for step in range(3):
            moved = lanes(relative[1], place[step])
            if step > 0:
                moved = jnp.where(upper[step], moved, lanes(relative[0], place[step]))
            score = scale * (content[:, step * width : (step + 1) * width] + moved)
            if step == 0:
                score = jnp.where(seen, score, -jnp.inf)
            else:
                score = score + biases[step - 1]
            scores.append(score)
        dprobs = [dprob[:, step * width : (step + 1) * width] for step in range(3)]
        top = jnp.max(jnp.maximum(jnp.maximum(scores[0], scores[1]), scores[2]), axis=1, keepdims=True)
        exps = [jnp.exp(score - top) for score in scores]
        total = jnp.sum(exps[0] + exps[1] + exps[2], axis=1, keepdims=True)
        mixed = exps[0] * dprobs[0] + exps[1] * dprobs[1] + exps[2] * dprobs[2]
        inverse = 1.0 / total
        delta = jnp.sum(mixed, axis=1, keepdims=True) * inverse
        probs = [e * inverse for e in exps]
        weights = jnp.concatenate([p.astype(jnp.bfloat16) for p in probs], axis=1)
        dscores = [scale * p * (d - delta) for p, d in zip(probs, dprobs)]
        over = jnp.where(high[0], dscores[0], 0.0) + jnp.where(high[1], dscores[1], 0.0)
        over = jnp.sum(over, axis=1, keepdims=True)
        under = jnp.sum(jnp.where(low, dscores[2], 0.0), axis=1, keepdims=True)
        moved = [lanes(item, index) for item, index in zip(dscores, source)]
        below = jnp.where(in_low[1], moved[1], 0.0) + jnp.where(in_low[2], moved[2], 0.0)
        above = jnp.where(in_high[0], moved[0], 0.0) + jnp.where(in_high[1], moved[1], 0.0)
        above = above + jnp.where(in_high[2], moved[2], 0.0)
        below = below + jnp.where(col == 0, under, 0.0)
        above = above + jnp.where(col == width - 1, over, 0.0)
        terms = jnp.concatenate(dscores + [below, above], axis=1).astype(jnp.bfloat16)
        query_out[:, part] = dot(terms, keys_all).astype(query_out.dtype)
        by_key = dot(terms, query, TN)
        by_value = dot(weights, grad, TN)
        own_out[0, :, part] = by_key[:width]
        own_out[1, :, part] = by_value[:width]
        near_out[0, :, part] = by_key[width : 2 * width].astype(jnp.bfloat16)
        near_out[1, :, part] = by_value[width : 2 * width].astype(jnp.bfloat16)
        far_out[0, :, part] = by_key[2 * width : 3 * width].astype(jnp.bfloat16)
        far_out[1, :, part] = by_value[2 * width :].astype(jnp.bfloat16)
        table_sum = table_sum + by_key[3 * width :]
    table_out[...] = table_sum


def block_grads(block, mask, shift, query, grad, key, value, far, pair, cross, table_flipped):
    width, span = query.shape
    vmem = pl.BlockSpec(memory_space=pltpu.VMEM)
    smem = pl.BlockSpec(memory_space=pltpu.SMEM)
    both = (2, width, span)
    return pl.pallas_call(
        block_kernel,
        out_shape=(
            jax.ShapeDtypeStruct((width, span), jnp.bfloat16),
            jax.ShapeDtypeStruct(both, jnp.float32),
            jax.ShapeDtypeStruct(both, jnp.bfloat16),
            jax.ShapeDtypeStruct(both, jnp.bfloat16),
            jax.ShapeDtypeStruct(table_flipped.shape, jnp.float32),
        ),
        in_specs=[smem] * 3 + [vmem] * 8,
        out_specs=(vmem,) * 5,
        scratch_shapes=[pltpu.VMEM(both, jnp.bfloat16)],
        compiler_params=pltpu.CompilerParams(vmem_limit_bytes=32 * 1024 * 1024),
        name="block_grads",
    )(block, mask, shift, query, grad, key, value, far, pair, cross, table_flipped)


def rings(mesh_sizes):
    ctx, head = mesh_sizes
    depth = 32
    columns = ctx // depth
    planes = [
        [
            ((column * depth + z * 2 + core) * head + half)
            for column in range(columns)
            for core in range(2)
            for half in range(head)
        ]
        for z in range(depth // 2)
    ]
    lines = [
        [((column * depth + z * 2 + core) * head + half) for z in range(depth // 2)]
        for column in range(columns)
        for core in range(2)
        for half in range(head)
    ]
    return planes, lines


def table_total(partial, mesh_sizes):
    rows, dim = partial.shape
    planes, lines = rings(mesh_sizes)
    plane, line = len(planes[0]), len(lines[0])
    small = rows // plane
    pieces = lax.all_to_all(
        partial.reshape(plane, small, dim), AXES, 0, 0, axis_index_groups=planes
    )
    piece = jnp.sum(pieces, axis=0)[::-1]
    copies = jnp.broadcast_to(piece[None], (line, small, dim))
    copies = lax.all_to_all(copies, AXES, 0, 0, axis_index_groups=lines)
    piece = jnp.sum(copies, axis=0)
    copies = jnp.broadcast_to(piece[None], (plane, small, dim))
    copies = lax.all_to_all(
        copies, AXES, 0, 0, axis_index_groups=[group[::-1] for group in planes]
    )
    return copies.reshape(rows, dim)


def shards(queries, key_states, value_states, out_grad, rel_table, block_mask, distance_shift):
    count = lax.axis_size("ctx")
    block = lax.axis_index("ctx").astype(jnp.int32).reshape(1)
    pairs = [[i, i + 1] for i in range(0, count, 2)]
    kv = jnp.stack([key_states, value_states])
    far = lax.ppermute(kv, "ctx", [(i, (i + 2) % count) for i in range(count)])
    pair = lax.all_gather(kv, "ctx", axis_index_groups=pairs)
    cross = lax.all_gather(far, "ctx", axis_index_groups=pairs)
    query_grad, own, near_part, far_part, table_part = block_grads(
        block, block_mask, distance_shift, queries, out_grad, key_states, value_states, far, pair,
        cross, rel_table[::-1]
    )
    near_part = lax.ppermute(near_part, "ctx", [(i, (i - 1) % count) for i in range(count)])
    far_part = lax.ppermute(far_part, "ctx", [(i, (i - 2) % count) for i in range(count)])
    table_grad = table_total(table_part, (count, lax.axis_size("head")))
    total = own + near_part.astype(jnp.float32) + far_part.astype(jnp.float32)
    total = total.astype(jnp.bfloat16)
    return query_grad, total[0], total[1], table_grad


def solution(mesh):
    return jax.shard_map(
        shards,
        mesh=mesh,
        in_specs=(
            P("ctx", "head"),
            P("ctx", "head"),
            P("ctx", "head"),
            P("ctx", "head"),
            P(),
            P("ctx", None),
            P("ctx", None),
        ),
        out_specs=(P("ctx", "head"), P("ctx", "head"), P("ctx", "head"), P()),
        check_vma=False,
    )
```

time: 560 us -> 89.7 us (0.16)
  waiting for transfers between devices: 461 us -> 16.5 us
  blocking collectives: 0 us -> 40 us
  local copies, waits for them, and re-layouts: 42.3 us -> 2.87 us
  between operations: 20.1 us -> 0.75 us
  matrix products: 14.2 us -> 0 us
  Pallas kernels: 0 us -> 8.82 us
    psum x1 -> x0, waiting for transfers between devices: 442 us -> none  [shards(): table_grad = lax.psum(folded_table(table_acc, width, rows), ('ctx', 'head'))]
    all_to_all x0 -> x2, blocking collectives: none -> 30.3 us  [the longest x1 17.7 us: table_total(): copies = lax.all_to_all(copies, AXES, 0, 0, axis_index_groups=lines)]
    unnamed x81 -> x15, local copies, waits for them, and re-layouts: 24.8 us -> 1.32 us
    dot_general x27 -> x0, matrix products: 14.2 us -> none  [the longest x3 3.16 us: shards(): jnp.einsum('hiu,ud->ihd', rel_grad, windows[step], preferred_element_type...]
    all_gather x0 -> x2, blocking collectives: none -> 9.63 us  [the longest x1 6.42 us: shards(): pair = lax.all_gather(kv, 'ctx', axis_index_groups=pairs)]
    all_to_all x0 -> x1, starting transfers between devices: none -> 9.2 us  [table_total(): lax.all_to_all(copies, AXES, 0, 0, axis_index_groups=[group[::-1] for gro...]
    pallas_call x0 -> x1, Pallas kernels: none -> 8.82 us  [block_grads(): pl.pallas_call(block_kernel, out_shape=(jax.ShapeDtypeStruct((width, span...]
    ppermute x6 -> x3, starting transfers between devices: 17 us -> 10 us  [the longest x1 4.38 us: shards(): far = lax.ppermute(kv, 'ctx', [(i, (i + 2) % count) for i in range(count)])]
  transfers between devices with their start and end apart: 7 -> 4, of which waited for: 4 -> 2; matrix products, arithmetic and copies ran while one was open for 5% -> 2% of each run, Pallas kernels for 0% -> 0%
where the time goes in v1:
time: 89.7 us; the launch traced here: 89.3 us
  blocking collectives  40 us (45%)
  starting transfers between devices  19.2 us (21%)
  waiting for transfers between devices  16.5 us (18%)
  Pallas kernels  8.82 us (10%)
  local copies, waits for them, and re-layouts  2.87 us (3%)
  other arithmetic  1.27 us (1%)
    all_to_all x1, blocking collectives, table_total(): copies = lax.all_to_all(copies, AXES, 0, 0, axis_index_groups=lines)  17.7 us
    ppermute x1, waiting for transfers between devices, shards(): far = lax.ppermute(kv, 'ctx', [(i, (i + 2) % count) for i in range(count)])  13.1 us
    all_to_all x1, blocking collectives, table_total(): lax.all_to_all(partial.reshape(plane, small, dim), AXES, 0, 0, axis_index...  12.7 us
    all_to_all x1, starting transfers between devices, table_total(): lax.all_to_all(copies, AXES, 0, 0, axis_index_groups=[group[::-1] for gro...  9.2 us
    pallas_call x1, Pallas kernels, block_grads(): pl.pallas_call(block_kernel, out_shape=(jax.ShapeDtypeStruct((width, span...  8.82 us
    all_gather x1, blocking collectives, shards(): pair = lax.all_gather(kv, 'ctx', axis_index_groups=pairs)  6.42 us
    ppermute x1, starting transfers between devices, shards(): far = lax.ppermute(kv, 'ctx', [(i, (i + 2) % count) for i in range(count)])  4.38 us
    all_to_all x1, waiting for transfers between devices, table_total(): lax.all_to_all(copies, AXES, 0, 0, axis_index_groups=[group[::-1] for gro...  3.41 us
  transfers between devices with their start and end apart: 4, of which 2 were waited for; matrix products, arithmetic and copies ran while one was open for 2% of the time, Pallas kernels for 0%

profile of v1, /device:TPU:1, one launch (start us, length us, event | category | flops | bytes accessed | tf_op | source)
XLA Modules:
  0.0 89.3 jit_solution(8591901247914327102)
XLA Ops:
  0.6 0.0 copy-start.6
  0.6 1.1 %pad_maximum_fusion = bf16[2,128,768]{2,1,0:T(8,128)(2,1)S(1)} fusion(bf16[1,128,768]{2,1,0:T(8,128)(2,1)} %bitcast.14, bf16[1,128,768]{2,1,0:T(8,128)(2,1)} %bitcast.13), kind=kLoop, calls=%fused_computation.1 | loop fusion | flops 196608 | bytes 786432 | tf_op jit(solution)/shard_map/stack | solution.py:182
  1.7 4.4 %collective-permute-start = (bf16[2,128,768]{2,1,0:T(8,128)(2,1)S(1)}, bf16[2,128,768]{2,1,0:T(8,128)(2,1)S(1)}, u32[]{:S(2)}, u32[]{:S(2)}) collective-permute-start(bf16[2,128,768]{2,1,0:T(8,128)(2,1)S(1)} %pad_maximum_fusion), channel_id=1, source_target_pairs={{0,4},{2,6},{4,8},{6,10},{8,12},{10,14},{12,16},{14,18},{16,20},{1... | collective-permute-start | bytes 1179656 | tf_op jit(solution)/shard_map/ppermute | solution.py:183
  6.1 0.0 copy-done.6
  6.1 0.1 rev.6.table_ref
  6.2 6.4 %all-gather = bf16[4,128,768]{2,1,0:T(8,128)(2,1)S(1)} all-gather(bf16[2,128,768]{2,1,0:T(8,128)(2,1)S(1)} %pad_maximum_fusion), channel_id=2, replica_groups={{0,2},{4,6},{8,10},{12,14},{16,18},{20,22},{24,26},{28,30},{32,34},{36,..., dimensions={0}, use_global_device_ids=true | all-gather | bytes 1179648 | tf_op jit(solution)/shard_map/all_gather | solution.py:184
  12.7 0.0 copy-start
  12.7 0.0 copy-start.1
  12.7 0.0 copy-start.2
  12.7 0.0 copy-start.3
  12.7 13.1 %collective-permute-done.far_ref = bf16[2,128,768]{2,1,0:T(8,128)(2,1)S(1)} collective-permute-done((bf16[2,128,768]{2,1,0:T(8,128)(2,1)S(1)}, bf16[2,128,768]{2,1,0:T(8,128)(2,1)S(1)}, u32[]{:S(2)}, u32[]{:S(2)}) %collective-permute-start) | collective-permute-done | bytes 393248 | tf_op jit(solution)/shard_map/ppermute | solution.py:183
  25.7 3.2 %all-gather.1 = bf16[4,128,768]{2,1,0:T(8,128)(2,1)S(1)} all-gather(bf16[2,128,768]{2,1,0:T(8,128)(2,1)S(1)} %collective-permute-done.far_ref), channel_id=3, replica_groups={{0,2},{4,6},{8,10},{12,14},{16,18},{20,22},{24,26},{28,30},{32,34},{36,..., dimensions={0}, use_global_device_ids=true | all-gather | bytes 1179648 | tf_op jit(solution)/shard_map/all_gather | solution.py:185
  28.9 0.0 copy-start.4
  28.9 0.0 copy-done
  28.9 0.0 copy-done.1
  29.0 0.0 copy-done.2
  29.0 0.0 copy-done.3
  29.0 0.6 copy-done.4
  29.6 0.0 copy-done.5
  29.6 8.8 %block_grads.1 = (bf16[128,768]{1,0:T(8,128)(2,1)}, f32[2,128,768]{2,1,0:T(8,128)S(1)}, bf16[2,128,768]{2,1,0:T(8,128)(2,1)S(1)}, bf16[2,128,768]{2,1,0:T(8,128)(2,1)S(1)}, f32[256,128]{1,0:T(8,128)S(1)}) custom-call(s32[1]{0:T(128)} %bitcast.block_ref, s32[1,3]{1,0:T(1,128)S(1)} %copy-done.4, s32[1,3]{1,0:T(1,128)S(1)} %copy-done.5, ...), custom_call_target="tpu_custom_call" | custom-call | tf_op jit(solution)/shard_map/block_grads/pallas_call | solution.py:120
  38.4 2.3 %collective-permute-start.1 = (bf16[2,128,768]{2,1,0:T(8,128)(2,1)S(1)}, bf16[2,128,768]{2,1,0:T(8,128)(2,1)S(1)}, u32[]{:S(2)}, u32[]{:S(2)}) collective-permute-start(bf16[2,128,768]{2,1,0:T(8,128)(2,1)S(1)} %get-tuple-element.11), channel_id=1, source_target_pairs={{0,510},{2,0},{4,2},{6,4},{8,6},{10,8},{12,10},{14,12},{16,14},{18... | collective-permute-start | bytes 1179656 | tf_op jit(solution)/shard_map/ppermute | solution.py:190
  40.7 3.4 %collective-permute-start.2 = (bf16[2,128,768]{2,1,0:T(8,128)(2,1)S(1)}, bf16[2,128,768]{2,1,0:T(8,128)(2,1)S(1)}, u32[]{:S(2)}, u32[]{:S(2)}) collective-permute-start(bf16[2,128,768]{2,1,0:T(8,128)(2,1)S(1)} %get-tuple-element.12), channel_id=1, source_target_pairs={{0,508},{2,510},{4,0},{6,2},{8,4},{10,6},{12,8},{14,10},{16,12},{1... | collective-permute-start | bytes 1179656 | tf_op jit(solution)/shard_map/ppermute | solution.py:191
  44.1 12.7 %all_to_all.15 = f32[32,8,128]{2,1,0:T(8,128)S(1)} all-to-all(f32[32,8,128]{2,1,0:T(8,128)S(1)} %bitcast.15), channel_id=1, replica_groups={{0,1,2,3,64,65,66,67,128,129,130,131,192,193,194,195,256,257,258,259,32..., dimensions={0} | all-to-all | bytes 262144 | tf_op jit(solution)/shard_map/all_to_all | solution.py:164
  56.8 17.7 %all_to_all.16 = f32[16,8,128]{2,1,0:T(8,128)S(1)} all-to-all(f32[16,8,128]{2,1,0:T(8,128)S(1)} %broadcast_in_dim.4), channel_id=1, replica_groups={{0,4,8,12,16,20,24,28,32,36,40,44,48,52,56,60},{1,5,9,13,17,21,25,29,33..., dimensions={0} | all-to-all | bytes 131072 | tf_op jit(solution)/shard_map/all_to_all | solution.py:169
  74.5 0.7 broadcast_in_dim.5
  75.2 9.2 %all-to-all-start.2 = ((f32[32,8,128]{2,1,0:T(8,128)}), f32[32,8,128]{2,1,0:T(8,128)S(1)}, u32[]{:S(2)}, u32[]{:S(2)}) async-start(f32[32,8,128]{2,1,0:T(8,128)} %broadcast_in_dim.5), calls=%async_computation.2 | async-start | bytes 262144 | tf_op jit(solution)/shard_map/all_to_all | solution.py:172
  84.4 0.0 collective-permute-done.1
  84.4 0.0 collective-permute-done.2
  84.4 0.1 add_convert_fusion
  84.5 0.8 slice_bitcast_fusion
  85.3 3.4 %all-to-all-done.2 = f32[32,8,128]{2,1,0:T(8,128)S(1)} async-done(((f32[32,8,128]{2,1,0:T(8,128)}), f32[32,8,128]{2,1,0:T(8,128)S(1)}, u32[]{:S(2)}, u32[]{:S(2)}) %all-to-all-start.2) | async-done | bytes 131104 | tf_op jit(solution)/shard_map/all_to_all | solution.py:172
  88.7 0.7 copy.12
  (5 shorter events, 0.1 us)
Async XLA Ops:
  0.6 5.5 %copy-start.6 = (bf16[256,128]{1,0:T(8,128)(2,1)S(1)}, bf16[256,128]{1,0:T(8,128)(2,1)}, u32[]{:S(2)}) copy-start(bf16[256,128]{1,0:T(8,128)(2,1)} %param.11) | copy-start | bytes 196612
  1.7 24.0 %collective-permute-start = (bf16[2,128,768]{2,1,0:T(8,128)(2,1)S(1)}, bf16[2,128,768]{2,1,0:T(8,128)(2,1)S(1)}, u32[]{:S(2)}, u32[]{:S(2)}) collective-permute-start(bf16[2,128,768]{2,1,0:T(8,128)(2,1)S(1)} %pad_maximum_fusion), channel_id=1, source_target_pairs={{0,4},{2,6},{4,8},{6,10},{8,12},{10,14},{12,16},{14,18},{16,20},{1... | collective-permute-start | bytes 1179656 | tf_op jit(solution)/shard_map/ppermute | solution.py:183
  12.7 16.3 %copy-start = (bf16[128,768]{1,0:T(8,128)(2,1)S(1)}, bf16[128,768]{1,0:T(8,128)(2,1)}, u32[]{:S(2)}) copy-start(bf16[128,768]{1,0:T(8,128)(2,1)} %key_ref.1) | copy-start | bytes 589828
  12.7 16.3 %copy-start.1 = (bf16[128,768]{1,0:T(8,128)(2,1)S(1)}, bf16[128,768]{1,0:T(8,128)(2,1)}, u32[]{:S(2)}) copy-start(bf16[128,768]{1,0:T(8,128)(2,1)} %value_ref.1) | copy-start | bytes 589828
  12.7 16.3 %copy-start.2 = (bf16[128,768]{1,0:T(8,128)(2,1)S(1)}, bf16[128,768]{1,0:T(8,128)(2,1)}, u32[]{:S(2)}) copy-start(bf16[128,768]{1,0:T(8,128)(2,1)} %query_ref.1) | copy-start | bytes 589828
  12.7 16.3 %copy-start.3 = (bf16[128,768]{1,0:T(8,128)(2,1)S(1)}, bf16[128,768]{1,0:T(8,128)(2,1)}, u32[]{:S(2)}) copy-start(bf16[128,768]{1,0:T(8,128)(2,1)} %grad_ref.1) | copy-start | bytes 589828
  28.9 0.7 copy-start.4
  28.9 0.7 copy-start.5
  38.4 45.9 %collective-permute-start.1 = (bf16[2,128,768]{2,1,0:T(8,128)(2,1)S(1)}, bf16[2,128,768]{2,1,0:T(8,128)(2,1)S(1)}, u32[]{:S(2)}, u32[]{:S(2)}) collective-permute-start(bf16[2,128,768]{2,1,0:T(8,128)(2,1)S(1)} %get-tuple-element.11), channel_id=1, source_target_pairs={{0,510},{2,0},{4,2},{6,4},{8,6},{10,8},{12,10},{14,12},{16,14},{18... | collective-permute-start | bytes 1179656 | tf_op jit(solution)/shard_map/ppermute | solution.py:190
  40.7 43.7 %collective-permute-start.2 = (bf16[2,128,768]{2,1,0:T(8,128)(2,1)S(1)}, bf16[2,128,768]{2,1,0:T(8,128)(2,1)S(1)}, u32[]{:S(2)}, u32[]{:S(2)}) collective-permute-start(bf16[2,128,768]{2,1,0:T(8,128)(2,1)S(1)} %get-tuple-element.12), channel_id=1, source_target_pairs={{0,508},{2,510},{4,0},{6,2},{8,4},{10,6},{12,8},{14,10},{16,12},{1... | collective-permute-start | bytes 1179656 | tf_op jit(solution)/shard_map/ppermute | solution.py:191
  75.2 13.5 %all-to-all-start.2 = ((f32[32,8,128]{2,1,0:T(8,128)}), f32[32,8,128]{2,1,0:T(8,128)S(1)}, u32[]{:S(2)}, u32[]{:S(2)}) async-start(f32[32,8,128]{2,1,0:T(8,128)} %broadcast_in_dim.5), calls=%async_computation.2 | async-start | bytes 262144 | tf_op jit(solution)/shard_map/all_to_all | solution.py:172

commit v2 on v1

v2 whole, which is shorter than its diff:
```python
import functools

import jax
import jax.numpy as jnp
from jax import lax
from jax.experimental import pallas as pl
from jax.experimental.pallas import tpu as pltpu
from jax.sharding import PartitionSpec as P

HEAD_DIM = 128
STEPS = 3
AXES = ("ctx", "head")
NN = (((1,), (0,)), ((), ()))
NT = (((1,), (1,)), ((), ()))
TN = (((0,), (0,)), ((), ()))
SCALE = HEAD_DIM ** (-0.5)


def dot(a, b, dims=NN):
    return lax.dot_general(a, b, dims, preferred_element_type=jnp.float32)


def lanes(values, index):
    return jnp.take_along_axis(values, index, axis=1, mode="promise_in_bounds")


def head_parts(span):
    return [slice(at, at + HEAD_DIM) for at in range(0, span, HEAD_DIM)]


def iotas(width):
    row = lax.broadcasted_iota(jnp.int32, (width, width), 0)
    col = lax.broadcasted_iota(jnp.int32, (width, width), 1)
    return row, col


def call(kernel, outs, ins, spaces, scratch, micros, name):
    return pl.pallas_call(
        kernel,
        out_shape=tuple(jax.ShapeDtypeStruct(shape, kind) for shape, kind in outs),
        in_specs=[pl.BlockSpec(memory_space=space) for space in spaces],
        out_specs=(pl.BlockSpec(memory_space=pltpu.VMEM),) * len(outs),
        scratch_shapes=scratch,
        compiler_params=pltpu.CompilerParams(vmem_limit_bytes=32 * 1024 * 1024),
        cost_estimate=pl.CostEstimate(
            flops=micros * 1_000_000_000, bytes_accessed=0, transcendentals=0
        ),
        name=name,
    )(*ins)


def own_kernel(
    block_ref, facts_ref, query_ref, grad_ref, key_ref, value_ref, near_ref, far_ref, table_ref,
    score_out, moved_out, dprob_out, turned_out
):
    width, span = query_ref.shape
    rows = table_ref.shape[0]
    other = 1 - lax.rem(block_ref[0], 2)
    row, col = iotas(width)
    seen = col <= row
    biases = [
        jnp.where(facts_ref[STEPS + step : STEPS + step + 1, :] == 1, 0.0, -jnp.inf)
        for step in range(STEPS)
    ]
    place = [
        jnp.clip(col - row + (rows - 1) - facts_ref[step : step + 1, :], 0, rows - 1)
        for step in range(STEPS)
    ]
    upper = [item >= width for item in place]
    place = [item & (width - 1) for item in place]
    table = table_ref[...]
    for part in head_parts(span):
        query = query_ref[:, part]
        turned_out[part, :] = query.T
        values = [value_ref[:, part], near_ref[other, :, part], far_ref[:, part]]
        dprob = dot(grad_ref[:, part], jnp.concatenate(values, axis=0), NT) * SCALE
        for step in range(STEPS):
            dprob_out[step, :, part] = dprob[:, step * width : (step + 1) * width]
        content = dot(query, jnp.concatenate([key_ref[:, part], table], axis=0), NT) * SCALE
        relative = [content[:, at : at + width] for at in (width, 2 * width)]
        for step in range(STEPS):
            moved = lanes(relative[1], place[step])
            if step == 0:
                score_out[:, part] = jnp.where(seen, content[:, :width] + moved, -jnp.inf)
            else:
                moved = jnp.where(upper[step], moved, lanes(relative[0], place[step]))
                moved_out[step - 1, :, part] = moved + biases[step]


def table_kernel(
    block_ref, facts_ref, query_ref, near_ref, far_ref, score_ref, moved_ref, dprob_ref, turned_ref,
    table_out, terms_out, weight_out
):
    width, span = query_ref.shape
    rows = table_out.shape[0]
    other = 1 - lax.rem(block_ref[0], 2)
    row, col = iotas(width)
    bases = [facts_ref[step : step + 1, :] for step in range(STEPS)]
    place = [col - row + (rows - 1) - base for base in bases]
    high = [place[0] > rows - 1, place[1] > rows - 1]
    low = place[2] < 0
    source = [col + row - (rows - 1) + base for base in bases]
    in_low = [(item >= 0) & (item < width) for item in source]
    in_high = [(item >= -width) & (item < 0) for item in source]
    source = [item & (width - 1) for item in source]
    table_sum = jnp.zeros((HEAD_DIM, rows), jnp.float32)
    for index, part in enumerate(head_parts(span)):
        keys = jnp.concatenate([near_ref[other, :, part], far_ref[:, part]], axis=0)
        content = dot(query_ref[:, part], keys, NT) * SCALE
        scores = [score_ref[:, part]]
        for step in range(1, STEPS):
            scores.append(content[:, (step - 1) * width : step * width] + moved_ref[step - 1, :, part])
        top = jnp.max(jnp.maximum(jnp.maximum(scores[0], scores[1]), scores[2]), axis=1, keepdims=True)
        exps = [jnp.exp(score - top) for score in scores]
        dprobs = [dprob_ref[step, :, part] for step in range(STEPS)]
        total = jnp.sum(exps[0] + exps[1] + exps[2], axis=1, keepdims=True)
        mixed = exps[0] * dprobs[0] + exps[1] * dprobs[1] + exps[2] * dprobs[2]
        mixed = jnp.sum(mixed, axis=1, keepdims=True)
        inverse = 1.0 / total
        delta = mixed * inverse
        probs = [item * inverse for item in exps]
        dscores = [p * (d - delta) for p, d in zip(probs, dprobs)]
        over = jnp.where(high[0], dscores[0], 0.0) + jnp.where(high[1], dscores[1], 0.0)
        over = jnp.sum(over, axis=1, keepdims=True)
        under = jnp.sum(jnp.where(low, dscores[2], 0.0), axis=1, keepdims=True)
        moved = [lanes(item, at) for item, at in zip(dscores, source)]
        below = jnp.where(in_low[1], moved[1], 0.0) + jnp.where(in_low[2], moved[2], 0.0)
        above = jnp.where(in_high[0], moved[0], 0.0) + jnp.where(in_high[1], moved[1], 0.0)
        above = above + jnp.where(in_high[2], moved[2], 0.0)
        below = below + jnp.where(col == 0, under, 0.0)
        above = above + jnp.where(col == width - 1, over, 0.0)
        relative = jnp.concatenate([below, above], axis=1).astype(jnp.bfloat16)
        table_sum = table_sum + dot(turned_ref[part, :], relative)
        for step in range(STEPS):
            at = slice(step * width, (step + 1) * width)
            terms_out[index, :, at] = dscores[step].astype(jnp.bfloat16)
            weight_out[index, :, at] = probs[step].astype(jnp.bfloat16)
        terms_out[index, :, STEPS * width :] = relative
    table_out[...] = table_sum.T


def grads_kernel(
    block_ref, query_ref, grad_ref, key_ref, near_ref, far_ref, table_ref, terms_ref, weight_ref,
    near_out, far_out, query_out, own_out
):
    width, span = query_ref.shape
    other = 1 - lax.rem(block_ref[0], 2)
    table = table_ref[...]
    for index, part in enumerate(head_parts(span)):
        query = query_ref[:, part]
        grad = grad_ref[:, part]
        terms = terms_ref[index]
        keys = [key_ref[:, part], near_ref[other, :, part], far_ref[:, part], table]
        query_out[:, part] = dot(terms, jnp.concatenate(keys, axis=0)).astype(query_out.dtype)
        by_key = dot(terms[:, : STEPS * width], query, TN)
        by_value = dot(weight_ref[index], grad, TN)
        for slot, item in enumerate((by_key, by_value)):
            own_out[slot, :, part] = item[:width]
            near_out[slot, :, part] = item[width : 2 * width].astype(jnp.bfloat16)
            far_out[slot, :, part] = item[2 * width :].astype(jnp.bfloat16)


def spread_kernel(flipped, pieces_ref, copies_out):
    total = pieces_ref[0]
    for index in range(1, pieces_ref.shape[0]):
        total = total + pieces_ref[index]
    if flipped:
        small = total.shape[0]
        total = jnp.concatenate([total[at : at + 1] for at in reversed(range(small))], axis=0)
    for index in range(copies_out.shape[0]):
        copies_out[index] = total


def rings(count, head):
    depth = 32
    columns = count // depth
    planes = [
        [
            (column * depth + z * 2 + core) * head + half
            for column in range(columns)
            for core in range(2)
            for half in range(head)
        ]
        for z in range(depth // 2)
    ]
    lines = [
        [(column * depth + z * 2 + core) * head + half for z in range(depth // 2)]
        for column in range(columns)
        for core in range(2)
        for half in range(head)
    ]
    return planes, lines


def shards(queries, key_states, value_states, out_grad, rel_table, block_mask, distance_shift):
    count = lax.axis_size("ctx")
    width, span = queries.shape
    rows = rel_table.shape[0]
    heads = span // HEAD_DIM
    block = lax.axis_index("ctx").astype(jnp.int32).reshape(1)
    odd = lax.rem(block[0], 2) == 1
    pairs = [[i, i + 1] for i in range(0, count, 2)]
    ahead = [(i, (i + 2) % count) for i in range(count)]
    one, two, three = (width, span), (2, width, span), (STEPS, width, span)
    bf, f32 = jnp.bfloat16, jnp.float32
    scalar, local = [pltpu.SMEM], [pltpu.VMEM]
    step = jnp.arange(STEPS, dtype=jnp.int32)
    visible = (block_mask[0] == 1) & (block[0] >= step)
    facts = [step * width - distance_shift[0], visible.astype(jnp.int32), step[:2]]
    facts = jnp.broadcast_to(jnp.concatenate(facts)[:, None], (8, width))
    table = rel_table[::-1]
    far_key = lax.ppermute(key_states, "ctx", ahead)
    far_value = lax.ppermute(value_states, "ctx", ahead)
    near_value = lax.all_gather(jnp.where(odd, far_value, value_states), "ctx", axis_index_groups=pairs)
    score, moved, dprob, turned = call(
        own_kernel,
        ((one, f32), (two, f32), (three, f32), ((span, width), bf)),
        (block, facts, queries, out_grad, key_states, value_states, near_value, far_value, table),
        scalar + local * 8, [], 3, "own_scores",
    )
    far_key, score = lax.optimization_barrier((far_key, score))
    near_key = lax.all_gather(jnp.where(odd, far_key, key_states), "ctx", axis_index_groups=pairs)
    table_part, terms, weight = call(
        table_kernel,
        (
            ((rows, HEAD_DIM), f32), ((heads, width, STEPS * width + rows), bf),
            ((heads, width, STEPS * width), bf),
        ),
        (block, facts, queries, near_key, far_key, score, moved, dprob, turned),
        scalar + local * 8, [], 4, "table_part",
    )
    near_part, far_part, query_grad, own = call(
        grads_kernel,
        ((two, bf), (two, bf), (one, bf), (two, f32)),
        (block, queries, out_grad, key_states, near_key, far_key, table, terms, weight),
        scalar + local * 8, [], 4, "block_grads",
    )
    planes, lines = rings(count, lax.axis_size("head"))
    small = rows // len(planes[0])
    shape = (len(planes[0]), small, HEAD_DIM)
    table_part, near_part, far_part = lax.optimization_barrier((table_part, near_part, far_part))
    near_part = lax.ppermute(near_part, "ctx", [(i, (i - 1) % count) for i in range(count)])
    far_part = lax.ppermute(far_part, "ctx", [(i, (i - 2) % count) for i in range(count)])
    pieces = lax.all_to_all(table_part.reshape(shape), AXES, 0, 0, axis_index_groups=planes)
    (copies,) = call(
        functools.partial(spread_kernel, True),
        (((len(lines[0]), small, HEAD_DIM), f32),), (pieces,), local, [], 40, "plane_sum",
    )
    pieces = lax.all_to_all(copies, AXES, 0, 0, axis_index_groups=lines)
    (copies,) = call(
        functools.partial(spread_kernel, False), ((shape, f32),), (pieces,), local, [], 1, "line_sum",
    )
    copies = lax.all_to_all(copies, AXES, 0, 0, axis_index_groups=[plane[::-1] for plane in planes])
    table_grad = copies.reshape(rows, HEAD_DIM)
    total = own + near_part.astype(f32) + far_part.astype(f32)
    total = total.astype(bf)
    return query_grad, total[0], total[1], table_grad


def solution(mesh):
    return jax.shard_map(
        shards,
        mesh=mesh,
        in_specs=(
            P("ctx", "head"),
            P("ctx", "head"),
            P("ctx", "head"),
            P("ctx", "head"),
            P(),
            P("ctx", None),
            P("ctx", None),
        ),
        out_specs=(P("ctx", "head"), P("ctx", "head"), P("ctx", "head"), P()),
        check_vma=False,
    )
```

time: 89.7 us -> 81.3 us (0.906)
  blocking collectives: 40 us -> 25.1 us
  starting transfers between devices: 19.2 us -> 30 us
  waiting for transfers between devices: 16.5 us -> 13.2 us
  Pallas kernels: 8.82 us -> 7.71 us
    all_to_all x2 -> x1, blocking collectives: 30.3 us -> 18.3 us  [shards(): pieces = lax.all_to_all(copies, AXES, 0, 0, axis_index_groups=lines)]
    all_to_all x1 -> x2, starting transfers between devices: 9.2 us -> 13.2 us  [the longest x1 8.51 us: shards(): lax.all_to_all(copies, AXES, 0, 0, axis_index_groups=[plane[::-1] for pla...]
    ppermute x1 -> x2, starting transfers between devices: 4.38 us -> 8.05 us  [the longest x1 4.51 us: shards(): far_value = lax.ppermute(value_states, 'ctx', ahead)]
    ppermute x1, starting transfers between devices: 3.36 us -> 6.64 us  [shards(): lax.ppermute(far_part, 'ctx', [(i, (i - 2) % count) for i in range(count)])]
    ppermute x1 -> x2, waiting for transfers between devices: 13.1 us -> 9.81 us  [the longest x1 9.81 us: shards(): far_value = lax.ppermute(value_states, 'ctx', ahead)]
    all_gather x2, blocking collectives: 9.63 us -> 6.79 us  [the longest x1 4.7 us: shards(): lax.all_gather(jnp.where(odd, far_value, value_states), 'ctx', axis_index...]
    pallas_call x1 -> x5, Pallas kernels: 8.82 us -> 7.71 us  [call(): pl.pallas_call(kernel, out_shape=tuple((jax.ShapeDtypeStruct(shape, kind)...]
    another operation x1 -> x0, other arithmetic: 1.09 us -> none  [shards(): kv = jnp.stack([key_states, value_states])]
  transfers between devices with their start and end apart: 4 -> 6, of which waited for: 2 -> 2; matrix products, arithmetic and copies ran while one was open for 2% -> 4% of each run, Pallas kernels for 0% -> 3%
where the time goes in v2:
time: 81.3 us; the launch traced here: 80.8 us
  starting transfers between devices  30 us (37%)
  blocking collectives  25.1 us (31%)
  waiting for transfers between devices  13.2 us (16%)
  Pallas kernels  7.71 us (9%)
  local copies, waits for them, and re-layouts  2.34 us (3%)
  other arithmetic  1.57 us (2%)
    all_to_all x1, blocking collectives, shards(): pieces = lax.all_to_all(copies, AXES, 0, 0, axis_index_groups=lines)  18.3 us
    ppermute x1, waiting for transfers between devices, shards(): far_value = lax.ppermute(value_states, 'ctx', ahead)  9.81 us
    all_to_all x1, starting transfers between devices, shards(): lax.all_to_all(copies, AXES, 0, 0, axis_index_groups=[plane[::-1] for pla...  8.51 us
    pallas_call x5, Pallas kernels, call(): pl.pallas_call(kernel, out_shape=tuple((jax.ShapeDtypeStruct(shape, kind)...  7.71 us
    ppermute x1, starting transfers between devices, shards(): lax.ppermute(far_part, 'ctx', [(i, (i - 2) % count) for i in range(count)])  6.64 us
    all_to_all x1, starting transfers between devices, shards(): lax.all_to_all(table_part.reshape(shape), AXES, 0, 0, axis_index_groups=p...  4.7 us
    all_gather x1, blocking collectives, shards(): lax.all_gather(jnp.where(odd, far_value, value_states), 'ctx', axis_index...  4.7 us
    ppermute x1, starting transfers between devices, shards(): far_value = lax.ppermute(value_states, 'ctx', ahead)  4.51 us
  transfers between devices with their start and end apart: 6, of which 2 were waited for; matrix products, arithmetic and copies ran while one was open for 4% of the time, Pallas kernels for 3%

profile of v2, /device:TPU:1, one launch (start us, length us, event | category | flops | bytes accessed | tf_op | source)
XLA Modules:
  0.0 80.8 jit_solution(15107210722174316307)
XLA Ops:
  0.6 0.0 copy-start
  0.6 0.0 copy-start.1
  0.7 0.0 copy-start.2
  0.7 0.0 copy-start.3
  0.7 4.5 %collective-permute-start.1 = (bf16[128,768]{1,0:T(8,128)(2,1)}, bf16[128,768]{1,0:T(8,128)(2,1)S(1)}, u32[]{:S(2)}, u32[]{:S(2)}) collective-permute-start(bf16[128,768]{1,0:T(8,128)(2,1)} %value_ref.1), channel_id=1, source_target_pairs={{0,4},{2,6},{4,8},{6,10},{8,12},{10,14},{12,16},{14,18},{16,20},{1... | collective-permute-start | bytes 589832 | tf_op jit(solution)/shard_map/ppermute | solution.py:213
  5.2 3.5 %collective-permute-start = (bf16[128,768]{1,0:T(8,128)(2,1)}, bf16[128,768]{1,0:T(8,128)(2,1)S(1)}, u32[]{:S(2)}, u32[]{:S(2)}) collective-permute-start(bf16[128,768]{1,0:T(8,128)(2,1)} %key_ref.3), channel_id=1, source_target_pairs={{0,4},{2,6},{4,8},{6,10},{8,12},{10,14},{12,16},{14,18},{16,20},{1... | collective-permute-start | bytes 589832 | tf_op jit(solution)/shard_map/ppermute | solution.py:212
  8.7 0.7 bitcast_subtract_fusion
  9.4 0.7 fusion
  10.1 0.8 %rev.3.table_ref = bf16[256,128]{1,0:T(8,128)(2,1)S(1)} reverse(bf16[256,128]{1,0:T(8,128)(2,1)} %param.11), dimensions={0} | reverse | bytes 131072 | tf_op jit(solution)/shard_map/rev | solution.py:211
  10.9 0.1 pad_add_fusion
  11.0 9.8 %collective-permute-done.1.far_ref = bf16[128,768]{1,0:T(8,128)(2,1)S(1)} collective-permute-done((bf16[128,768]{1,0:T(8,128)(2,1)}, bf16[128,768]{1,0:T(8,128)(2,1)S(1)}, u32[]{:S(2)}, u32[]{:S(2)}) %collective-permute-start.1) | collective-permute-done | bytes 196640 | tf_op jit(solution)/shard_map/ppermute | solution.py:213
  20.8 4.7 %all-gather = bf16[256,768]{1,0:T(8,128)(2,1)S(1)} all-gather(bf16[128,768]{1,0:T(8,128)(2,1)S(1)} %broadcast_select_fusion.1), channel_id=2, replica_groups={{0,2},{4,6},{8,10},{12,14},{16,18},{20,22},{24,26},{28,30},{32,34},{36,..., dimensions={0}, use_global_device_ids=true | all-gather | bytes 589824 | tf_op jit(solution)/shard_map/all_gather | solution.py:214
  25.5 0.1 broadcast_in_dim.2.facts_ref
  25.6 0.0 copy-done.2
  25.6 1.6 %own_scores.1 = (f32[128,768]{1,0:T(8,128)S(1)}, f32[2,128,768]{2,1,0:T(8,128)S(1)}, f32[3,128,768]{2,1,0:T(8,128)S(1)}, bf16[768,128]{1,0:T(8,128)(2,1)S(1)}) custom-call(s32[1]{0:T(128)} %bitcast.block_ref, s32[8,128]{1,0:T(8,128)S(1)} %broadcast_in_dim.2.facts_ref, bf16[128,768]{1,0:T(8,128)(2,1)S(1)} %copy-done.2, bf16[128,768]{1,0:T(8,128)(2,1)S(1)} %copy-done.3, ...), custom_call_target="tpu_custom_call" | custom-call | flops 3000000000 | tf_op jit(solution)/shard_map/own_scores/pallas_call | solution.py:38
  27.2 0.0 collective-permute-done.far_ref
  27.2 2.1 %all-gather.1 = bf16[256,768]{1,0:T(8,128)(2,1)S(1)} all-gather(bf16[128,768]{1,0:T(8,128)(2,1)S(1)} %broadcast_select_fusion), channel_id=3, replica_groups={{0,2},{4,6},{8,10},{12,14},{16,18},{20,22},{24,26},{28,30},{32,34},{36,..., dimensions={0}, use_global_device_ids=true | all-gather | bytes 589824 | tf_op jit(solution)/shard_map/all_gather | solution.py:222
  29.3 4.0 %table_part.1 = (f32[256,128]{1,0:T(8,128)}, bf16[6,128,640]{2,1,0:T(8,128)(2,1)S(1)}, bf16[6,128,384]{2,1,0:T(8,128)(2,1)S(1)}) custom-call(s32[1]{0:T(128)} %bitcast.block_ref, s32[8,128]{1,0:T(8,128)S(1)} %broadcast_in_dim.2.facts_ref, bf16[128,768]{1,0:T(8,128)(2,1)S(1)} %copy-done.2, bf16[2,128,768]{2,1,0:T(8,128)(2,1)S(1)} %bitcast.16, ...), custom_call_target="tpu_custom_call" | custom-call | flops 4000000000 | tf_op jit(solution)/shard_map/table_part/pallas_call | solution.py:38
  33.4 1.4 %block_grads.1 = (bf16[2,128,768]{2,1,0:T(8,128)(2,1)S(1)}, bf16[2,128,768]{2,1,0:T(8,128)(2,1)S(1)}, bf16[128,768]{1,0:T(8,128)(2,1)}, f32[2,128,768]{2,1,0:T(8,128)S(1)}) custom-call(s32[1]{0:T(128)} %bitcast.block_ref, bf16[128,768]{1,0:T(8,128)(2,1)S(1)} %copy-done.2, bf16[128,768]{1,0:T(8,128)(2,1)S(1)} %copy-done.3, bf16[128,768]{1,0:T(8,128)(2,1)S(1)} %copy-done.1, ...), custom_call_target="tpu_custom_call" | custom-call | flops 4000000000 | tf_op jit(solution)/shard_map/block_grads/pallas_call | solution.py:38
  34.7 4.7 %all-to-all-start = ((f32[32,8,128]{2,1,0:T(8,128)}), f32[32,8,128]{2,1,0:T(8,128)S(1)}, u32[]{:S(2)}, u32[]{:S(2)}) async-start(f32[32,8,128]{2,1,0:T(8,128)} %bitcast.7), calls=%async_computation | async-start | bytes 262144 | tf_op jit(solution)/shard_map/all_to_all | solution.py:244
  39.5 2.1 %collective-permute-start.2 = (bf16[2,128,768]{2,1,0:T(8,128)(2,1)S(1)}, bf16[2,128,768]{2,1,0:T(8,128)(2,1)S(1)}, u32[]{:S(2)}, u32[]{:S(2)}) collective-permute-start(bf16[2,128,768]{2,1,0:T(8,128)(2,1)S(1)} %get-tuple-element.33), channel_id=1, source_target_pairs={{0,510},{2,0},{4,2},{6,4},{8,6},{10,8},{12,10},{14,12},{16,14},{18... | collective-permute-start | bytes 1179656 | tf_op jit(solution)/shard_map/ppermute | solution.py:242
  41.6 6.6 %collective-permute-start.3 = (bf16[2,128,768]{2,1,0:T(8,128)(2,1)S(1)}, bf16[2,128,768]{2,1,0:T(8,128)(2,1)S(1)}, u32[]{:S(2)}, u32[]{:S(2)}) collective-permute-start(bf16[2,128,768]{2,1,0:T(8,128)(2,1)S(1)} %get-tuple-element.34), channel_id=1, source_target_pairs={{0,508},{2,510},{4,0},{6,2},{8,4},{10,6},{12,8},{14,10},{16,12},{1... | collective-permute-start | bytes 1179656 | tf_op jit(solution)/shard_map/ppermute | solution.py:243
  48.2 0.0 all-to-all-done.pieces_ref
  48.3 18.3 %all_to_all.15.pieces_ref = f32[16,8,128]{2,1,0:T(8,128)S(1)} all-to-all(f32[16,8,128]{2,1,0:T(8,128)S(1)} %plane_sum.1), channel_id=1, replica_groups={{0,4,8,12,16,20,24,28,32,36,40,44,48,52,56,60},{1,5,9,13,17,21,25,29,33..., dimensions={0} | all-to-all | bytes 131072 | tf_op jit(solution)/shard_map/all_to_all | solution.py:249
  66.6 0.7 line_sum.1
  67.3 8.5 %all-to-all-start.2 = ((f32[32,8,128]{2,1,0:T(8,128)}), f32[32,8,128]{2,1,0:T(8,128)S(1)}, u32[]{:S(2)}, u32[]{:S(2)}) async-start(f32[32,8,128]{2,1,0:T(8,128)} %line_sum.1), calls=%async_computation.2 | async-start | bytes 262144 | tf_op jit(solution)/shard_map/all_to_all | solution.py:253
  75.8 0.0 collective-permute-done.2
  75.8 0.0 collective-permute-done.3
  75.8 0.1 add_convert_fusion
  75.9 0.8 slice_bitcast_fusion
  76.7 3.4 %all-to-all-done.2 = f32[32,8,128]{2,1,0:T(8,128)S(1)} async-done(((f32[32,8,128]{2,1,0:T(8,128)}), f32[32,8,128]{2,1,0:T(8,128)S(1)}, u32[]{:S(2)}, u32[]{:S(2)}) %all-to-all-start.2) | async-done | bytes 131104 | tf_op jit(solution)/shard_map/all_to_all | solution.py:253
  80.1 0.7 copy.12
  (7 shorter events, 0.1 us)
Async XLA Ops:
  0.6 25.0 %copy-start = (bf16[128,768]{1,0:T(8,128)(2,1)S(1)}, bf16[128,768]{1,0:T(8,128)(2,1)}, u32[]{:S(2)}) copy-start(bf16[128,768]{1,0:T(8,128)(2,1)} %value_ref.1) | copy-start | bytes 589828
  0.6 25.0 %copy-start.1 = (bf16[128,768]{1,0:T(8,128)(2,1)S(1)}, bf16[128,768]{1,0:T(8,128)(2,1)}, u32[]{:S(2)}) copy-start(bf16[128,768]{1,0:T(8,128)(2,1)} %key_ref.3) | copy-start | bytes 589828
  0.7 24.9 %copy-start.2 = (bf16[128,768]{1,0:T(8,128)(2,1)S(1)}, bf16[128,768]{1,0:T(8,128)(2,1)}, u32[]{:S(2)}) copy-start(bf16[128,768]{1,0:T(8,128)(2,1)} %query_ref.5) | copy-start | bytes 589828
  0.7 24.9 %copy-start.3 = (bf16[128,768]{1,0:T(8,128)(2,1)S(1)}, bf16[128,768]{1,0:T(8,128)(2,1)}, u32[]{:S(2)}) copy-start(bf16[128,768]{1,0:T(8,128)(2,1)} %grad_ref.3) | copy-start | bytes 589828
  0.7 20.1 %collective-permute-start.1 = (bf16[128,768]{1,0:T(8,128)(2,1)}, bf16[128,768]{1,0:T(8,128)(2,1)S(1)}, u32[]{:S(2)}, u32[]{:S(2)}) collective-permute-start(bf16[128,768]{1,0:T(8,128)(2,1)} %value_ref.1), channel_id=1, source_target_pairs={{0,4},{2,6},{4,8},{6,10},{8,12},{10,14},{12,16},{14,18},{16,20},{1... | collective-permute-start | bytes 589832 | tf_op jit(solution)/shard_map/ppermute | solution.py:213
  5.2 22.0 %collective-permute-start = (bf16[128,768]{1,0:T(8,128)(2,1)}, bf16[128,768]{1,0:T(8,128)(2,1)S(1)}, u32[]{:S(2)}, u32[]{:S(2)}) collective-permute-start(bf16[128,768]{1,0:T(8,128)(2,1)} %key_ref.3), channel_id=1, source_target_pairs={{0,4},{2,6},{4,8},{6,10},{8,12},{10,14},{12,16},{14,18},{16,20},{1... | collective-permute-start | bytes 589832 | tf_op jit(solution)/shard_map/ppermute | solution.py:212
  34.7 13.5 %all-to-all-start = ((f32[32,8,128]{2,1,0:T(8,128)}), f32[32,8,128]{2,1,0:T(8,128)S(1)}, u32[]{:S(2)}, u32[]{:S(2)}) async-start(f32[32,8,128]{2,1,0:T(8,128)} %bitcast.7), calls=%async_computation | async-start | bytes 262144 | tf_op jit(solution)/shard_map/all_to_all | solution.py:244
  39.5 36.3 %collective-permute-start.2 = (bf16[2,128,768]{2,1,0:T(8,128)(2,1)S(1)}, bf16[2,128,768]{2,1,0:T(8,128)(2,1)S(1)}, u32[]{:S(2)}, u32[]{:S(2)}) collective-permute-start(bf16[2,128,768]{2,1,0:T(8,128)(2,1)S(1)} %get-tuple-element.33), channel_id=1, source_target_pairs={{0,510},{2,0},{4,2},{6,4},{8,6},{10,8},{12,10},{14,12},{16,14},{18... | collective-permute-start | bytes 1179656 | tf_op jit(solution)/shard_map/ppermute | solution.py:242
  41.6 34.2 %collective-permute-start.3 = (bf16[2,128,768]{2,1,0:T(8,128)(2,1)S(1)}, bf16[2,128,768]{2,1,0:T(8,128)(2,1)S(1)}, u32[]{:S(2)}, u32[]{:S(2)}) collective-permute-start(bf16[2,128,768]{2,1,0:T(8,128)(2,1)S(1)} %get-tuple-element.34), channel_id=1, source_target_pairs={{0,508},{2,510},{4,0},{6,2},{8,4},{10,6},{12,8},{14,10},{16,12},{1... | collective-permute-start | bytes 1179656 | tf_op jit(solution)/shard_map/ppermute | solution.py:243
  67.3 12.8 %all-to-all-start.2 = ((f32[32,8,128]{2,1,0:T(8,128)}), f32[32,8,128]{2,1,0:T(8,128)S(1)}, u32[]{:S(2)}, u32[]{:S(2)}) async-start(f32[32,8,128]{2,1,0:T(8,128)} %line_sum.1), calls=%async_computation.2 | async-start | bytes 262144 | tf_op jit(solution)/shard_map/all_to_all | solution.py:253

commit v3 on v2

--- a/solution.py
+++ b/solution.py
@@ -49,33 +49,39 @@
     )(*ins)
 
 
+def flip_kernel(flip_out):
+    row, col = iotas(flip_out.shape[0])
+    last = flip_out.shape[0] - 1
+    flip_out[...] = jnp.where(row + col == last, 1.0, 0.0).astype(flip_out.dtype)
+
+
 def own_kernel(
-    block_ref, facts_ref, query_ref, grad_ref, key_ref, value_ref, near_ref, far_ref, table_ref,
-    score_out, moved_out, dprob_out, turned_out
+    block_ref, mask_ref, shift_ref, query_ref, grad_ref, key_ref, value_ref, table_ref, flip_ref,
+    score_out, moved_out, dprob_out, turned_out, facts_out, table_out
 ):
     width, span = query_ref.shape
     rows = table_ref.shape[0]
-    other = 1 - lax.rem(block_ref[0], 2)
     row, col = iotas(width)
     seen = col <= row
+    bases = [step * width - shift_ref[0, step] for step in range(STEPS)]
     biases = [
-        jnp.where(facts_ref[STEPS + step : STEPS + step + 1, :] == 1, 0.0, -jnp.inf)
+        jnp.where((mask_ref[0, step] == 1) & (block_ref[0] >= step), 0.0, -jnp.inf)
         for step in range(STEPS)
     ]
-    place = [
-        jnp.clip(col - row + (rows - 1) - facts_ref[step : step + 1, :], 0, rows - 1)
-        for step in range(STEPS)
-    ]
+    line = lax.broadcasted_iota(jnp.int32, facts_out.shape, 0)
+    facts = jnp.zeros(facts_out.shape, jnp.int32)
+    for step in range(STEPS):
+        facts = jnp.where(line == step, bases[step], facts)
+    facts_out[...] = facts
+    place = [jnp.clip(col - row + (rows - 1) - base, 0, rows - 1) for base in bases]
     upper = [item >= width for item in place]
     place = [item & (width - 1) for item in place]
-    table = table_ref[...]
+    table = dot(flip_ref[...], table_ref[...]).astype(jnp.bfloat16)
+    table_out[...] = table
     for part in head_parts(span):
         query = query_ref[:, part]
         turned_out[part, :] = query.T
-        values = [value_ref[:, part], near_ref[other, :, part], far_ref[:, part]]
-        dprob = dot(grad_ref[:, part], jnp.concatenate(values, axis=0), NT) * SCALE
-        for step in range(STEPS):
-            dprob_out[step, :, part] = dprob[:, step * width : (step + 1) * width]
+        dprob_out[:, part] = dot(grad_ref[:, part], value_ref[:, part], NT) * SCALE
         content = dot(query, jnp.concatenate([key_ref[:, part], table], axis=0), NT) * SCALE
         relative = [content[:, at : at + width] for at in (width, 2 * width)]
         for step in range(STEPS):
@@ -88,31 +94,57 @@
 
 
 def table_kernel(
-    block_ref, facts_ref, query_ref, near_ref, far_ref, score_ref, moved_ref, dprob_ref, turned_ref,
-    table_out, terms_out, weight_out
+    block_ref, facts_ref, query_ref, grad_ref, near_key_ref, near_value_ref, far_key_ref, far_value_ref,
+    score_ref, moved_ref, dprob_ref, turned_ref, table_out, terms_out, weight_out
 ):
     width, span = query_ref.shape
     rows = table_out.shape[0]
+    parts = head_parts(span)
+    group = 3 if len(parts) % 3 == 0 else 1
     other = 1 - lax.rem(block_ref[0], 2)
     row, col = iotas(width)
     bases = [facts_ref[step : step + 1, :] for step in range(STEPS)]
     place = [col - row + (rows - 1) - base for base in bases]
-    high = [place[0] > rows - 1, place[1] > rows - 1]
-    low = place[2] < 0
+    clamps = [place[0] > rows - 1, place[1] > rows - 1, place[2] < 0]
     source = [col + row - (rows - 1) + base for base in bases]
     in_low = [(item >= 0) & (item < width) for item in source]
     in_high = [(item >= -width) & (item < 0) for item in source]
     source = [item & (width - 1) for item in source]
+    item_row = lax.broadcasted_iota(jnp.int32, (STEPS * width, rows), 0)
+    item_col = lax.broadcasted_iota(jnp.int32, (STEPS * width, rows), 1)
+    ends = item_col == jnp.where(item_row < 2 * width, rows - 1, 0)
+    ends = jnp.where(ends, 1.0, 0.0).astype(jnp.bfloat16)
     table_sum = jnp.zeros((HEAD_DIM, rows), jnp.float32)
-    for index, part in enumerate(head_parts(span)):
-        keys = jnp.concatenate([near_ref[other, :, part], far_ref[:, part]], axis=0)
-        content = dot(query_ref[:, part], keys, NT) * SCALE
-        scores = [score_ref[:, part]]
+
+    def many(item):
+        return jnp.concatenate([item] * group, axis=0)
+
+    for start in range(0, len(parts), group):
+        mine = parts[start : start + group]
+
+        def heads(load):
+            return jnp.concatenate([load(part) for part in mine], axis=0)
+
+        def products(left_ref, near_ref, far_ref):
+            return heads(
+                lambda part: dot(
+                    left_ref[:, part],
+                    jnp.concatenate([near_ref[other, :, part], far_ref[:, part]], axis=0),
+                    NT,
+                )
+            ) * SCALE
+
+        content = products(query_ref, near_key_ref, far_key_ref)
+        dprob = products(grad_ref, near_value_ref, far_value_ref)
+        scores = [heads(lambda part: score_ref[:, part])]
+        dprobs = [heads(lambda part: dprob_ref[:, part])]
         for step in range(1, STEPS):
-            scores.append(content[:, (step - 1) * width : step * width] + moved_ref[step - 1, :, part])
-        top = jnp.max(jnp.maximum(jnp.maximum(scores[0], scores[1]), scores[2]), axis=1, keepdims=True)
+            at = slice((step - 1) * width, step * width)
+            scores.append(content[:, at] + heads(lambda part: moved_ref[step - 1, :, part]))
+            dprobs.append(dprob[:, at])
+        top = jnp.maximum(jnp.maximum(scores[0], scores[1]), scores[2])
+        top = jnp.max(top, axis=1, keepdims=True)
         exps = [jnp.exp(score - top) for score in scores]
-        dprobs = [dprob_ref[step, :, part] for step in range(STEPS)]
         total = jnp.sum(exps[0] + exps[1] + exps[2], axis=1, keepdims=True)
         mixed = exps[0] * dprobs[0] + exps[1] * dprobs[1] + exps[2] * dprobs[2]
         mixed = jnp.sum(mixed, axis=1, keepdims=True)
@@ -120,22 +152,25 @@
         delta = mixed * inverse
         probs = [item * inverse for item in exps]
         dscores = [p * (d - delta) for p, d in zip(probs, dprobs)]
-        over = jnp.where(high[0], dscores[0], 0.0) + jnp.where(high[1], dscores[1], 0.0)
-        over = jnp.sum(over, axis=1, keepdims=True)
-        under = jnp.sum(jnp.where(low, dscores[2], 0.0), axis=1, keepdims=True)
-        moved = [lanes(item, at) for item, at in zip(dscores, source)]
-        below = jnp.where(in_low[1], moved[1], 0.0) + jnp.where(in_low[2], moved[2], 0.0)
-        above = jnp.where(in_high[0], moved[0], 0.0) + jnp.where(in_high[1], moved[1], 0.0)
-        above = above + jnp.where(in_high[2], moved[2], 0.0)
-        below = below + jnp.where(col == 0, under, 0.0)
-        above = above + jnp.where(col == width - 1, over, 0.0)
-        relative = jnp.concatenate([below, above], axis=1).astype(jnp.bfloat16)
-        table_sum = table_sum + dot(turned_ref[part, :], relative)
-        for step in range(STEPS):
-            at = slice(step * width, (step + 1) * width)
-            terms_out[index, :, at] = dscores[step].astype(jnp.bfloat16)
-            weight_out[index, :, at] = probs[step].astype(jnp.bfloat16)
-        terms_out[index, :, STEPS * width :] = relative
+        rounded = [item.astype(jnp.bfloat16) for item in dscores]
+        moved = [lanes(item, many(at)) for item, at in zip(dscores, source)]
+        below = jnp.where(many(in_low[1]), moved[1], 0.0) + jnp.where(many(in_low[2]), moved[2], 0.0)
+        above = jnp.where(many(in_high[0]), moved[0], 0.0) + jnp.where(many(in_high[1]), moved[1], 0.0)
+        above = above + jnp.where(many(in_high[2]), moved[2], 0.0)
+        clamped = [
+            jnp.where(many(mask), item, 0.0).astype(jnp.bfloat16)
+            for mask, item in zip(clamps, dscores)
+        ]
+        clamped = dot(jnp.concatenate(clamped, axis=1), ends)
+        relative = (jnp.concatenate([below, above], axis=1) + clamped).astype(jnp.bfloat16)
+        for at, part in enumerate(mine):
+            here = slice(at * width, (at + 1) * width)
+            table_sum = table_sum + dot(turned_ref[part, :], relative[here])
+            for step in range(STEPS):
+                to = slice(step * width, (step + 1) * width)
+                terms_out[start + at, :, to] = rounded[step][here]
+                weight_out[start + at, :, to] = probs[step][here].astype(jnp.bfloat16)
+            terms_out[start + at, :, STEPS * width :] = relative[here]
     table_out[...] = table_sum.T
 
 
@@ -172,19 +207,24 @@
 
 
 def rings(count, head):
-    depth = 32
-    columns = count // depth
-    planes = [
-        [
-            (column * depth + z * 2 + core) * head + half
+    depth = 16
+    columns = count // (2 * depth)
+    lead = 9
+    planes = []
+    for z in range(depth):
+        plane = [
+            (column * 2 * depth + z * 2 + core) * head + half
             for column in range(columns)
             for core in range(2)
             for half in range(head)
         ]
-        for z in range(depth // 2)
-    ]
+        far = plane.pop(len(plane) * 9 // 32)
+        planes.append(plane + [far])
     lines = [
-        [(column * depth + z * 2 + core) * head + half for z in range(depth // 2)]
+        [
+            (column * 2 * depth + (z + lead) % depth * 2 + core) * head + half
+            for z in range(depth)
+        ]
         for column in range(columns)
         for core in range(2)
         for half in range(head)
@@ -204,21 +244,24 @@
     one, two, three = (width, span), (2, width, span), (STEPS, width, span)
     bf, f32 = jnp.bfloat16, jnp.float32
     scalar, local = [pltpu.SMEM], [pltpu.VMEM]
-    step = jnp.arange(STEPS, dtype=jnp.int32)
-    visible = (block_mask[0] == 1) & (block[0] >= step)
-    facts = [step * width - distance_shift[0], visible.astype(jnp.int32), step[:2]]
-    facts = jnp.broadcast_to(jnp.concatenate(facts)[:, None], (8, width))
-    table = rel_table[::-1]
+    far_value = lax.ppermute(value_states, "ctx", ahead)
     far_key = lax.ppermute(key_states, "ctx", ahead)
-    far_value = lax.ppermute(value_states, "ctx", ahead)
+    (flip,) = call(flip_kernel, (((rows, rows), bf),), (), [], [], 10, "flip")
+    score, moved, dprob, turned, facts, table = call(
+        own_kernel,
+        (
+            (one, f32), (two, f32), (one, f32), ((span, width), bf), ((8, width), jnp.int32),
+            (rel_table.shape, bf),
+        ),
+        (
+            block, block_mask, distance_shift, queries, out_grad, key_states, value_states,
+            rel_table, flip,
+        ),
+        scalar * 3 + local * 6, [], 3, "own_scores",
+    )
+    far_value, score = lax.optimization_barrier((far_value, score))
     near_value = lax.all_gather(jnp.where(odd, far_value, value_states), "ctx", axis_index_groups=pairs)
-    score, moved, dprob, turned = call(
-        own_kernel,
-        ((one, f32), (two, f32), (three, f32), ((span, width), bf)),
-        (block, facts, queries, out_grad, key_states, value_states, near_value, far_value, table),
-        scalar + local * 8, [], 3, "own_scores",
-    )
-    far_key, score = lax.optimization_barrier((far_key, score))
+    far_key, near_value = lax.optimization_barrier((far_key, near_value))
     near_key = lax.all_gather(jnp.where(odd, far_key, key_states), "ctx", axis_index_groups=pairs)
     table_part, terms, weight = call(
         table_kernel,
@@ -226,8 +269,11 @@
             ((rows, HEAD_DIM), f32), ((heads, width, STEPS * width + rows), bf),
             ((heads, width, STEPS * width), bf),
         ),
-        (block, facts, queries, near_key, far_key, score, moved, dprob, turned),
-        scalar + local * 8, [], 4, "table_part",
+        (
+            block, facts, queries, out_grad, near_key, near_value, far_key, far_value,
+            score, moved, dprob, turned,
+        ),
+        scalar + local * 11, [], 4, "table_part",
     )
     near_part, far_part, query_grad, own = call(
         grads_kernel,

time: 81.3 us -> 74.4 us (0.915)
  blocking collectives: 25.1 us -> 21.1 us
  waiting for transfers between devices: 13.2 us -> 10.8 us
  other arithmetic: 1.57 us -> 0.16 us
    all_to_all x1, blocking collectives: 18.3 us -> 14.4 us  [shards(): pieces = lax.all_to_all(copies, AXES, 0, 0, axis_index_groups=lines)]
    all_to_all x1, waiting for transfers between devices: 3.41 us -> 1.77 us  [shards(): lax.all_to_all(copies, AXES, 0, 0, axis_index_groups=[plane[::-1] for pla...]
    ppermute x1, waiting for transfers between devices: 9.81 us -> 8.62 us  [shards(): far_value = lax.ppermute(value_states, 'ctx', ahead)]
    all_to_all x1, starting transfers between devices: 8.51 us -> 9.68 us  [shards(): lax.all_to_all(copies, AXES, 0, 0, axis_index_groups=[plane[::-1] for pla...]
    unnamed x9 -> x15, local copies, waits for them, and re-layouts: 0.67 us -> 1.79 us
    all_gather x1, blocking collectives: 4.7 us -> 3.77 us  [shards(): lax.all_gather(jnp.where(odd, far_value, value_states), 'ctx', axis_index...]
    all_gather x1, blocking collectives: 2.09 us -> 2.95 us  [shards(): lax.all_gather(jnp.where(odd, far_key, key_states), 'ctx', axis_index_gro...]
    rev x1 -> x0, local copies, waits for them, and re-layouts: 0.82 us -> none  [shards(): table = rel_table[::-1]]
  transfers between devices with their start and end apart: 6 -> 6, of which waited for: 2 -> 3; matrix products, arithmetic and copies ran while one was open for 4% -> 1% of each run, Pallas kernels for 3% -> 4%
where the time goes in v3:
time: 74.4 us; the launch traced here: 73.3 us
  starting transfers between devices  30.8 us (41%)
  blocking collectives  21.1 us (28%)
  waiting for transfers between devices  10.8 us (15%)
  Pallas kernels  7.11 us (10%)
  local copies, waits for them, and re-layouts  2.56 us (3%)
  between operations  0.81 us (1%)
    all_to_all x1, blocking collectives, shards(): pieces = lax.all_to_all(copies, AXES, 0, 0, axis_index_groups=lines)  14.4 us
    all_to_all x1, starting transfers between devices, shards(): lax.all_to_all(copies, AXES, 0, 0, axis_index_groups=[plane[::-1] for pla...  9.68 us
    ppermute x1, waiting for transfers between devices, shards(): far_value = lax.ppermute(value_states, 'ctx', ahead)  8.62 us
    pallas_call x6, Pallas kernels, call(): pl.pallas_call(kernel, out_shape=tuple((jax.ShapeDtypeStruct(shape, kind)...  7.11 us
    ppermute x1, starting transfers between devices, shards(): lax.ppermute(far_part, 'ctx', [(i, (i - 2) % count) for i in range(count)])  6.31 us
    all_to_all x1, starting transfers between devices, shards(): lax.all_to_all(table_part.reshape(shape), AXES, 0, 0, axis_index_groups=p...  4.7 us
    ppermute x1, starting transfers between devices, shards(): far_value = lax.ppermute(value_states, 'ctx', ahead)  4.37 us
    all_gather x1, blocking collectives, shards(): lax.all_gather(jnp.where(odd, far_value, value_states), 'ctx', axis_index...  3.77 us
  transfers between devices with their start and end apart: 6, of which 3 were waited for; matrix products, arithmetic and copies ran while one was open for 1% of the time, Pallas kernels for 4%

profile of v3, /device:TPU:1, one launch (start us, length us, event | category | flops | bytes accessed | tf_op | source)
XLA Modules:
  0.0 73.3 jit_solution(6968529790552675515)
XLA Ops:
  0.6 4.4 %collective-permute-start.1 = (bf16[128,768]{1,0:T(8,128)(2,1)}, bf16[128,768]{1,0:T(8,128)(2,1)S(1)}, u32[]{:S(2)}, u32[]{:S(2)}) collective-permute-start(bf16[128,768]{1,0:T(8,128)(2,1)} %value_ref.1), channel_id=1, source_target_pairs={{0,4},{2,6},{4,8},{6,10},{8,12},{10,14},{12,16},{14,18},{16,20},{1... | collective-permute-start | bytes 589832 | tf_op jit(solution)/shard_map/ppermute | solution.py:247
  5.0 3.5 %collective-permute-start = (bf16[128,768]{1,0:T(8,128)(2,1)}, bf16[128,768]{1,0:T(8,128)(2,1)S(1)}, u32[]{:S(2)}, u32[]{:S(2)}) collective-permute-start(bf16[128,768]{1,0:T(8,128)(2,1)} %key_ref.3), channel_id=1, source_target_pairs={{0,4},{2,6},{4,8},{6,10},{8,12},{10,14},{12,16},{14,18},{16,20},{1... | collective-permute-start | bytes 589832 | tf_op jit(solution)/shard_map/ppermute | solution.py:248
  8.6 0.0 copy-start
  8.6 0.0 copy-start.1
  8.6 0.0 copy-start.2
  8.6 0.0 copy-start.3
  8.7 0.0 copy-start.5
  8.7 0.0 copy-start.6
  8.7 0.8 %copy-done = bf16[128,768]{1,0:T(8,128)(2,1)S(1)} copy-done((bf16[128,768]{1,0:T(8,128)(2,1)S(1)}, bf16[128,768]{1,0:T(8,128)(2,1)}, u32[]{:S(2)}) %copy-start) | copy-done | bytes 196632
  9.5 0.1 copy-done.1
  9.6 0.1 copy-done.2
  9.7 0.1 copy-done.3
  9.8 2.2 %own_scores.1 = (f32[128,768]{1,0:T(8,128)S(1)}, f32[2,128,768]{2,1,0:T(8,128)S(1)}, f32[128,768]{1,0:T(8,128)S(1)}, bf16[768,128]{1,0:T(8,128)(2,1)S(1)}, s32[8...) custom-call(s32[1]{0:T(128)} %bitcast.block_ref, s32[1,3]{1,0:T(1,128)S(1)} %copy-done.5, s32[1,3]{1,0:T(1,128)S(1)} %copy-done.6, ...), custom_call_target="tpu_custom_call" | custom-call | flops 3000000000 | tf_op jit(solution)/shard_map/own_scores/pallas_call | solution.py:38
  12.0 8.6 %collective-permute-done.1.far_value_ref = bf16[128,768]{1,0:T(8,128)(2,1)S(1)} collective-permute-done((bf16[128,768]{1,0:T(8,128)(2,1)}, bf16[128,768]{1,0:T(8,128)(2,1)S(1)}, u32[]{:S(2)}, u32[]{:S(2)}) %collective-permute-start.1) | collective-permute-done | bytes 196640 | tf_op jit(solution)/shard_map/ppermute | solution.py:247
  20.6 3.8 %all-gather = bf16[256,768]{1,0:T(8,128)(2,1)S(1)} all-gather(bf16[128,768]{1,0:T(8,128)(2,1)S(1)} %broadcast_select_fusion.1), channel_id=2, replica_groups={{0,2},{4,6},{8,10},{12,14},{16,18},{20,22},{24,26},{28,30},{32,34},{36,..., dimensions={0}, use_global_device_ids=true | all-gather | bytes 589824 | tf_op jit(solution)/shard_map/all_gather | solution.py:263
  24.4 0.4 collective-permute-done.far_key_ref.far_ref
  24.9 2.9 %all-gather.1 = bf16[256,768]{1,0:T(8,128)(2,1)S(1)} all-gather(bf16[128,768]{1,0:T(8,128)(2,1)S(1)} %broadcast_select_fusion), channel_id=3, replica_groups={{0,2},{4,6},{8,10},{12,14},{16,18},{20,22},{24,26},{28,30},{32,34},{36,..., dimensions={0}, use_global_device_ids=true | all-gather | bytes 589824 | tf_op jit(solution)/shard_map/all_gather | solution.py:265
  27.8 2.8 %table_part.1 = (f32[256,128]{1,0:T(8,128)}, bf16[6,128,640]{2,1,0:T(8,128)(2,1)S(1)}, bf16[6,128,384]{2,1,0:T(8,128)(2,1)S(1)}) custom-call(s32[1]{0:T(128)} %bitcast.block_ref, s32[8,128]{1,0:T(8,128)S(1)} %get-tuple-element.28.facts_ref, bf16[128,768]{1,0:T(8,128)(2,1)S(1)} %copy-done.2, bf16[128,768]{1,0:T(8,128)(2,1)S(1)} %copy-done.3, ...), custom_call_target="tpu_custom_call" | custom-call | flops 4000000000 | tf_op jit(solution)/shard_map/table_part/pallas_call | solution.py:38
  30.6 1.4 %block_grads.1 = (bf16[2,128,768]{2,1,0:T(8,128)(2,1)S(1)}, bf16[2,128,768]{2,1,0:T(8,128)(2,1)S(1)}, bf16[128,768]{1,0:T(8,128)(2,1)}, f32[2,128,768]{2,1,0:T(8,128)S(1)}) custom-call(s32[1]{0:T(128)} %bitcast.block_ref, bf16[128,768]{1,0:T(8,128)(2,1)S(1)} %copy-done.2, bf16[128,768]{1,0:T(8,128)(2,1)S(1)} %copy-done.3, bf16[128,768]{1,0:T(8,128)(2,1)S(1)} %copy-done.1, ...), custom_call_target="tpu_custom_call" | custom-call | flops 4000000000 | tf_op jit(solution)/shard_map/block_grads/pallas_call | solution.py:38
  32.0 4.7 %all-to-all-start = ((f32[32,8,128]{2,1,0:T(8,128)}), f32[32,8,128]{2,1,0:T(8,128)S(1)}, u32[]{:S(2)}, u32[]{:S(2)}) async-start(f32[32,8,128]{2,1,0:T(8,128)} %bitcast.5), calls=%async_computation | async-start | bytes 262144 | tf_op jit(solution)/shard_map/all_to_all | solution.py:290
  36.7 2.1 %collective-permute-start.2 = (bf16[2,128,768]{2,1,0:T(8,128)(2,1)S(1)}, bf16[2,128,768]{2,1,0:T(8,128)(2,1)S(1)}, u32[]{:S(2)}, u32[]{:S(2)}) collective-permute-start(bf16[2,128,768]{2,1,0:T(8,128)(2,1)S(1)} %get-tuple-element.41), channel_id=1, source_target_pairs={{0,510},{2,0},{4,2},{6,4},{8,6},{10,8},{12,10},{14,12},{16,14},{18... | collective-permute-start | bytes 1179656 | tf_op jit(solution)/shard_map/ppermute | solution.py:288
  38.8 6.3 %collective-permute-start.3 = (bf16[2,128,768]{2,1,0:T(8,128)(2,1)S(1)}, bf16[2,128,768]{2,1,0:T(8,128)(2,1)S(1)}, u32[]{:S(2)}, u32[]{:S(2)}) collective-permute-start(bf16[2,128,768]{2,1,0:T(8,128)(2,1)S(1)} %get-tuple-element.42), channel_id=1, source_target_pairs={{0,508},{2,510},{4,0},{6,2},{8,4},{10,6},{12,8},{14,10},{16,12},{1... | collective-permute-start | bytes 1179656 | tf_op jit(solution)/shard_map/ppermute | solution.py:289
  45.2 0.0 all-to-all-done.pieces_ref
  45.2 14.4 %all_to_all.15.pieces_ref = f32[16,8,128]{2,1,0:T(8,128)S(1)} all-to-all(f32[16,8,128]{2,1,0:T(8,128)S(1)} %plane_sum.1), channel_id=1, replica_groups={{36,40,44,48,52,56,60,0,4,8,12,16,20,24,28,32},{37,41,45,49,53,57,61,1,..., dimensions={0} | all-to-all | bytes 131072 | tf_op jit(solution)/shard_map/all_to_all | solution.py:295
  59.6 0.7 line_sum.1
  60.3 9.7 %all-to-all-start.2 = ((f32[32,8,128]{2,1,0:T(8,128)}), f32[32,8,128]{2,1,0:T(8,128)S(1)}, u32[]{:S(2)}, u32[]{:S(2)}) async-start(f32[32,8,128]{2,1,0:T(8,128)} %line_sum.1), calls=%async_computation.2 | async-start | bytes 262144 | tf_op jit(solution)/shard_map/all_to_all | solution.py:299
  70.0 0.0 collective-permute-done.2
  70.0 0.0 collective-permute-done.3
  70.0 0.1 add_convert_fusion
  70.1 0.8 %slice_bitcast_fusion = (bf16[128,768]{1,0:T(8,128)(2,1)}, bf16[128,768]{1,0:T(8,128)(2,1)}) fusion(bf16[2,128,768]{2,1,0:T(8,128)(2,1)S(1)} %add_convert_fusion), kind=kLoop, calls=%fused_computation.1 | loop fusion | bytes 786432 | tf_op jit(solution)/shard_map/squeeze | solution.py:303
  70.9 1.8 %all-to-all-done.2 = f32[32,8,128]{2,1,0:T(8,128)S(1)} async-done(((f32[32,8,128]{2,1,0:T(8,128)}), f32[32,8,128]{2,1,0:T(8,128)S(1)}, u32[]{:S(2)}, u32[]{:S(2)}) %all-to-all-start.2) | async-done | bytes 131104 | tf_op jit(solution)/shard_map/all_to_all | solution.py:299
  72.7 0.7 copy.12
  (8 shorter events, 0.1 us)
Async XLA Ops:
  0.6 20.0 %collective-permute-start.1 = (bf16[128,768]{1,0:T(8,128)(2,1)}, bf16[128,768]{1,0:T(8,128)(2,1)S(1)}, u32[]{:S(2)}, u32[]{:S(2)}) collective-permute-start(bf16[128,768]{1,0:T(8,128)(2,1)} %value_ref.1), channel_id=1, source_target_pairs={{0,4},{2,6},{4,8},{6,10},{8,12},{10,14},{12,16},{14,18},{16,20},{1... | collective-permute-start | bytes 589832 | tf_op jit(solution)/shard_map/ppermute | solution.py:247
  5.0 19.8 %collective-permute-start = (bf16[128,768]{1,0:T(8,128)(2,1)}, bf16[128,768]{1,0:T(8,128)(2,1)S(1)}, u32[]{:S(2)}, u32[]{:S(2)}) collective-permute-start(bf16[128,768]{1,0:T(8,128)(2,1)} %key_ref.3), channel_id=1, source_target_pairs={{0,4},{2,6},{4,8},{6,10},{8,12},{10,14},{12,16},{14,18},{16,20},{1... | collective-permute-start | bytes 589832 | tf_op jit(solution)/shard_map/ppermute | solution.py:248
  8.6 0.9 %copy-start = (bf16[128,768]{1,0:T(8,128)(2,1)S(1)}, bf16[128,768]{1,0:T(8,128)(2,1)}, u32[]{:S(2)}) copy-start(bf16[128,768]{1,0:T(8,128)(2,1)} %value_ref.1) | copy-start | bytes 589828
  8.6 1.0 %copy-start.1 = (bf16[128,768]{1,0:T(8,128)(2,1)S(1)}, bf16[128,768]{1,0:T(8,128)(2,1)}, u32[]{:S(2)}) copy-start(bf16[128,768]{1,0:T(8,128)(2,1)} %key_ref.3) | copy-start | bytes 589828
  8.6 1.1 %copy-start.2 = (bf16[128,768]{1,0:T(8,128)(2,1)S(1)}, bf16[128,768]{1,0:T(8,128)(2,1)}, u32[]{:S(2)}) copy-start(bf16[128,768]{1,0:T(8,128)(2,1)} %query_ref.5) | copy-start | bytes 589828
  8.6 1.2 %copy-start.3 = (bf16[128,768]{1,0:T(8,128)(2,1)S(1)}, bf16[128,768]{1,0:T(8,128)(2,1)}, u32[]{:S(2)}) copy-start(bf16[128,768]{1,0:T(8,128)(2,1)} %grad_ref.5) | copy-start | bytes 589828
  8.6 1.2 %copy-start.4 = (bf16[256,128]{1,0:T(8,128)(2,1)S(1)}, bf16[256,128]{1,0:T(8,128)(2,1)}, u32[]{:S(2)}) copy-start(bf16[256,128]{1,0:T(8,128)(2,1)} %table_ref.1) | copy-start | bytes 196612
  8.7 1.1 %copy-start.5 = (s32[1,3]{1,0:T(1,128)S(1)}, s32[1,3]{1,0:T(1,128)}, u32[]{:S(2)}) copy-start(s32[1,3]{1,0:T(1,128)} %mask_ref.1) | copy-start | bytes 40
  8.7 1.1 %copy-start.6 = (s32[1,3]{1,0:T(1,128)S(1)}, s32[1,3]{1,0:T(1,128)}, u32[]{:S(2)}) copy-start(s32[1,3]{1,0:T(1,128)} %shift_ref.1) | copy-start | bytes 40
  32.0 13.2 %all-to-all-start = ((f32[32,8,128]{2,1,0:T(8,128)}), f32[32,8,128]{2,1,0:T(8,128)S(1)}, u32[]{:S(2)}, u32[]{:S(2)}) async-start(f32[32,8,128]{2,1,0:T(8,128)} %bitcast.5), calls=%async_computation | async-start | bytes 262144 | tf_op jit(solution)/shard_map/all_to_all | solution.py:290
  36.7 33.3 %collective-permute-start.2 = (bf16[2,128,768]{2,1,0:T(8,128)(2,1)S(1)}, bf16[2,128,768]{2,1,0:T(8,128)(2,1)S(1)}, u32[]{:S(2)}, u32[]{:S(2)}) collective-permute-start(bf16[2,128,768]{2,1,0:T(8,128)(2,1)S(1)} %get-tuple-element.41), channel_id=1, source_target_pairs={{0,510},{2,0},{4,2},{6,4},{8,6},{10,8},{12,10},{14,12},{16,14},{18... | collective-permute-start | bytes 1179656 | tf_op jit(solution)/shard_map/ppermute | solution.py:288
  38.8 31.1 %collective-permute-start.3 = (bf16[2,128,768]{2,1,0:T(8,128)(2,1)S(1)}, bf16[2,128,768]{2,1,0:T(8,128)(2,1)S(1)}, u32[]{:S(2)}, u32[]{:S(2)}) collective-permute-start(bf16[2,128,768]{2,1,0:T(8,128)(2,1)S(1)} %get-tuple-element.42), channel_id=1, source_target_pairs={{0,508},{2,510},{4,0},{6,2},{8,4},{10,6},{12,8},{14,10},{16,12},{1... | collective-permute-start | bytes 1179656 | tf_op jit(solution)/shard_map/ppermute | solution.py:289
  60.3 12.4 %all-to-all-start.2 = ((f32[32,8,128]{2,1,0:T(8,128)}), f32[32,8,128]{2,1,0:T(8,128)S(1)}, u32[]{:S(2)}, u32[]{:S(2)}) async-start(f32[32,8,128]{2,1,0:T(8,128)} %line_sum.1), calls=%async_computation.2 | async-start | bytes 262144 | tf_op jit(solution)/shard_map/all_to_all | solution.py:299

commit v4 on v3

--- a/solution.py
+++ b/solution.py
@@ -206,6 +206,13 @@
         copies_out[index] = total
 
 
+def final_kernel(own_ref, near_ref, far_ref, table_ref, key_out, value_out, table_out):
+    for slot, out in enumerate((key_out, value_out)):
+        total = own_ref[slot] + near_ref[slot].astype(jnp.float32) + far_ref[slot].astype(jnp.float32)
+        out[...] = total.astype(out.dtype)
+    table_out[...] = table_ref[...]
+
+
 def rings(count, head):
     depth = 16
     columns = count // (2 * depth)
@@ -286,21 +293,25 @@
     shape = (len(planes[0]), small, HEAD_DIM)
     table_part, near_part, far_part = lax.optimization_barrier((table_part, near_part, far_part))
     near_part = lax.ppermute(near_part, "ctx", [(i, (i - 1) % count) for i in range(count)])
-    far_part = lax.ppermute(far_part, "ctx", [(i, (i - 2) % count) for i in range(count)])
     pieces = lax.all_to_all(table_part.reshape(shape), AXES, 0, 0, axis_index_groups=planes)
     (copies,) = call(
         functools.partial(spread_kernel, True),
         (((len(lines[0]), small, HEAD_DIM), f32),), (pieces,), local, [], 40, "plane_sum",
     )
+    copies, far_part = lax.optimization_barrier((copies, far_part))
+    far_part = lax.ppermute(far_part, "ctx", [(i, (i - 2) % count) for i in range(count)])
     pieces = lax.all_to_all(copies, AXES, 0, 0, axis_index_groups=lines)
     (copies,) = call(
-        functools.partial(spread_kernel, False), ((shape, f32),), (pieces,), local, [], 1, "line_sum",
+        functools.partial(spread_kernel, False), ((shape, f32),), (pieces,), local, [], 4, "line_sum",
     )
     copies = lax.all_to_all(copies, AXES, 0, 0, axis_index_groups=[plane[::-1] for plane in planes])
-    table_grad = copies.reshape(rows, HEAD_DIM)
-    total = own + near_part.astype(f32) + far_part.astype(f32)
-    total = total.astype(bf)
-    return query_grad, total[0], total[1], table_grad
+    key_grad, value_grad, table_grad = call(
+        final_kernel,
+        ((one, bf), (one, bf), ((rows, HEAD_DIM), f32)),
+        (own, near_part, far_part, copies.reshape(rows, HEAD_DIM)),
+        local * 4, [], 1, "final_sums",
+    )
+    return query_grad, key_grad, value_grad, table_grad
 
 
 def solution(mesh):

time: 74.4 us -> 72.5 us (0.974)
  blocking collectives: 21.1 us -> 18.9 us
  local copies, waits for them, and re-layouts: 2.56 us -> 1.13 us
  waiting for transfers between devices: 10.8 us -> 11.7 us
  Pallas kernels: 7.11 us -> 7.99 us
  starting transfers between devices: 30.8 us -> 31.6 us
    all_to_all x1, starting transfers between devices: 4.7 us -> 10.6 us  [shards(): pieces = lax.all_to_all(copies, AXES, 0, 0, axis_index_groups=lines)]
    ppermute x1, starting transfers between devices: 6.31 us -> 2.84 us  [shards(): lax.ppermute(far_part, 'ctx', [(i, (i - 2) % count) for i in range(count)])]
    all_to_all x1, starting transfers between devices: 9.68 us -> 7.34 us  [shards(): lax.all_to_all(copies, AXES, 0, 0, axis_index_groups=[plane[::-1] for pla...]
    all_to_all x1, blocking collectives: 14.4 us -> 12.2 us  [shards(): lax.all_to_all(table_part.reshape(shape), AXES, 0, 0, axis_index_groups=p...]
    all_to_all x1, waiting for transfers between devices: 1.77 us -> 2.67 us  [shards(): lax.all_to_all(copies, AXES, 0, 0, axis_index_groups=[plane[::-1] for pla...]
    pallas_call x6 -> x7, Pallas kernels: 7.11 us -> 7.99 us  [call(): pl.pallas_call(kernel, out_shape=tuple((jax.ShapeDtypeStruct(shape, kind)...]
    squeeze x1 -> x0, local copies, waits for them, and re-layouts: 0.77 us -> none  [shards(): return (query_grad, total[0], total[1], table_grad)]
    unnamed x15 -> x14, local copies, waits for them, and re-layouts: 1.79 us -> 1.13 us
  transfers between devices with their start and end apart: 6 -> 6, of which waited for: 3 -> 3; matrix products, arithmetic and copies ran while one was open for 1% -> 0% of each run, Pallas kernels for 4% -> 4%
where the time goes in v4:
time: 72.5 us; the launch traced here: 72.1 us
  starting transfers between devices  31.6 us (44%)
  blocking collectives  18.9 us (26%)
  waiting for transfers between devices  11.7 us (16%)
  Pallas kernels  7.99 us (11%)
  local copies, waits for them, and re-layouts  1.13 us (2%)
  between operations  0.79 us (1%)
    all_to_all x1, blocking collectives, shards(): lax.all_to_all(table_part.reshape(shape), AXES, 0, 0, axis_index_groups=p...  12.2 us
    all_to_all x1, starting transfers between devices, shards(): pieces = lax.all_to_all(copies, AXES, 0, 0, axis_index_groups=lines)  10.6 us
    ppermute x1, waiting for transfers between devices, shards(): far_value = lax.ppermute(value_states, 'ctx', ahead)  8.62 us
    pallas_call x7, Pallas kernels, call(): pl.pallas_call(kernel, out_shape=tuple((jax.ShapeDtypeStruct(shape, kind)...  7.99 us
    all_to_all x1, starting transfers between devices, shards(): lax.all_to_all(copies, AXES, 0, 0, axis_index_groups=[plane[::-1] for pla...  7.34 us
    ppermute x1, starting transfers between devices, shards(): far_value = lax.ppermute(value_states, 'ctx', ahead)  4.37 us
    all_gather x1, blocking collectives, shards(): lax.all_gather(jnp.where(odd, far_value, value_states), 'ctx', axis_index...  3.77 us
    ppermute x1, starting transfers between devices, shards(): far_key = lax.ppermute(key_states, 'ctx', ahead)  3.55 us
  transfers between devices with their start and end apart: 6, of which 3 were waited for; matrix products, arithmetic and copies ran while one was open for 0% of the time, Pallas kernels for 4%

profile of v4, /device:TPU:1, one launch (start us, length us, event | category | flops | bytes accessed | tf_op | source)
XLA Modules:
  0.0 72.1 jit_solution(10787469413701084183)
XLA Ops:
  0.6 4.4 %collective-permute-start.1 = (bf16[128,768]{1,0:T(8,128)(2,1)}, bf16[128,768]{1,0:T(8,128)(2,1)S(1)}, u32[]{:S(2)}, u32[]{:S(2)}) collective-permute-start(bf16[128,768]{1,0:T(8,128)(2,1)} %value_ref.1), channel_id=1, source_target_pairs={{0,4},{2,6},{4,8},{6,10},{8,12},{10,14},{12,16},{14,18},{16,20},{1... | collective-permute-start | bytes 589832 | tf_op jit(solution)/shard_map/ppermute | solution.py:254
  5.0 3.5 %collective-permute-start = (bf16[128,768]{1,0:T(8,128)(2,1)}, bf16[128,768]{1,0:T(8,128)(2,1)S(1)}, u32[]{:S(2)}, u32[]{:S(2)}) collective-permute-start(bf16[128,768]{1,0:T(8,128)(2,1)} %key_ref.3), channel_id=1, source_target_pairs={{0,4},{2,6},{4,8},{6,10},{8,12},{10,14},{12,16},{14,18},{16,20},{1... | collective-permute-start | bytes 589832 | tf_op jit(solution)/shard_map/ppermute | solution.py:255
  8.6 0.0 copy-start
  8.6 0.0 copy-start.1
  8.6 0.0 copy-start.2
  8.6 0.0 copy-start.3
  8.6 0.0 copy-start.4
  8.7 0.0 copy-start.5
  8.7 0.0 copy-start.6
  8.7 0.8 %copy-done = bf16[128,768]{1,0:T(8,128)(2,1)S(1)} copy-done((bf16[128,768]{1,0:T(8,128)(2,1)S(1)}, bf16[128,768]{1,0:T(8,128)(2,1)}, u32[]{:S(2)}) %copy-start) | copy-done | bytes 196632
  9.5 0.1 copy-done.1
  9.6 0.1 copy-done.2
  9.7 0.1 copy-done.3
  9.8 2.2 %own_scores.1 = (f32[128,768]{1,0:T(8,128)S(1)}, f32[2,128,768]{2,1,0:T(8,128)S(1)}, f32[128,768]{1,0:T(8,128)S(1)}, bf16[768,128]{1,0:T(8,128)(2,1)S(1)}, s32[8...) custom-call(s32[1]{0:T(128)} %bitcast.block_ref, s32[1,3]{1,0:T(1,128)S(1)} %copy-done.5, s32[1,3]{1,0:T(1,128)S(1)} %copy-done.6, ...), custom_call_target="tpu_custom_call" | custom-call | flops 3000000000 | tf_op jit(solution)/shard_map/own_scores/pallas_call | solution.py:38
  12.0 8.6 %collective-permute-done.1.far_value_ref = bf16[128,768]{1,0:T(8,128)(2,1)S(1)} collective-permute-done((bf16[128,768]{1,0:T(8,128)(2,1)}, bf16[128,768]{1,0:T(8,128)(2,1)S(1)}, u32[]{:S(2)}, u32[]{:S(2)}) %collective-permute-start.1) | collective-permute-done | bytes 196640 | tf_op jit(solution)/shard_map/ppermute | solution.py:254
  20.6 3.8 %all-gather = bf16[256,768]{1,0:T(8,128)(2,1)S(1)} all-gather(bf16[128,768]{1,0:T(8,128)(2,1)S(1)} %broadcast_select_fusion.1), channel_id=2, replica_groups={{0,2},{4,6},{8,10},{12,14},{16,18},{20,22},{24,26},{28,30},{32,34},{36,..., dimensions={0}, use_global_device_ids=true | all-gather | bytes 589824 | tf_op jit(solution)/shard_map/all_gather | solution.py:270
  24.4 0.4 collective-permute-done.far_key_ref.far_ref
  24.9 2.9 %all-gather.1 = bf16[256,768]{1,0:T(8,128)(2,1)S(1)} all-gather(bf16[128,768]{1,0:T(8,128)(2,1)S(1)} %broadcast_select_fusion), channel_id=3, replica_groups={{0,2},{4,6},{8,10},{12,14},{16,18},{20,22},{24,26},{28,30},{32,34},{36,..., dimensions={0}, use_global_device_ids=true | all-gather | bytes 589824 | tf_op jit(solution)/shard_map/all_gather | solution.py:272
  27.8 2.2 %table_part.1 = (f32[256,128]{1,0:T(8,128)S(1)}, bf16[6,128,640]{2,1,0:T(8,128)(2,1)S(1)}, bf16[6,128,384]{2,1,0:T(8,128)(2,1)S(1)}) custom-call(s32[1]{0:T(128)} %bitcast.block_ref, s32[8,128]{1,0:T(8,128)S(1)} %get-tuple-element.33.facts_ref, bf16[128,768]{1,0:T(8,128)(2,1)S(1)} %copy-done.2, bf16[128,768]{1,0:T(8,128)(2,1)S(1)} %copy-done.3, ...), custom_call_target="tpu_custom_call" | custom-call | flops 4000000000 | tf_op jit(solution)/shard_map/table_part/pallas_call | solution.py:38
  30.0 1.4 %block_grads.1 = (bf16[2,128,768]{2,1,0:T(8,128)(2,1)S(1)}, bf16[2,128,768]{2,1,0:T(8,128)(2,1)S(1)}, bf16[128,768]{1,0:T(8,128)(2,1)}, f32[2,128,768]{2,1,0:T(8,128)S(1)}) custom-call(s32[1]{0:T(128)} %bitcast.block_ref, bf16[128,768]{1,0:T(8,128)(2,1)S(1)} %copy-done.2, bf16[128,768]{1,0:T(8,128)(2,1)S(1)} %copy-done.3, bf16[128,768]{1,0:T(8,128)(2,1)S(1)} %copy-done.1, ...), custom_call_target="tpu_custom_call" | custom-call | flops 4000000000 | tf_op jit(solution)/shard_map/block_grads/pallas_call | solution.py:38
  31.4 12.2 %all_to_all.15.pieces_ref = f32[32,8,128]{2,1,0:T(8,128)S(1)} all-to-all(f32[32,8,128]{2,1,0:T(8,128)S(1)} %bitcast.9), channel_id=1, replica_groups={{0,1,2,3,64,65,66,67,128,130,131,192,193,194,195,256,257,258,259,320,32..., dimensions={0} | all-to-all | bytes 262144 | tf_op jit(solution)/shard_map/all_to_all | solution.py:296
  43.5 0.7 plane_sum.1
  44.2 10.6 %all-to-all-start.1 = ((f32[16,8,128]{2,1,0:T(8,128)}), f32[16,8,128]{2,1,0:T(8,128)S(1)}, u32[]{:S(2)}, u32[]{:S(2)}) async-start(f32[16,8,128]{2,1,0:T(8,128)} %plane_sum.1), calls=%async_computation.1 | async-start | bytes 131072 | tf_op jit(solution)/shard_map/all_to_all | solution.py:303
  54.8 2.9 %collective-permute-start.2 = (bf16[2,128,768]{2,1,0:T(8,128)(2,1)S(1)}, bf16[2,128,768]{2,1,0:T(8,128)(2,1)S(1)}, u32[]{:S(2)}, u32[]{:S(2)}) collective-permute-start(bf16[2,128,768]{2,1,0:T(8,128)(2,1)S(1)} %get-tuple-element.46), channel_id=1, source_target_pairs={{0,510},{2,0},{4,2},{6,4},{8,6},{10,8},{12,10},{14,12},{16,14},{18... | collective-permute-start | bytes 1179656 | tf_op jit(solution)/shard_map/ppermute | solution.py:295
  57.7 2.8 %collective-permute-start.3 = (bf16[2,128,768]{2,1,0:T(8,128)(2,1)S(1)}, bf16[2,128,768]{2,1,0:T(8,128)(2,1)S(1)}, u32[]{:S(2)}, u32[]{:S(2)}) collective-permute-start(bf16[2,128,768]{2,1,0:T(8,128)(2,1)S(1)} %get-tuple-element.49), channel_id=1, source_target_pairs={{0,508},{2,510},{4,0},{6,2},{8,4},{10,6},{12,8},{14,10},{16,12},{1... | collective-permute-start | bytes 1179656 | tf_op jit(solution)/shard_map/ppermute | solution.py:302
  60.5 0.0 all-to-all-done.1.pieces_ref
  60.5 0.7 line_sum.1
  61.2 7.3 %all-to-all-start.2 = ((f32[32,8,128]{2,1,0:T(8,128)}), f32[32,8,128]{2,1,0:T(8,128)S(1)}, u32[]{:S(2)}, u32[]{:S(2)}) async-start(f32[32,8,128]{2,1,0:T(8,128)} %line_sum.1), calls=%async_computation.2 | async-start | bytes 262144 | tf_op jit(solution)/shard_map/all_to_all | solution.py:307
  68.6 0.0 collective-permute-done.2.near_ref
  68.6 2.7 %all-to-all-done.2 = f32[32,8,128]{2,1,0:T(8,128)S(1)} async-done(((f32[32,8,128]{2,1,0:T(8,128)}), f32[32,8,128]{2,1,0:T(8,128)S(1)}, u32[]{:S(2)}, u32[]{:S(2)}) %all-to-all-start.2) | async-done | bytes 131104 | tf_op jit(solution)/shard_map/all_to_all | solution.py:307
  71.2 0.0 collective-permute-done.3.far_ref
  71.2 0.9 %final_sums.1 = (bf16[128,768]{1,0:T(8,128)(2,1)}, bf16[128,768]{1,0:T(8,128)(2,1)}, f32[256,128]{1,0:T(8,128)}) custom-call(f32[2,128,768]{2,1,0:T(8,128)S(1)} %get-tuple-element.42.own_ref, bf16[2,128,768]{2,1,0:T(8,128)(2,1)S(1)} %collective-permute-done.2.near_ref, bf16[2,128,768]{2,1,0:T(8,128)(2,1)S(1)} %collective-permute-done.3.far_ref, ...), custom_call_target="tpu_custom_call" | custom-call | flops 1000000000 | tf_op jit(solution)/shard_map/final_sums/pallas_call | solution.py:38
  (6 shorter events, 0.1 us)
Async XLA Ops:
  0.6 20.0 %collective-permute-start.1 = (bf16[128,768]{1,0:T(8,128)(2,1)}, bf16[128,768]{1,0:T(8,128)(2,1)S(1)}, u32[]{:S(2)}, u32[]{:S(2)}) collective-permute-start(bf16[128,768]{1,0:T(8,128)(2,1)} %value_ref.1), channel_id=1, source_target_pairs={{0,4},{2,6},{4,8},{6,10},{8,12},{10,14},{12,16},{14,18},{16,20},{1... | collective-permute-start | bytes 589832 | tf_op jit(solution)/shard_map/ppermute | solution.py:254
  5.0 19.8 %collective-permute-start = (bf16[128,768]{1,0:T(8,128)(2,1)}, bf16[128,768]{1,0:T(8,128)(2,1)S(1)}, u32[]{:S(2)}, u32[]{:S(2)}) collective-permute-start(bf16[128,768]{1,0:T(8,128)(2,1)} %key_ref.3), channel_id=1, source_target_pairs={{0,4},{2,6},{4,8},{6,10},{8,12},{10,14},{12,16},{14,18},{16,20},{1... | collective-permute-start | bytes 589832 | tf_op jit(solution)/shard_map/ppermute | solution.py:255
  8.6 0.9 %copy-start = (bf16[128,768]{1,0:T(8,128)(2,1)S(1)}, bf16[128,768]{1,0:T(8,128)(2,1)}, u32[]{:S(2)}) copy-start(bf16[128,768]{1,0:T(8,128)(2,1)} %value_ref.1) | copy-start | bytes 589828
  8.6 1.0 %copy-start.1 = (bf16[128,768]{1,0:T(8,128)(2,1)S(1)}, bf16[128,768]{1,0:T(8,128)(2,1)}, u32[]{:S(2)}) copy-start(bf16[128,768]{1,0:T(8,128)(2,1)} %key_ref.3) | copy-start | bytes 589828
  8.6 1.1 %copy-start.2 = (bf16[128,768]{1,0:T(8,128)(2,1)S(1)}, bf16[128,768]{1,0:T(8,128)(2,1)}, u32[]{:S(2)}) copy-start(bf16[128,768]{1,0:T(8,128)(2,1)} %query_ref.5) | copy-start | bytes 589828
  8.6 1.2 %copy-start.3 = (bf16[128,768]{1,0:T(8,128)(2,1)S(1)}, bf16[128,768]{1,0:T(8,128)(2,1)}, u32[]{:S(2)}) copy-start(bf16[128,768]{1,0:T(8,128)(2,1)} %grad_ref.5) | copy-start | bytes 589828
  8.6 1.2 %copy-start.4 = (bf16[256,128]{1,0:T(8,128)(2,1)S(1)}, bf16[256,128]{1,0:T(8,128)(2,1)}, u32[]{:S(2)}) copy-start(bf16[256,128]{1,0:T(8,128)(2,1)} %table_ref.1) | copy-start | bytes 196612
  8.7 1.1 %copy-start.5 = (s32[1,3]{1,0:T(1,128)S(1)}, s32[1,3]{1,0:T(1,128)}, u32[]{:S(2)}) copy-start(s32[1,3]{1,0:T(1,128)} %mask_ref.1) | copy-start | bytes 40
  8.7 1.1 %copy-start.6 = (s32[1,3]{1,0:T(1,128)S(1)}, s32[1,3]{1,0:T(1,128)}, u32[]{:S(2)}) copy-start(s32[1,3]{1,0:T(1,128)} %shift_ref.1) | copy-start | bytes 40
  44.2 16.3 %all-to-all-start.1 = ((f32[16,8,128]{2,1,0:T(8,128)}), f32[16,8,128]{2,1,0:T(8,128)S(1)}, u32[]{:S(2)}, u32[]{:S(2)}) async-start(f32[16,8,128]{2,1,0:T(8,128)} %plane_sum.1), calls=%async_computation.1 | async-start | bytes 131072 | tf_op jit(solution)/shard_map/all_to_all | solution.py:303
  54.8 13.8 %collective-permute-start.2 = (bf16[2,128,768]{2,1,0:T(8,128)(2,1)S(1)}, bf16[2,128,768]{2,1,0:T(8,128)(2,1)S(1)}, u32[]{:S(2)}, u32[]{:S(2)}) collective-permute-start(bf16[2,128,768]{2,1,0:T(8,128)(2,1)S(1)} %get-tuple-element.46), channel_id=1, source_target_pairs={{0,510},{2,0},{4,2},{6,4},{8,6},{10,8},{12,10},{14,12},{16,14},{18... | collective-permute-start | bytes 1179656 | tf_op jit(solution)/shard_map/ppermute | solution.py:295
  57.7 13.6 %collective-permute-start.3 = (bf16[2,128,768]{2,1,0:T(8,128)(2,1)S(1)}, bf16[2,128,768]{2,1,0:T(8,128)(2,1)S(1)}, u32[]{:S(2)}, u32[]{:S(2)}) collective-permute-start(bf16[2,128,768]{2,1,0:T(8,128)(2,1)S(1)} %get-tuple-element.49), channel_id=1, source_target_pairs={{0,508},{2,510},{4,0},{6,2},{8,4},{10,6},{12,8},{14,10},{16,12},{1... | collective-permute-start | bytes 1179656 | tf_op jit(solution)/shard_map/ppermute | solution.py:302
  61.2 10.0 %all-to-all-start.2 = ((f32[32,8,128]{2,1,0:T(8,128)}), f32[32,8,128]{2,1,0:T(8,128)S(1)}, u32[]{:S(2)}, u32[]{:S(2)}) async-start(f32[32,8,128]{2,1,0:T(8,128)} %line_sum.1), calls=%async_computation.2 | async-start | bytes 262144 | tf_op jit(solution)/shard_map/all_to_all | solution.py:307

commit v5 on v4

--- a/solution.py
+++ b/solution.py
@@ -57,7 +57,7 @@
 
 def own_kernel(
     block_ref, mask_ref, shift_ref, query_ref, grad_ref, key_ref, value_ref, table_ref, flip_ref,
-    score_out, moved_out, dprob_out, turned_out, facts_out, table_out
+    score_out, moved_out, dprob_out, turned_out, facts_out, table_out, key_out, value_out
 ):
     width, span = query_ref.shape
     rows = table_ref.shape[0]
@@ -78,6 +78,8 @@
     place = [item & (width - 1) for item in place]
     table = dot(flip_ref[...], table_ref[...]).astype(jnp.bfloat16)
     table_out[...] = table
+    key_out[...] = key_ref[...]
+    value_out[...] = value_ref[...]
     for part in head_parts(span):
         query = query_ref[:, part]
         turned_out[part, :] = query.T
@@ -93,12 +95,47 @@
                 moved_out[step - 1, :, part] = moved + biases[step]
 
 
-def table_kernel(
-    block_ref, facts_ref, query_ref, grad_ref, near_key_ref, near_value_ref, far_key_ref, far_value_ref,
-    score_ref, moved_ref, dprob_ref, turned_ref, table_out, terms_out, weight_out
+def prob_kernel(block_ref, query_ref, near_ref, far_ref, score_ref, moved_ref, prob_out):
+    width, span = query_ref.shape
+    parts = head_parts(span)
+    group = 3 if len(parts) % 3 == 0 else 1
+    other = 1 - lax.rem(block_ref[0], 2)
+    for start in range(0, len(parts), group):
+        mine = parts[start : start + group]
+
+        def heads(load):
+            return jnp.concatenate([load(part) for part in mine], axis=0)
+
+        content = heads(
+            lambda part: dot(
+                query_ref[:, part],
+                jnp.concatenate([near_ref[other, :, part], far_ref[:, part]], axis=0),
+                NT,
+            )
+        ) * SCALE
+        scores = [heads(lambda part: score_ref[:, part])]
+        for step in range(1, STEPS):
+            at = slice((step - 1) * width, step * width)
+            scores.append(content[:, at] + heads(lambda part: moved_ref[step - 1, :, part]))
+        top = jnp.maximum(jnp.maximum(scores[0], scores[1]), scores[2])
+        top = jnp.max(top, axis=1, keepdims=True)
+        exps = [jnp.exp(score - top) for score in scores]
+        total = jnp.sum(exps[0] + exps[1] + exps[2], axis=1, keepdims=True)
+        inverse = 1.0 / total
+        for step in range(STEPS):
+            prob = exps[step] * inverse
+            for at, part in enumerate(mine):
+                prob_out[step, :, part] = prob[at * width : (at + 1) * width]
+
+
+def grads_kernel(
+    block_ref, facts_ref, query_ref, grad_ref, key_ref, near_key_ref, near_value_ref, far_key_ref,
+    far_value_ref, prob_ref, dprob_ref, turned_ref, table_ref,
+    table_out, near_out, far_out, query_out, own_out
 ):
     width, span = query_ref.shape
     rows = table_out.shape[0]
+    table = table_ref[...]
     parts = head_parts(span)
     group = 3 if len(parts) % 3 == 0 else 1
     other = 1 - lax.rem(block_ref[0], 2)
@@ -119,6 +156,7 @@
     def many(item):
         return jnp.concatenate([item] * group, axis=0)
 
+    done = []
     for start in range(0, len(parts), group):
         mine = parts[start : start + group]
 
@@ -134,23 +172,19 @@
                 )
             ) * SCALE
 
-        content = products(query_ref, near_key_ref, far_key_ref)
         dprob = products(grad_ref, near_value_ref, far_value_ref)
-        scores = [heads(lambda part: score_ref[:, part])]
+        done.append((start, mine, dprob))
+    for start, mine, dprob in done:
+
+        def heads(load):
+            return jnp.concatenate([load(part) for part in mine], axis=0)
+
+        probs = [heads(lambda part: prob_ref[step, :, part]) for step in range(STEPS)]
         dprobs = [heads(lambda part: dprob_ref[:, part])]
         for step in range(1, STEPS):
-            at = slice((step - 1) * width, step * width)
-            scores.append(content[:, at] + heads(lambda part: moved_ref[step - 1, :, part]))
-            dprobs.append(dprob[:, at])
-        top = jnp.maximum(jnp.maximum(scores[0], scores[1]), scores[2])
-        top = jnp.max(top, axis=1, keepdims=True)
-        exps = [jnp.exp(score - top) for score in scores]
-        total = jnp.sum(exps[0] + exps[1] + exps[2], axis=1, keepdims=True)
-        mixed = exps[0] * dprobs[0] + exps[1] * dprobs[1] + exps[2] * dprobs[2]
-        mixed = jnp.sum(mixed, axis=1, keepdims=True)
-        inverse = 1.0 / total
-        delta = mixed * inverse
-        probs = [item * inverse for item in exps]
+            dprobs.append(dprob[:, (step - 1) * width : step * width])
+        mixed = probs[0] * dprobs[0] + probs[1] * dprobs[1] + probs[2] * dprobs[2]
+        delta = jnp.sum(mixed, axis=1, keepdims=True)
         dscores = [p * (d - delta) for p, d in zip(probs, dprobs)]
         rounded = [item.astype(jnp.bfloat16) for item in dscores]
         moved = [lanes(item, many(at)) for item, at in zip(dscores, source)]
@@ -166,33 +200,19 @@
         for at, part in enumerate(mine):
             here = slice(at * width, (at + 1) * width)
             table_sum = table_sum + dot(turned_ref[part, :], relative[here])
-            for step in range(STEPS):
-                to = slice(step * width, (step + 1) * width)
-                terms_out[start + at, :, to] = rounded[step][here]
-                weight_out[start + at, :, to] = probs[step][here].astype(jnp.bfloat16)
-            terms_out[start + at, :, STEPS * width :] = relative[here]
+        for at, part in enumerate(mine):
+            here = slice(at * width, (at + 1) * width)
+            terms = jnp.concatenate([item[here] for item in rounded] + [relative[here]], axis=1)
+            weight = jnp.concatenate([item[here].astype(jnp.bfloat16) for item in probs], axis=1)
+            keys = [key_ref[:, part], near_key_ref[other, :, part], far_key_ref[:, part], table]
+            query_out[:, part] = dot(terms, jnp.concatenate(keys, axis=0)).astype(query_out.dtype)
+            by_key = dot(terms[:, : STEPS * width], query_ref[:, part], TN)
+            by_value = dot(weight, grad_ref[:, part], TN)
+            for slot, item in enumerate((by_key, by_value)):
+                own_out[slot, :, part] = item[:width]
+                near_out[slot, :, part] = item[width : 2 * width].astype(jnp.bfloat16)
+                far_out[slot, :, part] = item[2 * width :].astype(jnp.bfloat16)
     table_out[...] = table_sum.T
-
-
-def grads_kernel(
-    block_ref, query_ref, grad_ref, key_ref, near_ref, far_ref, table_ref, terms_ref, weight_ref,
-    near_out, far_out, query_out, own_out
-):
-    width, span = query_ref.shape
-    other = 1 - lax.rem(block_ref[0], 2)
-    table = table_ref[...]
-    for index, part in enumerate(head_parts(span)):
-        query = query_ref[:, part]
-        grad = grad_ref[:, part]
-        terms = terms_ref[index]
-        keys = [key_ref[:, part], near_ref[other, :, part], far_ref[:, part], table]
-        query_out[:, part] = dot(terms, jnp.concatenate(keys, axis=0)).astype(query_out.dtype)
-        by_key = dot(terms[:, : STEPS * width], query, TN)
-        by_value = dot(weight_ref[index], grad, TN)
-        for slot, item in enumerate((by_key, by_value)):
-            own_out[slot, :, part] = item[:width]
-            near_out[slot, :, part] = item[width : 2 * width].astype(jnp.bfloat16)
-            far_out[slot, :, part] = item[2 * width :].astype(jnp.bfloat16)
 
 
 def spread_kernel(flipped, pieces_ref, copies_out):
@@ -254,11 +274,11 @@
     far_value = lax.ppermute(value_states, "ctx", ahead)
     far_key = lax.ppermute(key_states, "ctx", ahead)
     (flip,) = call(flip_kernel, (((rows, rows), bf),), (), [], [], 10, "flip")
-    score, moved, dprob, turned, facts, table = call(
+    score, moved, dprob, turned, facts, table, key_states, value_states = call(
         own_kernel,
         (
             (one, f32), (two, f32), (one, f32), ((span, width), bf), ((8, width), jnp.int32),
-            (rel_table.shape, bf),
+            (rel_table.shape, bf), (one, bf), (one, bf),
         ),
         (
             block, block_mask, distance_shift, queries, out_grad, key_states, value_states,
@@ -266,27 +286,24 @@
         ),
         scalar * 3 + local * 6, [], 3, "own_scores",
     )
-    far_value, score = lax.optimization_barrier((far_value, score))
+    far_key, score = lax.optimization_barrier((far_key, score))
+    near_key = lax.all_gather(jnp.where(odd, far_key, key_states), "ctx", axis_index_groups=pairs)
+    (prob,) = call(
+        prob_kernel,
+        ((three, f32),),
+        (block, queries, near_key, far_key, score, moved),
+        scalar + local * 5, [], 1, "probabilities",
+    )
+    far_value, prob = lax.optimization_barrier((far_value, prob))
     near_value = lax.all_gather(jnp.where(odd, far_value, value_states), "ctx", axis_index_groups=pairs)
-    far_key, near_value = lax.optimization_barrier((far_key, near_value))
-    near_key = lax.all_gather(jnp.where(odd, far_key, key_states), "ctx", axis_index_groups=pairs)
-    table_part, terms, weight = call(
-        table_kernel,
+    table_part, near_part, far_part, query_grad, own = call(
+        grads_kernel,
+        (((rows, HEAD_DIM), f32), (two, bf), (two, bf), (one, bf), (two, f32)),
         (
-            ((rows, HEAD_DIM), f32), ((heads, width, STEPS * width + rows), bf),
-            ((heads, width, STEPS * width), bf),
-        ),
-        (
-            block, facts, queries, out_grad, near_key, near_value, far_key, far_value,
-            score, moved, dprob, turned,
-        ),
-        scalar + local * 11, [], 4, "table_part",
-    )
-    near_part, far_part, query_grad, own = call(
-        grads_kernel,
-        ((two, bf), (two, bf), (one, bf), (two, f32)),
-        (block, queries, out_grad, key_states, near_key, far_key, table, terms, weight),
-        scalar + local * 8, [], 4, "block_grads",
+            block, facts, queries, out_grad, key_states, near_key, near_value, far_key, far_value,
+            prob, dprob, turned, table,
+        ),
+        scalar + local * 12, [], 6, "block_grads",
     )
     planes, lines = rings(count, lax.axis_size("head"))
     small = rows // len(planes[0])

time: 72.5 us -> 71.6 us (0.988)
    ppermute x1, waiting for transfers between devices: 8.62 us -> 0.01 us  [shards(): far_value = lax.ppermute(value_states, 'ctx', ahead)]
    ppermute x1, waiting for transfers between devices: 0.41 us -> 8.62 us  [shards(): far_key = lax.ppermute(key_states, 'ctx', ahead)]
    all_gather x1, blocking collectives: 3.77 us -> 2.82 us  [shards(): lax.all_gather(jnp.where(odd, far_value, value_states), 'ctx', axis_index...]
    ppermute x1, starting transfers between devices: 3.55 us -> 4.37 us  [shards(): far_key = lax.ppermute(key_states, 'ctx', ahead)]
    ppermute x1, starting transfers between devices: 4.37 us -> 3.55 us  [shards(): far_value = lax.ppermute(value_states, 'ctx', ahead)]
    all_gather x1, blocking collectives: 2.95 us -> 3.77 us  [shards(): lax.all_gather(jnp.where(odd, far_key, key_states), 'ctx', axis_index_gro...]
  transfers between devices with their start and end apart: 6 -> 6, of which waited for: 3 -> 2; matrix products, arithmetic and copies ran while one was open for 0% -> 0% of each run, Pallas kernels for 4% -> 5%
where the time goes in v5:
time: 71.6 us; the launch traced here: 71.2 us
  starting transfers between devices  31.6 us (44%)
  blocking collectives  18.8 us (26%)
  waiting for transfers between devices  11.3 us (16%)
  Pallas kernels  7.62 us (11%)
  local copies, waits for them, and re-layouts  1.13 us (2%)
  between operations  0.8 us (1%)
    all_to_all x1, blocking collectives, shards(): lax.all_to_all(table_part.reshape(shape), AXES, 0, 0, axis_index_groups=p...  12.2 us
    all_to_all x1, starting transfers between devices, shards(): pieces = lax.all_to_all(copies, AXES, 0, 0, axis_index_groups=lines)  10.6 us
    ppermute x1, waiting for transfers between devices, shards(): far_key = lax.ppermute(key_states, 'ctx', ahead)  8.62 us
    pallas_call x7, Pallas kernels, call(): pl.pallas_call(kernel, out_shape=tuple((jax.ShapeDtypeStruct(shape, kind)...  7.62 us
    all_to_all x1, starting transfers between devices, shards(): lax.all_to_all(copies, AXES, 0, 0, axis_index_groups=[plane[::-1] for pla...  7.34 us
    ppermute x1, starting transfers between devices, shards(): far_key = lax.ppermute(key_states, 'ctx', ahead)  4.37 us
    all_gather x1, blocking collectives, shards(): lax.all_gather(jnp.where(odd, far_key, key_states), 'ctx', axis_index_gro...  3.77 us
    ppermute x1, starting transfers between devices, shards(): far_value = lax.ppermute(value_states, 'ctx', ahead)  3.55 us
  transfers between devices with their start and end apart: 6, of which 2 were waited for; matrix products, arithmetic and copies ran while one was open for 0% of the time, Pallas kernels for 5%

profile of v5, /device:TPU:1, one launch (start us, length us, event | category | flops | bytes accessed | tf_op | source)
XLA Modules:
  0.0 71.2 jit_solution(11799757819657366013)
XLA Ops:
  0.6 4.4 %collective-permute-start = (bf16[128,768]{1,0:T(8,128)(2,1)}, bf16[128,768]{1,0:T(8,128)(2,1)S(1)}, u32[]{:S(2)}, u32[]{:S(2)}) collective-permute-start(bf16[128,768]{1,0:T(8,128)(2,1)} %key_ref.1), channel_id=1, source_target_pairs={{0,4},{2,6},{4,8},{6,10},{8,12},{10,14},{12,16},{14,18},{16,20},{1... | collective-permute-start | bytes 589832 | tf_op jit(solution)/shard_map/ppermute | solution.py:275
  5.0 3.5 %collective-permute-start.1 = (bf16[128,768]{1,0:T(8,128)(2,1)}, bf16[128,768]{1,0:T(8,128)(2,1)S(1)}, u32[]{:S(2)}, u32[]{:S(2)}) collective-permute-start(bf16[128,768]{1,0:T(8,128)(2,1)} %value_ref.1), channel_id=1, source_target_pairs={{0,4},{2,6},{4,8},{6,10},{8,12},{10,14},{12,16},{14,18},{16,20},{1... | collective-permute-start | bytes 589832 | tf_op jit(solution)/shard_map/ppermute | solution.py:274
  8.6 0.0 copy-start
  8.6 0.0 copy-start.1
  8.6 0.0 copy-start.2
  8.6 0.0 copy-start.3
  8.6 0.0 copy-start.4
  8.6 0.0 copy-start.5
  8.7 0.8 %copy-done = bf16[128,768]{1,0:T(8,128)(2,1)S(1)} copy-done((bf16[128,768]{1,0:T(8,128)(2,1)S(1)}, bf16[128,768]{1,0:T(8,128)(2,1)}, u32[]{:S(2)}) %copy-start) | copy-done | bytes 196632
  9.5 0.1 copy-done.1
  9.6 0.1 copy-done.2
  9.7 0.1 copy-done.3
  9.8 0.0 copy-done.6
  9.8 2.2 %own_scores.1 = (f32[128,768]{1,0:T(8,128)S(1)}, f32[2,128,768]{2,1,0:T(8,128)S(1)}, f32[128,768]{1,0:T(8,128)S(1)}, bf16[768,128]{1,0:T(8,128)(2,1)S(1)}, s32[8...) custom-call(s32[1]{0:T(128)} %bitcast.block_ref, ...), custom_call_target="tpu_custom_call" | custom-call | flops 3000000000 | tf_op jit(solution)/shard_map/own_scores/pallas_call | solution.py:38
  12.0 8.6 %collective-permute-done.far_ref.far_key_ref = bf16[128,768]{1,0:T(8,128)(2,1)S(1)} collective-permute-done((bf16[128,768]{1,0:T(8,128)(2,1)}, bf16[128,768]{1,0:T(8,128)(2,1)S(1)}, u32[]{:S(2)}, u32[]{:S(2)}) %collective-permute-start) | collective-permute-done | bytes 196640 | tf_op jit(solution)/shard_map/ppermute | solution.py:275
  20.6 3.8 %all-gather = bf16[256,768]{1,0:T(8,128)(2,1)S(1)} all-gather(bf16[128,768]{1,0:T(8,128)(2,1)S(1)} %broadcast_select_fusion.1), channel_id=2, replica_groups={{0,2},{4,6},{8,10},{12,14},{16,18},{20,22},{24,26},{28,30},{32,34},{36,..., dimensions={0}, use_global_device_ids=true | all-gather | bytes 589824 | tf_op jit(solution)/shard_map/all_gather | solution.py:290
  24.4 0.5 probabilities.1.prob_ref
  24.9 0.0 collective-permute-done.1.far_value_ref
  25.0 2.8 %all-gather.1 = bf16[256,768]{1,0:T(8,128)(2,1)S(1)} all-gather(bf16[128,768]{1,0:T(8,128)(2,1)S(1)} %broadcast_select_fusion), channel_id=3, replica_groups={{0,2},{4,6},{8,10},{12,14},{16,18},{20,22},{24,26},{28,30},{32,34},{36,..., dimensions={0}, use_global_device_ids=true | all-gather | bytes 589824 | tf_op jit(solution)/shard_map/all_gather | solution.py:298
  27.8 2.7 %block_grads.1 = (f32[256,128]{1,0:T(8,128)S(1)}, bf16[2,128,768]{2,1,0:T(8,128)(2,1)S(1)}, bf16[2,128,768]{2,1,0:T(8,128)(2,1)S(1)}, bf16[128,768]{1,0:T(8,128)(2,1)}, f32[2,128,768]{2,1,0:T(8,128)S(1)}) custom-call(s32[1]{0:T(128)} %bitcast.block_ref, s32[8,128]{1,0:T(8,128)S(1)} %get-tuple-element.29.facts_ref, bf16[128,768]{1,0:T(8,128)(2,1)S(1)} %copy-done.2, ...), custom_call_target="tpu_custom_call" | custom-call | flops 6000000000 | tf_op jit(solution)/shard_map/block_grads/pallas_call | solution.py:38
  30.5 12.2 %all_to_all.15.pieces_ref = f32[32,8,128]{2,1,0:T(8,128)S(1)} all-to-all(f32[32,8,128]{2,1,0:T(8,128)S(1)} %bitcast.9), channel_id=1, replica_groups={{0,1,2,3,64,65,66,67,128,130,131,192,193,194,195,256,257,258,259,320,32..., dimensions={0} | all-to-all | bytes 262144 | tf_op jit(solution)/shard_map/all_to_all | solution.py:313
  42.6 0.7 plane_sum.1
  43.3 10.6 %all-to-all-start.1 = ((f32[16,8,128]{2,1,0:T(8,128)}), f32[16,8,128]{2,1,0:T(8,128)S(1)}, u32[]{:S(2)}, u32[]{:S(2)}) async-start(f32[16,8,128]{2,1,0:T(8,128)} %plane_sum.1), calls=%async_computation.1 | async-start | bytes 131072 | tf_op jit(solution)/shard_map/all_to_all | solution.py:320
  53.9 2.9 %collective-permute-start.2 = (bf16[2,128,768]{2,1,0:T(8,128)(2,1)S(1)}, bf16[2,128,768]{2,1,0:T(8,128)(2,1)S(1)}, u32[]{:S(2)}, u32[]{:S(2)}) collective-permute-start(bf16[2,128,768]{2,1,0:T(8,128)(2,1)S(1)} %get-tuple-element.46), channel_id=1, source_target_pairs={{0,510},{2,0},{4,2},{6,4},{8,6},{10,8},{12,10},{14,12},{16,14},{18... | collective-permute-start | bytes 1179656 | tf_op jit(solution)/shard_map/ppermute | solution.py:312
  56.8 2.8 %collective-permute-start.3 = (bf16[2,128,768]{2,1,0:T(8,128)(2,1)S(1)}, bf16[2,128,768]{2,1,0:T(8,128)(2,1)S(1)}, u32[]{:S(2)}, u32[]{:S(2)}) collective-permute-start(bf16[2,128,768]{2,1,0:T(8,128)(2,1)S(1)} %get-tuple-element.49), channel_id=1, source_target_pairs={{0,508},{2,510},{4,0},{6,2},{8,4},{10,6},{12,8},{14,10},{16,12},{1... | collective-permute-start | bytes 1179656 | tf_op jit(solution)/shard_map/ppermute | solution.py:319
  59.6 0.0 all-to-all-done.1.pieces_ref
  59.6 0.7 line_sum.1
  60.3 7.3 %all-to-all-start.2 = ((f32[32,8,128]{2,1,0:T(8,128)}), f32[32,8,128]{2,1,0:T(8,128)S(1)}, u32[]{:S(2)}, u32[]{:S(2)}) async-start(f32[32,8,128]{2,1,0:T(8,128)} %line_sum.1), calls=%async_computation.2 | async-start | bytes 262144 | tf_op jit(solution)/shard_map/all_to_all | solution.py:324
  67.7 0.0 collective-permute-done.2.near_ref
  67.7 2.7 %all-to-all-done.2 = f32[32,8,128]{2,1,0:T(8,128)S(1)} async-done(((f32[32,8,128]{2,1,0:T(8,128)}), f32[32,8,128]{2,1,0:T(8,128)S(1)}, u32[]{:S(2)}, u32[]{:S(2)}) %all-to-all-start.2) | async-done | bytes 131104 | tf_op jit(solution)/shard_map/all_to_all | solution.py:324
  70.3 0.0 collective-permute-done.3.far_ref
  70.4 0.9 %final_sums.1 = (bf16[128,768]{1,0:T(8,128)(2,1)}, bf16[128,768]{1,0:T(8,128)(2,1)}, f32[256,128]{1,0:T(8,128)}) custom-call(f32[2,128,768]{2,1,0:T(8,128)S(1)} %get-tuple-element.42.own_ref, bf16[2,128,768]{2,1,0:T(8,128)(2,1)S(1)} %collective-permute-done.2.near_ref, bf16[2,128,768]{2,1,0:T(8,128)(2,1)S(1)} %collective-permute-done.3.far_ref, ...), custom_call_target="tpu_custom_call" | custom-call | flops 1000000000 | tf_op jit(solution)/shard_map/final_sums/pallas_call | solution.py:38
  (6 shorter events, 0.1 us)
Async XLA Ops:
  0.6 20.0 %collective-permute-start = (bf16[128,768]{1,0:T(8,128)(2,1)}, bf16[128,768]{1,0:T(8,128)(2,1)S(1)}, u32[]{:S(2)}, u32[]{:S(2)}) collective-permute-start(bf16[128,768]{1,0:T(8,128)(2,1)} %key_ref.1), channel_id=1, source_target_pairs={{0,4},{2,6},{4,8},{6,10},{8,12},{10,14},{12,16},{14,18},{16,20},{1... | collective-permute-start | bytes 589832 | tf_op jit(solution)/shard_map/ppermute | solution.py:275
  5.0 19.9 %collective-permute-start.1 = (bf16[128,768]{1,0:T(8,128)(2,1)}, bf16[128,768]{1,0:T(8,128)(2,1)S(1)}, u32[]{:S(2)}, u32[]{:S(2)}) collective-permute-start(bf16[128,768]{1,0:T(8,128)(2,1)} %value_ref.1), channel_id=1, source_target_pairs={{0,4},{2,6},{4,8},{6,10},{8,12},{10,14},{12,16},{14,18},{16,20},{1... | collective-permute-start | bytes 589832 | tf_op jit(solution)/shard_map/ppermute | solution.py:274
  8.6 0.9 %copy-start = (bf16[128,768]{1,0:T(8,128)(2,1)S(1)}, bf16[128,768]{1,0:T(8,128)(2,1)}, u32[]{:S(2)}) copy-start(bf16[128,768]{1,0:T(8,128)(2,1)} %key_ref.1) | copy-start | bytes 589828
  8.6 1.0 %copy-start.1 = (bf16[128,768]{1,0:T(8,128)(2,1)S(1)}, bf16[128,768]{1,0:T(8,128)(2,1)}, u32[]{:S(2)}) copy-start(bf16[128,768]{1,0:T(8,128)(2,1)} %value_ref.1) | copy-start | bytes 589828
  8.6 1.1 %copy-start.2 = (bf16[128,768]{1,0:T(8,128)(2,1)S(1)}, bf16[128,768]{1,0:T(8,128)(2,1)}, u32[]{:S(2)}) copy-start(bf16[128,768]{1,0:T(8,128)(2,1)} %query_ref.5) | copy-start | bytes 589828
  8.6 1.2 %copy-start.3 = (bf16[128,768]{1,0:T(8,128)(2,1)S(1)}, bf16[128,768]{1,0:T(8,128)(2,1)}, u32[]{:S(2)}) copy-start(bf16[128,768]{1,0:T(8,128)(2,1)} %grad_ref.3) | copy-start | bytes 589828
  8.6 1.2 %copy-start.4 = (bf16[256,128]{1,0:T(8,128)(2,1)S(1)}, bf16[256,128]{1,0:T(8,128)(2,1)}, u32[]{:S(2)}) copy-start(bf16[256,128]{1,0:T(8,128)(2,1)} %table_ref.1) | copy-start | bytes 196612
  8.6 1.2 %copy-start.5 = (s32[1,3]{1,0:T(1,128)S(1)}, s32[1,3]{1,0:T(1,128)}, u32[]{:S(2)}) copy-start(s32[1,3]{1,0:T(1,128)} %mask_ref.1) | copy-start | bytes 40
  8.6 1.2 %copy-start.6 = (s32[1,3]{1,0:T(1,128)S(1)}, s32[1,3]{1,0:T(1,128)}, u32[]{:S(2)}) copy-start(s32[1,3]{1,0:T(1,128)} %shift_ref.1) | copy-start | bytes 40
  43.3 16.3 %all-to-all-start.1 = ((f32[16,8,128]{2,1,0:T(8,128)}), f32[16,8,128]{2,1,0:T(8,128)S(1)}, u32[]{:S(2)}, u32[]{:S(2)}) async-start(f32[16,8,128]{2,1,0:T(8,128)} %plane_sum.1), calls=%async_computation.1 | async-start | bytes 131072 | tf_op jit(solution)/shard_map/all_to_all | solution.py:320
  53.9 13.8 %collective-permute-start.2 = (bf16[2,128,768]{2,1,0:T(8,128)(2,1)S(1)}, bf16[2,128,768]{2,1,0:T(8,128)(2,1)S(1)}, u32[]{:S(2)}, u32[]{:S(2)}) collective-permute-start(bf16[2,128,768]{2,1,0:T(8,128)(2,1)S(1)} %get-tuple-element.46), channel_id=1, source_target_pairs={{0,510},{2,0},{4,2},{6,4},{8,6},{10,8},{12,10},{14,12},{16,14},{18... | collective-permute-start | bytes 1179656 | tf_op jit(solution)/shard_map/ppermute | solution.py:312
  56.8 13.6 %collective-permute-start.3 = (bf16[2,128,768]{2,1,0:T(8,128)(2,1)S(1)}, bf16[2,128,768]{2,1,0:T(8,128)(2,1)S(1)}, u32[]{:S(2)}, u32[]{:S(2)}) collective-permute-start(bf16[2,128,768]{2,1,0:T(8,128)(2,1)S(1)} %get-tuple-element.49), channel_id=1, source_target_pairs={{0,508},{2,510},{4,0},{6,2},{8,4},{10,6},{12,8},{14,10},{16,12},{1... | collective-permute-start | bytes 1179656 | tf_op jit(solution)/shard_map/ppermute | solution.py:319
  60.3 10.0 %all-to-all-start.2 = ((f32[32,8,128]{2,1,0:T(8,128)}), f32[32,8,128]{2,1,0:T(8,128)S(1)}, u32[]{:S(2)}, u32[]{:S(2)}) async-start(f32[32,8,128]{2,1,0:T(8,128)} %line_sum.1), calls=%async_computation.2 | async-start | bytes 262144 | tf_op jit(solution)/shard_map/all_to_all | solution.py:324

commit v6 on v5

--- a/solution.py
+++ b/solution.py
@@ -236,7 +236,7 @@
 def rings(count, head):
     depth = 16
     columns = count // (2 * depth)
-    lead = 9
+    lead = 11
     planes = []
     for z in range(depth):
         plane = [

time: 71.6 us -> 71.4 us (level)
    all_to_all x1, starting transfers between devices: 10.6 us -> 8.77 us  [shards(): pieces = lax.all_to_all(copies, AXES, 0, 0, axis_index_groups=lines)]
    all_to_all x1, starting transfers between devices: 7.34 us -> 8.66 us  [shards(): lax.all_to_all(copies, AXES, 0, 0, axis_index_groups=[plane[::-1] for pla...]
  transfers between devices with their start and end apart: 6 -> 6, of which waited for: 2 -> 3; matrix products, arithmetic and copies ran while one was open for 0% -> 0% of each run, Pallas kernels for 5% -> 5%
where the time goes in v6:
time: 71.4 us; the launch traced here: 71 us
  starting transfers between devices  31.1 us (44%)
  blocking collectives  18.8 us (26%)
  waiting for transfers between devices  11.6 us (16%)
  Pallas kernels  7.62 us (11%)
  local copies, waits for them, and re-layouts  1.13 us (2%)
  between operations  0.79 us (1%)
    all_to_all x1, blocking collectives, shards(): lax.all_to_all(table_part.reshape(shape), AXES, 0, 0, axis_index_groups=p...  12.2 us
    all_to_all x1, starting transfers between devices, shards(): pieces = lax.all_to_all(copies, AXES, 0, 0, axis_index_groups=lines)  8.77 us
    all_to_all x1, starting transfers between devices, shards(): lax.all_to_all(copies, AXES, 0, 0, axis_index_groups=[plane[::-1] for pla...  8.66 us
    ppermute x1, waiting for transfers between devices, shards(): far_key = lax.ppermute(key_states, 'ctx', ahead)  8.62 us
    pallas_call x7, Pallas kernels, call(): pl.pallas_call(kernel, out_shape=tuple((jax.ShapeDtypeStruct(shape, kind)...  7.62 us
    ppermute x1, starting transfers between devices, shards(): far_key = lax.ppermute(key_states, 'ctx', ahead)  4.37 us
    all_gather x1, blocking collectives, shards(): lax.all_gather(jnp.where(odd, far_key, key_states), 'ctx', axis_index_gro...  3.77 us
    ppermute x1, starting transfers between devices, shards(): far_value = lax.ppermute(value_states, 'ctx', ahead)  3.55 us
  transfers between devices with their start and end apart: 6, of which 3 were waited for; matrix products, arithmetic and copies ran while one was open for 0% of the time, Pallas kernels for 5%

profile of v6, /device:TPU:1, one launch (start us, length us, event | category | flops | bytes accessed | tf_op | source)
XLA Modules:
  0.0 71.0 jit_solution(11483464977510895950)
XLA Ops:
  0.6 4.4 %collective-permute-start = (bf16[128,768]{1,0:T(8,128)(2,1)}, bf16[128,768]{1,0:T(8,128)(2,1)S(1)}, u32[]{:S(2)}, u32[]{:S(2)}) collective-permute-start(bf16[128,768]{1,0:T(8,128)(2,1)} %key_ref.1), channel_id=1, source_target_pairs={{0,4},{2,6},{4,8},{6,10},{8,12},{10,14},{12,16},{14,18},{16,20},{1... | collective-permute-start | bytes 589832 | tf_op jit(solution)/shard_map/ppermute | solution.py:275
  5.0 3.5 %collective-permute-start.1 = (bf16[128,768]{1,0:T(8,128)(2,1)}, bf16[128,768]{1,0:T(8,128)(2,1)S(1)}, u32[]{:S(2)}, u32[]{:S(2)}) collective-permute-start(bf16[128,768]{1,0:T(8,128)(2,1)} %value_ref.1), channel_id=1, source_target_pairs={{0,4},{2,6},{4,8},{6,10},{8,12},{10,14},{12,16},{14,18},{16,20},{1... | collective-permute-start | bytes 589832 | tf_op jit(solution)/shard_map/ppermute | solution.py:274
  8.6 0.0 copy-start
  8.6 0.0 copy-start.1
  8.6 0.0 copy-start.2
  8.6 0.0 copy-start.3
  8.6 0.0 copy-start.4
  8.6 0.0 copy-start.5
  8.7 0.8 %copy-done = bf16[128,768]{1,0:T(8,128)(2,1)S(1)} copy-done((bf16[128,768]{1,0:T(8,128)(2,1)S(1)}, bf16[128,768]{1,0:T(8,128)(2,1)}, u32[]{:S(2)}) %copy-start) | copy-done | bytes 196632
  9.5 0.1 copy-done.1
  9.6 0.1 copy-done.2
  9.7 0.1 copy-done.3
  9.8 0.0 copy-done.6
  9.8 2.2 %own_scores.1 = (f32[128,768]{1,0:T(8,128)S(1)}, f32[2,128,768]{2,1,0:T(8,128)S(1)}, f32[128,768]{1,0:T(8,128)S(1)}, bf16[768,128]{1,0:T(8,128)(2,1)S(1)}, s32[8...) custom-call(s32[1]{0:T(128)} %bitcast.block_ref, ...), custom_call_target="tpu_custom_call" | custom-call | flops 3000000000 | tf_op jit(solution)/shard_map/own_scores/pallas_call | solution.py:38
  12.0 8.6 %collective-permute-done.far_ref.far_key_ref = bf16[128,768]{1,0:T(8,128)(2,1)S(1)} collective-permute-done((bf16[128,768]{1,0:T(8,128)(2,1)}, bf16[128,768]{1,0:T(8,128)(2,1)S(1)}, u32[]{:S(2)}, u32[]{:S(2)}) %collective-permute-start) | collective-permute-done | bytes 196640 | tf_op jit(solution)/shard_map/ppermute | solution.py:275
  20.6 3.8 %all-gather = bf16[256,768]{1,0:T(8,128)(2,1)S(1)} all-gather(bf16[128,768]{1,0:T(8,128)(2,1)S(1)} %broadcast_select_fusion.1), channel_id=2, replica_groups={{0,2},{4,6},{8,10},{12,14},{16,18},{20,22},{24,26},{28,30},{32,34},{36,..., dimensions={0}, use_global_device_ids=true | all-gather | bytes 589824 | tf_op jit(solution)/shard_map/all_gather | solution.py:290
  24.4 0.5 probabilities.1.prob_ref
  24.9 0.0 collective-permute-done.1.far_value_ref
  25.0 2.8 %all-gather.1 = bf16[256,768]{1,0:T(8,128)(2,1)S(1)} all-gather(bf16[128,768]{1,0:T(8,128)(2,1)S(1)} %broadcast_select_fusion), channel_id=3, replica_groups={{0,2},{4,6},{8,10},{12,14},{16,18},{20,22},{24,26},{28,30},{32,34},{36,..., dimensions={0}, use_global_device_ids=true | all-gather | bytes 589824 | tf_op jit(solution)/shard_map/all_gather | solution.py:298
  27.8 2.7 %block_grads.1 = (f32[256,128]{1,0:T(8,128)S(1)}, bf16[2,128,768]{2,1,0:T(8,128)(2,1)S(1)}, bf16[2,128,768]{2,1,0:T(8,128)(2,1)S(1)}, bf16[128,768]{1,0:T(8,128)(2,1)}, f32[2,128,768]{2,1,0:T(8,128)S(1)}) custom-call(s32[1]{0:T(128)} %bitcast.block_ref, s32[8,128]{1,0:T(8,128)S(1)} %get-tuple-element.29.facts_ref, bf16[128,768]{1,0:T(8,128)(2,1)S(1)} %copy-done.2, ...), custom_call_target="tpu_custom_call" | custom-call | flops 6000000000 | tf_op jit(solution)/shard_map/block_grads/pallas_call | solution.py:38
  30.5 12.2 %all_to_all.15.pieces_ref = f32[32,8,128]{2,1,0:T(8,128)S(1)} all-to-all(f32[32,8,128]{2,1,0:T(8,128)S(1)} %bitcast.9), channel_id=1, replica_groups={{0,1,2,3,64,65,66,67,128,130,131,192,193,194,195,256,257,258,259,320,32..., dimensions={0} | all-to-all | bytes 262144 | tf_op jit(solution)/shard_map/all_to_all | solution.py:313
  42.6 0.7 plane_sum.1
  43.3 8.8 %all-to-all-start.1 = ((f32[16,8,128]{2,1,0:T(8,128)}), f32[16,8,128]{2,1,0:T(8,128)S(1)}, u32[]{:S(2)}, u32[]{:S(2)}) async-start(f32[16,8,128]{2,1,0:T(8,128)} %plane_sum.1), calls=%async_computation.1 | async-start | bytes 131072 | tf_op jit(solution)/shard_map/all_to_all | solution.py:320
  52.1 2.9 %collective-permute-start.2 = (bf16[2,128,768]{2,1,0:T(8,128)(2,1)S(1)}, bf16[2,128,768]{2,1,0:T(8,128)(2,1)S(1)}, u32[]{:S(2)}, u32[]{:S(2)}) collective-permute-start(bf16[2,128,768]{2,1,0:T(8,128)(2,1)S(1)} %get-tuple-element.46), channel_id=1, source_target_pairs={{0,510},{2,0},{4,2},{6,4},{8,6},{10,8},{12,10},{14,12},{16,14},{18... | collective-permute-start | bytes 1179656 | tf_op jit(solution)/shard_map/ppermute | solution.py:312
  55.0 2.8 %collective-permute-start.3 = (bf16[2,128,768]{2,1,0:T(8,128)(2,1)S(1)}, bf16[2,128,768]{2,1,0:T(8,128)(2,1)S(1)}, u32[]{:S(2)}, u32[]{:S(2)}) collective-permute-start(bf16[2,128,768]{2,1,0:T(8,128)(2,1)S(1)} %get-tuple-element.49), channel_id=1, source_target_pairs={{0,508},{2,510},{4,0},{6,2},{8,4},{10,6},{12,8},{14,10},{16,12},{1... | collective-permute-start | bytes 1179656 | tf_op jit(solution)/shard_map/ppermute | solution.py:319
  57.8 0.2 all-to-all-done.1.pieces_ref
  58.1 0.7 line_sum.1
  58.8 8.7 %all-to-all-start.2 = ((f32[32,8,128]{2,1,0:T(8,128)}), f32[32,8,128]{2,1,0:T(8,128)S(1)}, u32[]{:S(2)}, u32[]{:S(2)}) async-start(f32[32,8,128]{2,1,0:T(8,128)} %line_sum.1), calls=%async_computation.2 | async-start | bytes 262144 | tf_op jit(solution)/shard_map/all_to_all | solution.py:324
  67.4 0.0 collective-permute-done.2.near_ref
  67.4 2.7 %all-to-all-done.2 = f32[32,8,128]{2,1,0:T(8,128)S(1)} async-done(((f32[32,8,128]{2,1,0:T(8,128)}), f32[32,8,128]{2,1,0:T(8,128)S(1)}, u32[]{:S(2)}, u32[]{:S(2)}) %all-to-all-start.2) | async-done | bytes 131104 | tf_op jit(solution)/shard_map/all_to_all | solution.py:324
  70.1 0.0 collective-permute-done.3.far_ref
  70.1 0.9 %final_sums.1 = (bf16[128,768]{1,0:T(8,128)(2,1)}, bf16[128,768]{1,0:T(8,128)(2,1)}, f32[256,128]{1,0:T(8,128)}) custom-call(f32[2,128,768]{2,1,0:T(8,128)S(1)} %get-tuple-element.42.own_ref, bf16[2,128,768]{2,1,0:T(8,128)(2,1)S(1)} %collective-permute-done.2.near_ref, bf16[2,128,768]{2,1,0:T(8,128)(2,1)S(1)} %collective-permute-done.3.far_ref, ...), custom_call_target="tpu_custom_call" | custom-call | flops 1000000000 | tf_op jit(solution)/shard_map/final_sums/pallas_call | solution.py:38
  (6 shorter events, 0.1 us)
Async XLA Ops:
  0.6 20.0 %collective-permute-start = (bf16[128,768]{1,0:T(8,128)(2,1)}, bf16[128,768]{1,0:T(8,128)(2,1)S(1)}, u32[]{:S(2)}, u32[]{:S(2)}) collective-permute-start(bf16[128,768]{1,0:T(8,128)(2,1)} %key_ref.1), channel_id=1, source_target_pairs={{0,4},{2,6},{4,8},{6,10},{8,12},{10,14},{12,16},{14,18},{16,20},{1... | collective-permute-start | bytes 589832 | tf_op jit(solution)/shard_map/ppermute | solution.py:275
  5.0 19.9 %collective-permute-start.1 = (bf16[128,768]{1,0:T(8,128)(2,1)}, bf16[128,768]{1,0:T(8,128)(2,1)S(1)}, u32[]{:S(2)}, u32[]{:S(2)}) collective-permute-start(bf16[128,768]{1,0:T(8,128)(2,1)} %value_ref.1), channel_id=1, source_target_pairs={{0,4},{2,6},{4,8},{6,10},{8,12},{10,14},{12,16},{14,18},{16,20},{1... | collective-permute-start | bytes 589832 | tf_op jit(solution)/shard_map/ppermute | solution.py:274
  8.6 0.9 %copy-start = (bf16[128,768]{1,0:T(8,128)(2,1)S(1)}, bf16[128,768]{1,0:T(8,128)(2,1)}, u32[]{:S(2)}) copy-start(bf16[128,768]{1,0:T(8,128)(2,1)} %key_ref.1) | copy-start | bytes 589828
  8.6 1.0 %copy-start.1 = (bf16[128,768]{1,0:T(8,128)(2,1)S(1)}, bf16[128,768]{1,0:T(8,128)(2,1)}, u32[]{:S(2)}) copy-start(bf16[128,768]{1,0:T(8,128)(2,1)} %value_ref.1) | copy-start | bytes 589828
  8.6 1.1 %copy-start.2 = (bf16[128,768]{1,0:T(8,128)(2,1)S(1)}, bf16[128,768]{1,0:T(8,128)(2,1)}, u32[]{:S(2)}) copy-start(bf16[128,768]{1,0:T(8,128)(2,1)} %query_ref.5) | copy-start | bytes 589828
  8.6 1.2 %copy-start.3 = (bf16[128,768]{1,0:T(8,128)(2,1)S(1)}, bf16[128,768]{1,0:T(8,128)(2,1)}, u32[]{:S(2)}) copy-start(bf16[128,768]{1,0:T(8,128)(2,1)} %grad_ref.3) | copy-start | bytes 589828
  8.6 1.2 %copy-start.4 = (bf16[256,128]{1,0:T(8,128)(2,1)S(1)}, bf16[256,128]{1,0:T(8,128)(2,1)}, u32[]{:S(2)}) copy-start(bf16[256,128]{1,0:T(8,128)(2,1)} %table_ref.1) | copy-start | bytes 196612
  8.6 1.2 %copy-start.5 = (s32[1,3]{1,0:T(1,128)S(1)}, s32[1,3]{1,0:T(1,128)}, u32[]{:S(2)}) copy-start(s32[1,3]{1,0:T(1,128)} %mask_ref.1) | copy-start | bytes 40
  8.6 1.2 %copy-start.6 = (s32[1,3]{1,0:T(1,128)S(1)}, s32[1,3]{1,0:T(1,128)}, u32[]{:S(2)}) copy-start(s32[1,3]{1,0:T(1,128)} %shift_ref.1) | copy-start | bytes 40
  43.3 14.8 %all-to-all-start.1 = ((f32[16,8,128]{2,1,0:T(8,128)}), f32[16,8,128]{2,1,0:T(8,128)S(1)}, u32[]{:S(2)}, u32[]{:S(2)}) async-start(f32[16,8,128]{2,1,0:T(8,128)} %plane_sum.1), calls=%async_computation.1 | async-start | bytes 131072 | tf_op jit(solution)/shard_map/all_to_all | solution.py:320
  52.1 15.3 %collective-permute-start.2 = (bf16[2,128,768]{2,1,0:T(8,128)(2,1)S(1)}, bf16[2,128,768]{2,1,0:T(8,128)(2,1)S(1)}, u32[]{:S(2)}, u32[]{:S(2)}) collective-permute-start(bf16[2,128,768]{2,1,0:T(8,128)(2,1)S(1)} %get-tuple-element.46), channel_id=1, source_target_pairs={{0,510},{2,0},{4,2},{6,4},{8,6},{10,8},{12,10},{14,12},{16,14},{18... | collective-permute-start | bytes 1179656 | tf_op jit(solution)/shard_map/ppermute | solution.py:312
  55.0 15.1 %collective-permute-start.3 = (bf16[2,128,768]{2,1,0:T(8,128)(2,1)S(1)}, bf16[2,128,768]{2,1,0:T(8,128)(2,1)S(1)}, u32[]{:S(2)}, u32[]{:S(2)}) collective-permute-start(bf16[2,128,768]{2,1,0:T(8,128)(2,1)S(1)} %get-tuple-element.49), channel_id=1, source_target_pairs={{0,508},{2,510},{4,0},{6,2},{8,4},{10,6},{12,8},{14,10},{16,12},{1... | collective-permute-start | bytes 1179656 | tf_op jit(solution)/shard_map/ppermute | solution.py:319
  58.8 11.3 %all-to-all-start.2 = ((f32[32,8,128]{2,1,0:T(8,128)}), f32[32,8,128]{2,1,0:T(8,128)S(1)}, u32[]{:S(2)}, u32[]{:S(2)}) async-start(f32[32,8,128]{2,1,0:T(8,128)} %line_sum.1), calls=%async_computation.2 | async-start | bytes 262144 | tf_op jit(solution)/shard_map/all_to_all | solution.py:324

commit v7 on v6

--- a/solution.py
+++ b/solution.py
@@ -319,7 +319,7 @@
     far_part = lax.ppermute(far_part, "ctx", [(i, (i - 2) % count) for i in range(count)])
     pieces = lax.all_to_all(copies, AXES, 0, 0, axis_index_groups=lines)
     (copies,) = call(
-        functools.partial(spread_kernel, False), ((shape, f32),), (pieces,), local, [], 4, "line_sum",
+        functools.partial(spread_kernel, False), ((shape, f32),), (pieces,), local, [], 12, "line_sum",
     )
     copies = lax.all_to_all(copies, AXES, 0, 0, axis_index_groups=[plane[::-1] for plane in planes])
     key_grad, value_grad, table_grad = call(

time: 71.4 us -> 71.4 us (level)
  no operation moved by 1% of the time
where the time goes in v7:
time: 71.4 us; the launch traced here: 71 us
  starting transfers between devices  31.1 us (44%)
  blocking collectives  18.8 us (26%)
  waiting for transfers between devices  11.6 us (16%)
  Pallas kernels  7.62 us (11%)
  local copies, waits for them, and re-layouts  1.13 us (2%)
  between operations  0.79 us (1%)
    all_to_all x1, blocking collectives, shards(): lax.all_to_all(table_part.reshape(shape), AXES, 0, 0, axis_index_groups=p...  12.2 us
    all_to_all x1, starting transfers between devices, shards(): pieces = lax.all_to_all(copies, AXES, 0, 0, axis_index_groups=lines)  8.77 us
    all_to_all x1, starting transfers between devices, shards(): lax.all_to_all(copies, AXES, 0, 0, axis_index_groups=[plane[::-1] for pla...  8.66 us
    ppermute x1, waiting for transfers between devices, shards(): far_key = lax.ppermute(key_states, 'ctx', ahead)  8.62 us
    pallas_call x7, Pallas kernels, call(): pl.pallas_call(kernel, out_shape=tuple((jax.ShapeDtypeStruct(shape, kind)...  7.62 us
    ppermute x1, starting transfers between devices, shards(): far_key = lax.ppermute(key_states, 'ctx', ahead)  4.37 us
    all_gather x1, blocking collectives, shards(): lax.all_gather(jnp.where(odd, far_key, key_states), 'ctx', axis_index_gro...  3.77 us
    ppermute x1, starting transfers between devices, shards(): far_value = lax.ppermute(value_states, 'ctx', ahead)  3.55 us
  transfers between devices with their start and end apart: 6, of which 3 were waited for; matrix products, arithmetic and copies ran while one was open for 0% of the time, Pallas kernels for 5%

profile of v7, /device:TPU:1, one launch (start us, length us, event | category | flops | bytes accessed | tf_op | source)
XLA Modules:
  0.0 71.0 jit_solution(11483464977510895950)
XLA Ops:
  0.6 4.4 %collective-permute-start = (bf16[128,768]{1,0:T(8,128)(2,1)}, bf16[128,768]{1,0:T(8,128)(2,1)S(1)}, u32[]{:S(2)}, u32[]{:S(2)}) collective-permute-start(bf16[128,768]{1,0:T(8,128)(2,1)} %key_ref.1), channel_id=1, source_target_pairs={{0,4},{2,6},{4,8},{6,10},{8,12},{10,14},{12,16},{14,18},{16,20},{1... | collective-permute-start | bytes 589832 | tf_op jit(solution)/shard_map/ppermute | solution.py:275
  5.0 3.5 %collective-permute-start.1 = (bf16[128,768]{1,0:T(8,128)(2,1)}, bf16[128,768]{1,0:T(8,128)(2,1)S(1)}, u32[]{:S(2)}, u32[]{:S(2)}) collective-permute-start(bf16[128,768]{1,0:T(8,128)(2,1)} %value_ref.1), channel_id=1, source_target_pairs={{0,4},{2,6},{4,8},{6,10},{8,12},{10,14},{12,16},{14,18},{16,20},{1... | collective-permute-start | bytes 589832 | tf_op jit(solution)/shard_map/ppermute | solution.py:274
  8.6 0.0 copy-start
  8.6 0.0 copy-start.1
  8.6 0.0 copy-start.2
  8.6 0.0 copy-start.3
  8.6 0.0 copy-start.4
  8.6 0.0 copy-start.5
  8.7 0.8 %copy-done = bf16[128,768]{1,0:T(8,128)(2,1)S(1)} copy-done((bf16[128,768]{1,0:T(8,128)(2,1)S(1)}, bf16[128,768]{1,0:T(8,128)(2,1)}, u32[]{:S(2)}) %copy-start) | copy-done | bytes 196632
  9.5 0.1 copy-done.1
  9.6 0.1 copy-done.2
  9.7 0.1 copy-done.3
  9.8 0.0 copy-done.6
  9.8 2.2 %own_scores.1 = (f32[128,768]{1,0:T(8,128)S(1)}, f32[2,128,768]{2,1,0:T(8,128)S(1)}, f32[128,768]{1,0:T(8,128)S(1)}, bf16[768,128]{1,0:T(8,128)(2,1)S(1)}, s32[8...) custom-call(s32[1]{0:T(128)} %bitcast.block_ref, ...), custom_call_target="tpu_custom_call" | custom-call | flops 3000000000 | tf_op jit(solution)/shard_map/own_scores/pallas_call | solution.py:38
  12.0 8.6 %collective-permute-done.far_ref.far_key_ref = bf16[128,768]{1,0:T(8,128)(2,1)S(1)} collective-permute-done((bf16[128,768]{1,0:T(8,128)(2,1)}, bf16[128,768]{1,0:T(8,128)(2,1)S(1)}, u32[]{:S(2)}, u32[]{:S(2)}) %collective-permute-start) | collective-permute-done | bytes 196640 | tf_op jit(solution)/shard_map/ppermute | solution.py:275
  20.6 3.8 %all-gather = bf16[256,768]{1,0:T(8,128)(2,1)S(1)} all-gather(bf16[128,768]{1,0:T(8,128)(2,1)S(1)} %broadcast_select_fusion.1), channel_id=2, replica_groups={{0,2},{4,6},{8,10},{12,14},{16,18},{20,22},{24,26},{28,30},{32,34},{36,..., dimensions={0}, use_global_device_ids=true | all-gather | bytes 589824 | tf_op jit(solution)/shard_map/all_gather | solution.py:290
  24.4 0.5 probabilities.1.prob_ref
  24.9 0.0 collective-permute-done.1.far_value_ref
  25.0 2.8 %all-gather.1 = bf16[256,768]{1,0:T(8,128)(2,1)S(1)} all-gather(bf16[128,768]{1,0:T(8,128)(2,1)S(1)} %broadcast_select_fusion), channel_id=3, replica_groups={{0,2},{4,6},{8,10},{12,14},{16,18},{20,22},{24,26},{28,30},{32,34},{36,..., dimensions={0}, use_global_device_ids=true | all-gather | bytes 589824 | tf_op jit(solution)/shard_map/all_gather | solution.py:298
  27.8 2.7 %block_grads.1 = (f32[256,128]{1,0:T(8,128)S(1)}, bf16[2,128,768]{2,1,0:T(8,128)(2,1)S(1)}, bf16[2,128,768]{2,1,0:T(8,128)(2,1)S(1)}, bf16[128,768]{1,0:T(8,128)(2,1)}, f32[2,128,768]{2,1,0:T(8,128)S(1)}) custom-call(s32[1]{0:T(128)} %bitcast.block_ref, s32[8,128]{1,0:T(8,128)S(1)} %get-tuple-element.29.facts_ref, bf16[128,768]{1,0:T(8,128)(2,1)S(1)} %copy-done.2, ...), custom_call_target="tpu_custom_call" | custom-call | flops 6000000000 | tf_op jit(solution)/shard_map/block_grads/pallas_call | solution.py:38
  30.5 12.2 %all_to_all.15.pieces_ref = f32[32,8,128]{2,1,0:T(8,128)S(1)} all-to-all(f32[32,8,128]{2,1,0:T(8,128)S(1)} %bitcast.9), channel_id=1, replica_groups={{0,1,2,3,64,65,66,67,128,130,131,192,193,194,195,256,257,258,259,320,32..., dimensions={0} | all-to-all | bytes 262144 | tf_op jit(solution)/shard_map/all_to_all | solution.py:313
  42.6 0.7 plane_sum.1
  43.3 8.8 %all-to-all-start.1 = ((f32[16,8,128]{2,1,0:T(8,128)}), f32[16,8,128]{2,1,0:T(8,128)S(1)}, u32[]{:S(2)}, u32[]{:S(2)}) async-start(f32[16,8,128]{2,1,0:T(8,128)} %plane_sum.1), calls=%async_computation.1 | async-start | bytes 131072 | tf_op jit(solution)/shard_map/all_to_all | solution.py:320
  52.1 2.9 %collective-permute-start.2 = (bf16[2,128,768]{2,1,0:T(8,128)(2,1)S(1)}, bf16[2,128,768]{2,1,0:T(8,128)(2,1)S(1)}, u32[]{:S(2)}, u32[]{:S(2)}) collective-permute-start(bf16[2,128,768]{2,1,0:T(8,128)(2,1)S(1)} %get-tuple-element.46), channel_id=1, source_target_pairs={{0,510},{2,0},{4,2},{6,4},{8,6},{10,8},{12,10},{14,12},{16,14},{18... | collective-permute-start | bytes 1179656 | tf_op jit(solution)/shard_map/ppermute | solution.py:312
  55.0 2.8 %collective-permute-start.3 = (bf16[2,128,768]{2,1,0:T(8,128)(2,1)S(1)}, bf16[2,128,768]{2,1,0:T(8,128)(2,1)S(1)}, u32[]{:S(2)}, u32[]{:S(2)}) collective-permute-start(bf16[2,128,768]{2,1,0:T(8,128)(2,1)S(1)} %get-tuple-element.49), channel_id=1, source_target_pairs={{0,508},{2,510},{4,0},{6,2},{8,4},{10,6},{12,8},{14,10},{16,12},{1... | collective-permute-start | bytes 1179656 | tf_op jit(solution)/shard_map/ppermute | solution.py:319
  57.8 0.2 all-to-all-done.1.pieces_ref
  58.1 0.7 line_sum.1
  58.8 8.7 %all-to-all-start.2 = ((f32[32,8,128]{2,1,0:T(8,128)}), f32[32,8,128]{2,1,0:T(8,128)S(1)}, u32[]{:S(2)}, u32[]{:S(2)}) async-start(f32[32,8,128]{2,1,0:T(8,128)} %line_sum.1), calls=%async_computation.2 | async-start | bytes 262144 | tf_op jit(solution)/shard_map/all_to_all | solution.py:324
  67.4 0.0 collective-permute-done.2.near_ref
  67.4 2.7 %all-to-all-done.2 = f32[32,8,128]{2,1,0:T(8,128)S(1)} async-done(((f32[32,8,128]{2,1,0:T(8,128)}), f32[32,8,128]{2,1,0:T(8,128)S(1)}, u32[]{:S(2)}, u32[]{:S(2)}) %all-to-all-start.2) | async-done | bytes 131104 | tf_op jit(solution)/shard_map/all_to_all | solution.py:324
  70.1 0.0 collective-permute-done.3.far_ref
  70.1 0.9 %final_sums.1 = (bf16[128,768]{1,0:T(8,128)(2,1)}, bf16[128,768]{1,0:T(8,128)(2,1)}, f32[256,128]{1,0:T(8,128)}) custom-call(f32[2,128,768]{2,1,0:T(8,128)S(1)} %get-tuple-element.42.own_ref, bf16[2,128,768]{2,1,0:T(8,128)(2,1)S(1)} %collective-permute-done.2.near_ref, bf16[2,128,768]{2,1,0:T(8,128)(2,1)S(1)} %collective-permute-done.3.far_ref, ...), custom_call_target="tpu_custom_call" | custom-call | flops 1000000000 | tf_op jit(solution)/shard_map/final_sums/pallas_call | solution.py:38
  (6 shorter events, 0.1 us)
Async XLA Ops:
  0.6 20.0 %collective-permute-start = (bf16[128,768]{1,0:T(8,128)(2,1)}, bf16[128,768]{1,0:T(8,128)(2,1)S(1)}, u32[]{:S(2)}, u32[]{:S(2)}) collective-permute-start(bf16[128,768]{1,0:T(8,128)(2,1)} %key_ref.1), channel_id=1, source_target_pairs={{0,4},{2,6},{4,8},{6,10},{8,12},{10,14},{12,16},{14,18},{16,20},{1... | collective-permute-start | bytes 589832 | tf_op jit(solution)/shard_map/ppermute | solution.py:275
  5.0 19.9 %collective-permute-start.1 = (bf16[128,768]{1,0:T(8,128)(2,1)}, bf16[128,768]{1,0:T(8,128)(2,1)S(1)}, u32[]{:S(2)}, u32[]{:S(2)}) collective-permute-start(bf16[128,768]{1,0:T(8,128)(2,1)} %value_ref.1), channel_id=1, source_target_pairs={{0,4},{2,6},{4,8},{6,10},{8,12},{10,14},{12,16},{14,18},{16,20},{1... | collective-permute-start | bytes 589832 | tf_op jit(solution)/shard_map/ppermute | solution.py:274
  8.6 0.9 %copy-start = (bf16[128,768]{1,0:T(8,128)(2,1)S(1)}, bf16[128,768]{1,0:T(8,128)(2,1)}, u32[]{:S(2)}) copy-start(bf16[128,768]{1,0:T(8,128)(2,1)} %key_ref.1) | copy-start | bytes 589828
  8.6 1.0 %copy-start.1 = (bf16[128,768]{1,0:T(8,128)(2,1)S(1)}, bf16[128,768]{1,0:T(8,128)(2,1)}, u32[]{:S(2)}) copy-start(bf16[128,768]{1,0:T(8,128)(2,1)} %value_ref.1) | copy-start | bytes 589828
  8.6 1.1 %copy-start.2 = (bf16[128,768]{1,0:T(8,128)(2,1)S(1)}, bf16[128,768]{1,0:T(8,128)(2,1)}, u32[]{:S(2)}) copy-start(bf16[128,768]{1,0:T(8,128)(2,1)} %query_ref.5) | copy-start | bytes 589828
  8.6 1.2 %copy-start.3 = (bf16[128,768]{1,0:T(8,128)(2,1)S(1)}, bf16[128,768]{1,0:T(8,128)(2,1)}, u32[]{:S(2)}) copy-start(bf16[128,768]{1,0:T(8,128)(2,1)} %grad_ref.3) | copy-start | bytes 589828
  8.6 1.2 %copy-start.4 = (bf16[256,128]{1,0:T(8,128)(2,1)S(1)}, bf16[256,128]{1,0:T(8,128)(2,1)}, u32[]{:S(2)}) copy-start(bf16[256,128]{1,0:T(8,128)(2,1)} %table_ref.1) | copy-start | bytes 196612
  8.6 1.2 %copy-start.5 = (s32[1,3]{1,0:T(1,128)S(1)}, s32[1,3]{1,0:T(1,128)}, u32[]{:S(2)}) copy-start(s32[1,3]{1,0:T(1,128)} %mask_ref.1) | copy-start | bytes 40
  8.6 1.2 %copy-start.6 = (s32[1,3]{1,0:T(1,128)S(1)}, s32[1,3]{1,0:T(1,128)}, u32[]{:S(2)}) copy-start(s32[1,3]{1,0:T(1,128)} %shift_ref.1) | copy-start | bytes 40
  43.3 14.8 %all-to-all-start.1 = ((f32[16,8,128]{2,1,0:T(8,128)}), f32[16,8,128]{2,1,0:T(8,128)S(1)}, u32[]{:S(2)}, u32[]{:S(2)}) async-start(f32[16,8,128]{2,1,0:T(8,128)} %plane_sum.1), calls=%async_computation.1 | async-start | bytes 131072 | tf_op jit(solution)/shard_map/all_to_all | solution.py:320
  52.1 15.3 %collective-permute-start.2 = (bf16[2,128,768]{2,1,0:T(8,128)(2,1)S(1)}, bf16[2,128,768]{2,1,0:T(8,128)(2,1)S(1)}, u32[]{:S(2)}, u32[]{:S(2)}) collective-permute-start(bf16[2,128,768]{2,1,0:T(8,128)(2,1)S(1)} %get-tuple-element.46), channel_id=1, source_target_pairs={{0,510},{2,0},{4,2},{6,4},{8,6},{10,8},{12,10},{14,12},{16,14},{18... | collective-permute-start | bytes 1179656 | tf_op jit(solution)/shard_map/ppermute | solution.py:312
  55.0 15.1 %collective-permute-start.3 = (bf16[2,128,768]{2,1,0:T(8,128)(2,1)S(1)}, bf16[2,128,768]{2,1,0:T(8,128)(2,1)S(1)}, u32[]{:S(2)}, u32[]{:S(2)}) collective-permute-start(bf16[2,128,768]{2,1,0:T(8,128)(2,1)S(1)} %get-tuple-element.49), channel_id=1, source_target_pairs={{0,508},{2,510},{4,0},{6,2},{8,4},{10,6},{12,8},{14,10},{16,12},{1... | collective-permute-start | bytes 1179656 | tf_op jit(solution)/shard_map/ppermute | solution.py:319
  58.8 11.3 %all-to-all-start.2 = ((f32[32,8,128]{2,1,0:T(8,128)}), f32[32,8,128]{2,1,0:T(8,128)S(1)}, u32[]{:S(2)}, u32[]{:S(2)}) async-start(f32[32,8,128]{2,1,0:T(8,128)} %line_sum.1), calls=%async_computation.2 | async-start | bytes 262144 | tf_op jit(solution)/shard_map/all_to_all | solution.py:324

commit v8 on v7

--- a/solution.py
+++ b/solution.py
@@ -236,7 +236,6 @@
 def rings(count, head):
     depth = 16
     columns = count // (2 * depth)
-    lead = 11
     planes = []
     for z in range(depth):
         plane = [
@@ -249,8 +248,8 @@
         planes.append(plane + [far])
     lines = [
         [
-            (column * 2 * depth + (z + lead) % depth * 2 + core) * head + half
-            for z in range(depth)
+            (column * 2 * depth + z * 2 + core) * head + half
+            for z in (11, 0, 15, 1, 14, 2, 13, 3, 12, 4, 5, 10, 6, 9, 7, 8)
         ]
         for column in range(columns)
         for core in range(2)

time: 71.4 us -> 71 us (level)
  transfers between devices with their start and end apart: 6 -> 6, of which waited for: 3 -> 2; matrix products, arithmetic and copies ran while one was open for 0% -> 0% of each run, Pallas kernels for 5% -> 5%
where the time goes in v8:
time: 71 us; the launch traced here: 70.6 us
  starting transfers between devices  31 us (44%)
  blocking collectives  18.8 us (26%)
  waiting for transfers between devices  11.3 us (16%)
  Pallas kernels  7.62 us (11%)
  local copies, waits for them, and re-layouts  1.13 us (2%)
  between operations  0.8 us (1%)
    all_to_all x1, blocking collectives, shards(): lax.all_to_all(table_part.reshape(shape), AXES, 0, 0, axis_index_groups=p...  12.2 us
    all_to_all x1, starting transfers between devices, shards(): pieces = lax.all_to_all(copies, AXES, 0, 0, axis_index_groups=lines)  8.77 us
    ppermute x1, waiting for transfers between devices, shards(): far_key = lax.ppermute(key_states, 'ctx', ahead)  8.62 us
    all_to_all x1, starting transfers between devices, shards(): lax.all_to_all(copies, AXES, 0, 0, axis_index_groups=[plane[::-1] for pla...  8.55 us
    pallas_call x7, Pallas kernels, call(): pl.pallas_call(kernel, out_shape=tuple((jax.ShapeDtypeStruct(shape, kind)...  7.62 us
    ppermute x1, starting transfers between devices, shards(): far_key = lax.ppermute(key_states, 'ctx', ahead)  4.37 us
    all_gather x1, blocking collectives, shards(): lax.all_gather(jnp.where(odd, far_key, key_states), 'ctx', axis_index_gro...  3.77 us
    ppermute x1, starting transfers between devices, shards(): far_value = lax.ppermute(value_states, 'ctx', ahead)  3.55 us
  transfers between devices with their start and end apart: 6, of which 2 were waited for; matrix products, arithmetic and copies ran while one was open for 0% of the time, Pallas kernels for 5%

profile of v8, /device:TPU:1, one launch (start us, length us, event | category | flops | bytes accessed | tf_op | source)
XLA Modules:
  0.0 70.6 jit_solution(13320971084307398285)
XLA Ops:
  0.6 4.4 %collective-permute-start = (bf16[128,768]{1,0:T(8,128)(2,1)}, bf16[128,768]{1,0:T(8,128)(2,1)S(1)}, u32[]{:S(2)}, u32[]{:S(2)}) collective-permute-start(bf16[128,768]{1,0:T(8,128)(2,1)} %key_ref.1), channel_id=1, source_target_pairs={{0,4},{2,6},{4,8},{6,10},{8,12},{10,14},{12,16},{14,18},{16,20},{1... | collective-permute-start | bytes 589832 | tf_op jit(solution)/shard_map/ppermute | solution.py:274
  5.0 3.5 %collective-permute-start.1 = (bf16[128,768]{1,0:T(8,128)(2,1)}, bf16[128,768]{1,0:T(8,128)(2,1)S(1)}, u32[]{:S(2)}, u32[]{:S(2)}) collective-permute-start(bf16[128,768]{1,0:T(8,128)(2,1)} %value_ref.1), channel_id=1, source_target_pairs={{0,4},{2,6},{4,8},{6,10},{8,12},{10,14},{12,16},{14,18},{16,20},{1... | collective-permute-start | bytes 589832 | tf_op jit(solution)/shard_map/ppermute | solution.py:273
  8.6 0.0 copy-start
  8.6 0.0 copy-start.1
  8.6 0.0 copy-start.2
  8.6 0.0 copy-start.3
  8.6 0.0 copy-start.4
  8.6 0.0 copy-start.5
  8.6 0.0 copy-start.6
  8.7 0.8 %copy-done = bf16[128,768]{1,0:T(8,128)(2,1)S(1)} copy-done((bf16[128,768]{1,0:T(8,128)(2,1)S(1)}, bf16[128,768]{1,0:T(8,128)(2,1)}, u32[]{:S(2)}) %copy-start) | copy-done | bytes 196632
  9.5 0.1 copy-done.1
  9.6 0.1 copy-done.2
  9.7 0.1 copy-done.3
  9.8 2.2 %own_scores.1 = (f32[128,768]{1,0:T(8,128)S(1)}, f32[2,128,768]{2,1,0:T(8,128)S(1)}, f32[128,768]{1,0:T(8,128)S(1)}, bf16[768,128]{1,0:T(8,128)(2,1)S(1)}, s32[8...) custom-call(s32[1]{0:T(128)} %bitcast.block_ref, ...), custom_call_target="tpu_custom_call" | custom-call | flops 3000000000 | tf_op jit(solution)/shard_map/own_scores/pallas_call | solution.py:38
  12.0 8.6 %collective-permute-done.far_ref.far_key_ref = bf16[128,768]{1,0:T(8,128)(2,1)S(1)} collective-permute-done((bf16[128,768]{1,0:T(8,128)(2,1)}, bf16[128,768]{1,0:T(8,128)(2,1)S(1)}, u32[]{:S(2)}, u32[]{:S(2)}) %collective-permute-start) | collective-permute-done | bytes 196640 | tf_op jit(solution)/shard_map/ppermute | solution.py:274
  20.6 3.8 %all-gather = bf16[256,768]{1,0:T(8,128)(2,1)S(1)} all-gather(bf16[128,768]{1,0:T(8,128)(2,1)S(1)} %broadcast_select_fusion.1), channel_id=2, replica_groups={{0,2},{4,6},{8,10},{12,14},{16,18},{20,22},{24,26},{28,30},{32,34},{36,..., dimensions={0}, use_global_device_ids=true | all-gather | bytes 589824 | tf_op jit(solution)/shard_map/all_gather | solution.py:289
  24.4 0.5 probabilities.1.prob_ref
  24.9 0.0 collective-permute-done.1.far_value_ref
  25.0 2.8 %all-gather.1 = bf16[256,768]{1,0:T(8,128)(2,1)S(1)} all-gather(bf16[128,768]{1,0:T(8,128)(2,1)S(1)} %broadcast_select_fusion), channel_id=3, replica_groups={{0,2},{4,6},{8,10},{12,14},{16,18},{20,22},{24,26},{28,30},{32,34},{36,..., dimensions={0}, use_global_device_ids=true | all-gather | bytes 589824 | tf_op jit(solution)/shard_map/all_gather | solution.py:297
  27.8 2.7 %block_grads.1 = (f32[256,128]{1,0:T(8,128)S(1)}, bf16[2,128,768]{2,1,0:T(8,128)(2,1)S(1)}, bf16[2,128,768]{2,1,0:T(8,128)(2,1)S(1)}, bf16[128,768]{1,0:T(8,128)(2,1)}, f32[2,128,768]{2,1,0:T(8,128)S(1)}) custom-call(s32[1]{0:T(128)} %bitcast.block_ref, s32[8,128]{1,0:T(8,128)S(1)} %get-tuple-element.29.facts_ref, bf16[128,768]{1,0:T(8,128)(2,1)S(1)} %copy-done.2, ...), custom_call_target="tpu_custom_call" | custom-call | flops 6000000000 | tf_op jit(solution)/shard_map/block_grads/pallas_call | solution.py:38
  30.5 12.2 %all_to_all.15.pieces_ref = f32[32,8,128]{2,1,0:T(8,128)S(1)} all-to-all(f32[32,8,128]{2,1,0:T(8,128)S(1)} %bitcast.9), channel_id=1, replica_groups={{0,1,2,3,64,65,66,67,128,130,131,192,193,194,195,256,257,258,259,320,32..., dimensions={0} | all-to-all | bytes 262144 | tf_op jit(solution)/shard_map/all_to_all | solution.py:312
  42.6 0.7 plane_sum.1
  43.3 8.8 %all-to-all-start.1 = ((f32[16,8,128]{2,1,0:T(8,128)}), f32[16,8,128]{2,1,0:T(8,128)S(1)}, u32[]{:S(2)}, u32[]{:S(2)}) async-start(f32[16,8,128]{2,1,0:T(8,128)} %plane_sum.1), calls=%async_computation.1 | async-start | bytes 131072 | tf_op jit(solution)/shard_map/all_to_all | solution.py:319
  52.1 2.9 %collective-permute-start.2 = (bf16[2,128,768]{2,1,0:T(8,128)(2,1)S(1)}, bf16[2,128,768]{2,1,0:T(8,128)(2,1)S(1)}, u32[]{:S(2)}, u32[]{:S(2)}) collective-permute-start(bf16[2,128,768]{2,1,0:T(8,128)(2,1)S(1)} %get-tuple-element.46), channel_id=1, source_target_pairs={{0,510},{2,0},{4,2},{6,4},{8,6},{10,8},{12,10},{14,12},{16,14},{18... | collective-permute-start | bytes 1179656 | tf_op jit(solution)/shard_map/ppermute | solution.py:311
  55.0 2.8 %collective-permute-start.3 = (bf16[2,128,768]{2,1,0:T(8,128)(2,1)S(1)}, bf16[2,128,768]{2,1,0:T(8,128)(2,1)S(1)}, u32[]{:S(2)}, u32[]{:S(2)}) collective-permute-start(bf16[2,128,768]{2,1,0:T(8,128)(2,1)S(1)} %get-tuple-element.49), channel_id=1, source_target_pairs={{0,508},{2,510},{4,0},{6,2},{8,4},{10,6},{12,8},{14,10},{16,12},{1... | collective-permute-start | bytes 1179656 | tf_op jit(solution)/shard_map/ppermute | solution.py:318
  57.8 0.0 all-to-all-done.1.pieces_ref
  57.8 0.7 line_sum.1
  58.5 8.6 %all-to-all-start.2 = ((f32[32,8,128]{2,1,0:T(8,128)}), f32[32,8,128]{2,1,0:T(8,128)S(1)}, u32[]{:S(2)}, u32[]{:S(2)}) async-start(f32[32,8,128]{2,1,0:T(8,128)} %line_sum.1), calls=%async_computation.2 | async-start | bytes 262144 | tf_op jit(solution)/shard_map/all_to_all | solution.py:323
  67.1 0.0 collective-permute-done.2.near_ref
  67.1 2.7 %all-to-all-done.2 = f32[32,8,128]{2,1,0:T(8,128)S(1)} async-done(((f32[32,8,128]{2,1,0:T(8,128)}), f32[32,8,128]{2,1,0:T(8,128)S(1)}, u32[]{:S(2)}, u32[]{:S(2)}) %all-to-all-start.2) | async-done | bytes 131104 | tf_op jit(solution)/shard_map/all_to_all | solution.py:323
  69.8 0.0 collective-permute-done.3.far_ref
  69.8 0.9 %final_sums.1 = (bf16[128,768]{1,0:T(8,128)(2,1)}, bf16[128,768]{1,0:T(8,128)(2,1)}, f32[256,128]{1,0:T(8,128)}) custom-call(f32[2,128,768]{2,1,0:T(8,128)S(1)} %get-tuple-element.42.own_ref, bf16[2,128,768]{2,1,0:T(8,128)(2,1)S(1)} %collective-permute-done.2.near_ref, bf16[2,128,768]{2,1,0:T(8,128)(2,1)S(1)} %collective-permute-done.3.far_ref, ...), custom_call_target="tpu_custom_call" | custom-call | flops 1000000000 | tf_op jit(solution)/shard_map/final_sums/pallas_call | solution.py:38
  (6 shorter events, 0.1 us)
Async XLA Ops:
  0.6 20.0 %collective-permute-start = (bf16[128,768]{1,0:T(8,128)(2,1)}, bf16[128,768]{1,0:T(8,128)(2,1)S(1)}, u32[]{:S(2)}, u32[]{:S(2)}) collective-permute-start(bf16[128,768]{1,0:T(8,128)(2,1)} %key_ref.1), channel_id=1, source_target_pairs={{0,4},{2,6},{4,8},{6,10},{8,12},{10,14},{12,16},{14,18},{16,20},{1... | collective-permute-start | bytes 589832 | tf_op jit(solution)/shard_map/ppermute | solution.py:274
  5.0 19.9 %collective-permute-start.1 = (bf16[128,768]{1,0:T(8,128)(2,1)}, bf16[128,768]{1,0:T(8,128)(2,1)S(1)}, u32[]{:S(2)}, u32[]{:S(2)}) collective-permute-start(bf16[128,768]{1,0:T(8,128)(2,1)} %value_ref.1), channel_id=1, source_target_pairs={{0,4},{2,6},{4,8},{6,10},{8,12},{10,14},{12,16},{14,18},{16,20},{1... | collective-permute-start | bytes 589832 | tf_op jit(solution)/shard_map/ppermute | solution.py:273
  8.6 0.9 %copy-start = (bf16[128,768]{1,0:T(8,128)(2,1)S(1)}, bf16[128,768]{1,0:T(8,128)(2,1)}, u32[]{:S(2)}) copy-start(bf16[128,768]{1,0:T(8,128)(2,1)} %key_ref.1) | copy-start | bytes 589828
  8.6 1.0 %copy-start.1 = (bf16[128,768]{1,0:T(8,128)(2,1)S(1)}, bf16[128,768]{1,0:T(8,128)(2,1)}, u32[]{:S(2)}) copy-start(bf16[128,768]{1,0:T(8,128)(2,1)} %value_ref.1) | copy-start | bytes 589828
  8.6 1.1 %copy-start.2 = (bf16[128,768]{1,0:T(8,128)(2,1)S(1)}, bf16[128,768]{1,0:T(8,128)(2,1)}, u32[]{:S(2)}) copy-start(bf16[128,768]{1,0:T(8,128)(2,1)} %query_ref.5) | copy-start | bytes 589828
  8.6 1.2 %copy-start.3 = (bf16[128,768]{1,0:T(8,128)(2,1)S(1)}, bf16[128,768]{1,0:T(8,128)(2,1)}, u32[]{:S(2)}) copy-start(bf16[128,768]{1,0:T(8,128)(2,1)} %grad_ref.3) | copy-start | bytes 589828
  8.6 1.2 %copy-start.4 = (bf16[256,128]{1,0:T(8,128)(2,1)S(1)}, bf16[256,128]{1,0:T(8,128)(2,1)}, u32[]{:S(2)}) copy-start(bf16[256,128]{1,0:T(8,128)(2,1)} %table_ref.1) | copy-start | bytes 196612
  8.6 1.2 %copy-start.5 = (s32[1,3]{1,0:T(1,128)S(1)}, s32[1,3]{1,0:T(1,128)}, u32[]{:S(2)}) copy-start(s32[1,3]{1,0:T(1,128)} %mask_ref.1) | copy-start | bytes 40
  8.6 1.2 %copy-start.6 = (s32[1,3]{1,0:T(1,128)S(1)}, s32[1,3]{1,0:T(1,128)}, u32[]{:S(2)}) copy-start(s32[1,3]{1,0:T(1,128)} %shift_ref.1) | copy-start | bytes 40
  43.3 14.5 %all-to-all-start.1 = ((f32[16,8,128]{2,1,0:T(8,128)}), f32[16,8,128]{2,1,0:T(8,128)S(1)}, u32[]{:S(2)}, u32[]{:S(2)}) async-start(f32[16,8,128]{2,1,0:T(8,128)} %plane_sum.1), calls=%async_computation.1 | async-start | bytes 131072 | tf_op jit(solution)/shard_map/all_to_all | solution.py:319
  52.1 15.0 %collective-permute-start.2 = (bf16[2,128,768]{2,1,0:T(8,128)(2,1)S(1)}, bf16[2,128,768]{2,1,0:T(8,128)(2,1)S(1)}, u32[]{:S(2)}, u32[]{:S(2)}) collective-permute-start(bf16[2,128,768]{2,1,0:T(8,128)(2,1)S(1)} %get-tuple-element.46), channel_id=1, source_target_pairs={{0,510},{2,0},{4,2},{6,4},{8,6},{10,8},{12,10},{14,12},{16,14},{18... | collective-permute-start | bytes 1179656 | tf_op jit(solution)/shard_map/ppermute | solution.py:311
  55.0 14.8 %collective-permute-start.3 = (bf16[2,128,768]{2,1,0:T(8,128)(2,1)S(1)}, bf16[2,128,768]{2,1,0:T(8,128)(2,1)S(1)}, u32[]{:S(2)}, u32[]{:S(2)}) collective-permute-start(bf16[2,128,768]{2,1,0:T(8,128)(2,1)S(1)} %get-tuple-element.49), channel_id=1, source_target_pairs={{0,508},{2,510},{4,0},{6,2},{8,4},{10,6},{12,8},{14,10},{16,12},{1... | collective-permute-start | bytes 1179656 | tf_op jit(solution)/shard_map/ppermute | solution.py:318
  58.5 11.2 %all-to-all-start.2 = ((f32[32,8,128]{2,1,0:T(8,128)}), f32[32,8,128]{2,1,0:T(8,128)S(1)}, u32[]{:S(2)}, u32[]{:S(2)}) async-start(f32[32,8,128]{2,1,0:T(8,128)} %line_sum.1), calls=%async_computation.2 | async-start | bytes 262144 | tf_op jit(solution)/shard_map/all_to_all | solution.py:323
